TPU v7x, 256 devices: a whole 4x4x8 slice. The times are simulated.
256 devices in a mesh: gx: 8 (over x, core), gy: 32 (over y, z).
Axes of the slice: x: 4, y: 4, z: 8, core: 2. Of those that a mesh axis runs over, the one named last changes fastest.
Arguments:
- field: bfloat16 [128, 128, 20, 1024], P('gx', 'gy'), may hold values from -6 to 6
- cotangent: bfloat16 [128, 128, 20, 1024], P('gx', 'gy'), may hold values from -6 to 6
- spectral_weight: float32 [2, 20, 20, 24, 24, 96], P(None, None, None, None, 'gx', 'gy'), may hold values from -16 to 16
- pointwise_weight: bfloat16 [20, 20], replicated, may hold values from -1.25 to 1.25
- channel_bias: float32 [20], replicated, may hold values from -3 to 3
Outputs:
- output: bfloat16 [128, 128, 20, 1024], P('gx', 'gy')
- grad_field: bfloat16 [128, 128, 20, 1024], P('gx', 'gy')
- grad_weight: float32 [2, 20, 20, 24, 24, 96], P(None, None, None, None, 'gx', 'gy')
All inputs are finite; a program needn't handle non-finite values.
Results may differ from a plain program's by a relative error of at most 0.0054.
Values sent between devices are 32-bit elements; how exact they have to be, the bound alone decides.
No kernel may reach another device: no remote copies, remote signals or barrier semaphores. Data moves between devices by JAX's collectives and lax.ppermute only.
A program may use at most 192 MiB of HBM per device.

v0:
```python
import math

import jax
import jax.numpy as jnp
from jax import lax
from jax.sharding import PartitionSpec as P

NX = 128
NY = 128
NZ = 64
NT = 16
KX = 24
KY = 24
KZ = 12
KT = 8


HIGHEST_PRECISION = lax.Precision.HIGHEST
GELU_SCALE = math.sqrt(2.0 / math.pi)
GELU_CUBIC = 0.044715


def signed_modes(tally_index, modes_total):
    return jnp.where(tally_index < modes_total // 2, tally_index, tally_index - modes_total)


def angle_of(phase, period):
    return phase.astype(jnp.float32) * (2.0 * math.pi / period)


def complex_analysis(positions, period, modes_total):
    frequency = signed_modes(jnp.arange(modes_total, dtype=jnp.int32), modes_total)
    angles = angle_of(jnp.mod(positions[:, None] * frequency[None, :], period), period)
    cosines = jnp.cos(angles)
    sine_part = jnp.sin(angles)
    return jnp.stack(
        [jnp.stack([cosines, -sine_part], axis=1), jnp.stack([sine_part, cosines], axis=1)], axis=0
    )


def complex_synthesis(positions, period, modes_total):
    frequency = signed_modes(jnp.arange(modes_total, dtype=jnp.int32), modes_total)
    angles = angle_of(jnp.mod(frequency[:, None] * positions[None, :], period), period)
    cosines = jnp.cos(angles) / period
    sine_part = jnp.sin(angles) / period
    return jnp.stack(
        [jnp.stack([cosines, sine_part], axis=1), jnp.stack([-sine_part, cosines], axis=1)], axis=0
    )


def flattened_lookup(table):
    return table.reshape(table.shape[0] * table.shape[1], table.shape[2] * table.shape[3])


def axis_inward(positions, period, modes_total, forward):
    if forward:
        return flattened_lookup(complex_analysis(positions, period, modes_total))
    return flattened_lookup(
        jnp.transpose(complex_synthesis(positions, period, modes_total), (2, 3, 0, 1))
    )


def axis_outward(positions, period, modes_total, forward):
    if forward:
        return flattened_lookup(complex_synthesis(positions, period, modes_total))
    return flattened_lookup(
        jnp.transpose(complex_analysis(positions, period, modes_total), (2, 3, 0, 1))
    )


def time_angles():
    cells = jnp.arange(NZ * NT, dtype=jnp.int32)
    spectrum_stack = jnp.arange(KZ * KT, dtype=jnp.int32)
    depth_freq = signed_modes(spectrum_stack // KT, KZ)
    time_freq = spectrum_stack % KT
    phase = (
        depth_freq[None, :] * (cells // NT)[:, None] * NT
        + time_freq[None, :] * (cells % NT)[:, None] * NZ
    )
    return (angle_of(jnp.mod(phase, NZ * NT), NZ * NT), time_freq)


def depth_clock_lookup(forward):
    angles, time_freq = time_angles()
    analysis = jnp.stack([jnp.cos(angles), -jnp.sin(angles)], axis=1)
    weights = jnp.where(time_freq == 0, 1.0, 2.0).astype(jnp.float32) / (NZ * NT)
    synthesis = jnp.stack(
        [jnp.cos(angles).T * weights[:, None], -jnp.sin(angles).T * weights[:, None]], axis=0
    )
    if forward:
        toward_spectrum, outward = (analysis, synthesis)
    else:
        toward_spectrum, outward = (
            jnp.transpose(synthesis, (2, 0, 1)),
            jnp.transpose(analysis, (1, 2, 0)),
        )
    return (toward_spectrum.astype(jnp.bfloat16), outward)


def along_last(spectrum_stack, table):
    leading = spectrum_stack.shape[:-2]
    flat = spectrum_stack.reshape(leading + (spectrum_stack.shape[-2] * spectrum_stack.shape[-1],))
    product = jnp.dot(flat, table, precision=HIGHEST_PRECISION)
    return product.reshape(leading + (2, table.shape[1] // 2))


def mix_modes(weight, spectrum_stack):
    return jnp.einsum("ioxym,myix->myox", weight, spectrum_stack, precision=HIGHEST_PRECISION)


def unmix_modes(weight, spectrum_stack):
    return jnp.einsum("ioxym,myox->myix", weight, spectrum_stack, precision=HIGHEST_PRECISION)


def outer_modes(inputs, grads):
    return jnp.einsum("myix,myox->ioxym", inputs, grads, precision=HIGHEST_PRECISION)


def spectral_apply(weight, spectrum_stack):
    real_part, imag_part = (spectrum_stack[:, :, :, 0], spectrum_stack[:, :, :, 1])
    real_out = mix_modes(weight[0], real_part) - mix_modes(weight[1], imag_part)
    imag_out = mix_modes(weight[0], imag_part) + mix_modes(weight[1], real_part)
    return jnp.stack([real_out, imag_out], axis=3)


def spectral_adjoint(weight, grads):
    real_part, imag_part = (grads[:, :, :, 0], grads[:, :, :, 1])
    real_in = unmix_modes(weight[0], real_part) + unmix_modes(weight[1], imag_part)
    imag_in = unmix_modes(weight[0], imag_part) - unmix_modes(weight[1], real_part)
    return jnp.stack([real_in, imag_in], axis=3)


def spectral_weight_grad(inputs, grads):
    in_real, in_imag = (inputs[:, :, :, 0], inputs[:, :, :, 1])
    grad_real, grad_imag = (grads[:, :, :, 0], grads[:, :, :, 1])
    real_grad = outer_modes(in_real, grad_real) + outer_modes(in_imag, grad_imag)
    imag_grad = outer_modes(in_real, grad_imag) - outer_modes(in_imag, grad_real)
    return jnp.stack([real_grad, imag_grad], axis=0)


def gelu_parts(values):
    inner = GELU_SCALE * (values + GELU_CUBIC * values * values * values)
    tangent = jnp.tanh(inner)
    result = 0.5 * values * (1.0 + tangent)
    slope = 0.5 * (1.0 + tangent) + 0.5 * values * (1.0 - tangent * tangent) * GELU_SCALE * (
        1.0 + 3.0 * GELU_CUBIC * values * values
    )
    return (result, slope)


def per_device(field, cotangent, spectral_weight, pointwise_weight, channel_bias):
    rows_x = field.shape[0]
    local_x = lax.axis_index("gx") * rows_x + jnp.arange(rows_x, dtype=jnp.int32)
    whole_y = jnp.arange(NY, dtype=jnp.int32)

    def analyze(spatial_lattice, forward):
        toward_spectrum = depth_clock_lookup(forward)[0]
        spectrum_stack = jnp.einsum(
            "tdve,eoh->htvod", spatial_lattice, toward_spectrum, preferred_element_type=jnp.float32
        )
        spectrum_stack = lax.all_to_all(
            spectrum_stack, "gy", split_axis=0, concat_axis=4, tiled=True
        )
        spectrum_stack = along_last(spectrum_stack, axis_inward(whole_y, NY, KY, forward))
        spectrum_stack = jnp.transpose(spectrum_stack, (0, 4, 2, 3, 1))
        spectrum_stack = along_last(spectrum_stack, axis_inward(local_x, NX, KX, forward))
        spectrum_stack = lax.psum_scatter(spectrum_stack, "gx", scatter_dimension=1, tiled=True)
        return spectrum_stack

    def synthesize(spectrum_stack, forward):
        spectrum_stack = lax.all_gather(spectrum_stack, "gx", axis=1, tiled=True)
        spectrum_stack = along_last(spectrum_stack, axis_outward(local_x, NX, KX, forward))
        spectrum_stack = jnp.transpose(spectrum_stack, (0, 4, 2, 3, 1))
        spectrum_stack = along_last(spectrum_stack, axis_outward(whole_y, NY, KY, forward))
        spectrum_stack = lax.all_to_all(
            spectrum_stack, "gy", split_axis=4, concat_axis=0, tiled=True
        )
        outward = depth_clock_lookup(forward)[1]
        return jnp.einsum("macpb,pmq->abcq", spectrum_stack, outward, precision=HIGHEST_PRECISION)

    field_spectrum = analyze(field, True)
    spectral_part = synthesize(spectral_apply(spectral_weight, field_spectrum), True)
    linear = jnp.einsum(
        "abiq,io->aboq", field, pointwise_weight, preferred_element_type=jnp.float32
    )
    before = spectral_part + linear + channel_bias[None, None, :, None]
    result, slope = gelu_parts(before)
    output = result.astype(jnp.bfloat16)
    pre_grad = (cotangent.astype(jnp.float32) * slope).astype(jnp.bfloat16)
    grad_spectrum = analyze(pre_grad, False)
    grad_weight = spectral_weight_grad(field_spectrum, grad_spectrum)
    back_part = synthesize(spectral_adjoint(spectral_weight, grad_spectrum), False)
    linear_back = jnp.einsum(
        "aboq,io->abiq", pre_grad, pointwise_weight, preferred_element_type=jnp.float32
    )
    grad_field = (back_part + linear_back).astype(jnp.bfloat16)
    return (output, grad_field, grad_weight)


def solution(mesh):
    return jax.shard_map(
        per_device,
        mesh=mesh,
        in_specs=(
            P("gx", "gy", None, None),
            P("gx", "gy", None, None),
            P(None, None, None, None, "gx", "gy"),
            P(),
            P(),
        ),
        out_specs=(
            P("gx", "gy", None, None),
            P("gx", "gy", None, None),
            P(None, None, None, None, "gx", "gy"),
        ),
        check_vma=False,
    )
```

profile of v0, /device:TPU:32, one launch (start us, length us, event | category | flops | bytes accessed | tf_op | source)
XLA Modules:
  0.0 568.6 jit_solution(7812289124160482346)
XLA Ops:
  9.8 3.0 fusion.45
  12.8 5.4 copy.161
  18.2 9.9 %reshape.1258 = f32[32,1,7680]{2,1,0:T(1,128)} reshape(f32[96,2,16,4,20]{4,3,2,1,0:T(4,128)} %bitcast.368) | data formatting | bytes 1966080
  28.2 11.4 %all-to-all-start = ((f32[32,1,7680]{2,1,0:T(1,128)}), f32[32,1,7680]{2,1,0:T(1,128)S(1)}, u32[]{:S(2)}, u32[]{:S(2)}) async-start(f32[32,1,7680]{2,1,0:T(1,128)} %reshape.1258), calls=%async_computation | async-start | bytes 1966080 | tf_op jit(solution)/shard_map/all_to_all | solution.py:161
  41.9 7.6 %fusion.122 = (f32[1,20,20,24,3,3]{3,0,5,4,2,1:T(1,128)S(1)}, f32[1,20,20,24,3,3]{3,0,5,4,2,1:T(1,128)}) fusion(f32[2,20,20,24,3,3]{3,0,5,4,2,1:T(2,128)} %param.7), kind=kLoop, calls=%fused_computation.202 | loop fusion | bytes 1382400 | tf_op jit(solution)/shard_map/slice | solution.py:121
  49.4 17.3 %all-to-all-done = f32[32,1,7680]{2,1,0:T(1,128)S(1)} async-done(((f32[32,1,7680]{2,1,0:T(1,128)}), f32[32,1,7680]{2,1,0:T(1,128)S(1)}, u32[]{:S(2)}, u32[]{:S(2)}) %all-to-all-start) | async-done | bytes 983072 | tf_op jit(solution)/shard_map/all_to_all | solution.py:161
  68.2 4.1 reduce.16
  72.3 10.8 %reshape.1259 = f32[96,2,16,4,20]{4,3,2,1,0:T(4,128)} reshape(f32[32,7680]{1,0:T(8,128)S(1)} %reduce.16) | data formatting | bytes 1966080
  83.1 3.7 copy.162
  87.9 10.4 %fusion.48 = f32[3,24,20,2,16]{1,2,3,4,0:T(8,128)S(1)} fusion(f32[2,24,256,1,1]{2,1,0,4,3:T(8,128)S(1)} %bitcast.380, f32[3,16,20,256,1]{2,1,3,0,4:T(8,128)S(1)} %bitcast.359), kind=kOutput, calls=%fused_computation.54 | convolution fusion | flops 141557760 | bytes 1216512 | tf_op jit(solution)/shard_map/dot_general | solution.py:103
  100.4 2.3 copy.170
  104.7 63.4 %all-reduce.5.cloned.1.call-done = f32[3,24,20,2,24]{4,3,2,0,1:T(2,128)} async-done(((f32[3,24,20,2,24]{4,3,2,0,1:T(2,128)}), f32[3,24,20,2,24]{4,3,2,0,1:T(2,128)}) %all-reduce.5.cloned.1.call-update) | async-done | bytes 276496
  169.4 2.6 fusion.38
  172.1 14.6 %all_gather.6 = f32[3,24,20,2,24]{4,2,1,0,3:T(8,128)S(1)} all-gather(f32[3,3,20,2,24]{4,2,1,0,3:T(8,128)S(1)} %pad_maximum_fusion.5), channel_id=1, replica_groups=mesh['gx'=8,'gy'=32] {'gx'}, dimensions={1}, use_global_device_ids=true | all-gather | bytes 311040 | tf_op jit(solution)/shard_map/all_gather | solution.py:171
  189.5 5.4 convolution_bitcast_fusion.1
  197.0 5.2 copy.179
  202.2 11.1 %reshape.1260 = f32[32,1,7680]{2,1,0:T(1,128)} reshape(f32[128,3,16,2,20]{4,3,2,1,0:T(2,128)} %bitcast.360) | data formatting | bytes 1966080
  213.3 10.1 %all-to-all-start.1 = ((f32[32,1,7680]{2,1,0:T(1,128)}), f32[32,1,7680]{2,1,0:T(1,128)}, u32[]{:S(2)}, u32[]{:S(2)}) async-start(f32[32,1,7680]{2,1,0:T(1,128)} %reshape.1260), calls=%async_computation.1 | async-start | bytes 1966080 | tf_op jit(solution)/shard_map/all_to_all | solution.py:175
  223.5 2.6 cosine_multiply_fusion
  226.0 24.7 %all-to-all-done.1 = f32[32,1,7680]{2,1,0:T(1,128)} async-done(((f32[32,1,7680]{2,1,0:T(1,128)}), f32[32,1,7680]{2,1,0:T(1,128)}, u32[]{:S(2)}, u32[]{:S(2)}) %all-to-all-start.1) | async-done | bytes 983072 | tf_op jit(solution)/shard_map/all_to_all | solution.py:175
  250.8 4.1 reduce.17
  254.9 12.3 %reshape.1261 = f32[128,3,16,2,20]{4,3,2,1,0:T(2,128)} reshape(f32[32,7680]{1,0:T(8,128)S(1)} %reduce.17) | data formatting | bytes 1966080
  267.2 3.3 copy.180
  271.7 13.3 %fusion.15 = f32[1024,16,20,4,1]{0,2,4,3,1:T(8,128)S(1)} fusion(f32[96,16,20,2,4]{2,1,4,3,0:T(8,128)S(1)} %bitcast.355, f32[1,96,1024]{2,1,0:T(8,128)S(1)} %copy-done.10, f32[1,96,1024]{2,1,0:T(8,128)S(1)} %get-tuple-element.60), kind=kOutput, calls=%fused_computation.19 | convolution fusion | flops 3020095488 | bytes 7012352 | tf_op jit(solution)/shard_map/macpb,pmq->abcq/dot_general | solution.py:179
  285.1 7.8 %fusion.6 = (bf16[16,4,20,1024]{3,2,1,0:T(8,128)(2,1)S(1)}, bf16[16,4,20,1024]{3,2,1,0:T(8,128)(2,1)}) fusion(bf16[16,4,20,1024]{3,1,2,0:T(4,128)(2,1)S(1)} %copy-done.18, f32[20]{0:T(128)S(1)} %copy-done.20, bf16[16,4,20,1024]{3,1,2,0:T(4,128)(2,1)S(1)} %copy-done.19, bf16[20,20]{1,0:T(8,128)(2,1)S(1)} %copy-done, f32[1024,16,20,4,1]{0,2,4,3,1:T(8,128)S(1)} %fusion.15), kind=kOutput, calls=%fused_computation.8 | convolution fusion | flops 83886080 | bytes 15729520 | tf_op jit(solution)/shard_map/abiq,io->aboq/dot_general | solution.py:183
  295.6 5.4 copy.186
  301.0 9.9 %reshape.1262 = f32[32,1,7680]{2,1,0:T(1,128)} reshape(f32[96,2,16,4,20]{4,3,2,1,0:T(4,128)} %bitcast.369) | data formatting | bytes 1966080
  310.9 5.6 all-to-all-start.2
  316.8 26.5 %all-to-all-done.2 = f32[32,1,7680]{2,1,0:T(1,128)} async-done(((f32[32,1,7680]{2,1,0:T(1,128)}), f32[32,1,7680]{2,1,0:T(1,128)}, u32[]{:S(2)}, u32[]{:S(2)}) %all-to-all-start.2) | async-done | bytes 983072 | tf_op jit(solution)/shard_map/all_to_all | solution.py:161
  343.3 4.1 reduce.18
  347.4 10.7 %reshape.1263 = f32[96,2,16,4,20]{4,3,2,1,0:T(4,128)} reshape(f32[32,7680]{1,0:T(8,128)S(1)} %reduce.18) | data formatting | bytes 1966080
  358.2 3.7 copy.187
  363.0 10.4 %fusion.51 = f32[3,24,20,2,16]{1,2,3,4,0:T(8,128)S(1)} fusion(f32[2,24,256,1,1]{2,1,0,4,3:T(8,128)S(1)} %bitcast.382, f32[3,16,20,256,1]{2,1,3,0,4:T(8,128)S(1)} %bitcast.356), kind=kOutput, calls=%fused_computation.55 | convolution fusion | flops 141557760 | bytes 1216512 | tf_op jit(solution)/shard_map/dot_general | solution.py:103
  377.9 63.9 %all-reduce.7.cloned.1.call-done = f32[3,24,20,2,24]{4,3,2,0,1:T(2,128)} async-done(((f32[3,24,20,2,24]{4,3,2,0,1:T(2,128)}), f32[3,24,20,2,24]{4,3,2,0,1:T(2,128)}) %all-reduce.7.cloned.1.call-update) | async-done | bytes 276496
  443.0 4.0 fusion.40
  447.1 14.6 %all_gather.7 = f32[3,24,20,2,24]{4,2,1,0,3:T(8,128)S(1)} all-gather(f32[3,3,20,2,24]{4,2,1,0,3:T(8,128)S(1)} %pad_maximum_fusion.6), channel_id=1, replica_groups=mesh['gx'=8,'gy'=32] {'gx'}, dimensions={1}, use_global_device_ids=true | all-gather | bytes 311040 | tf_op jit(solution)/shard_map/all_gather | solution.py:171
  463.6 4.3 convolution_bitcast_fusion
  470.0 5.0 copy.200
  475.0 11.2 %reshape.1264 = f32[32,1,7680]{2,1,0:T(1,128)} reshape(f32[128,3,16,2,20]{4,3,2,1,0:T(2,128)} %bitcast.365) | data formatting | bytes 1966080
  486.1 10.4 %all-to-all-start.3 = ((f32[32,1,7680]{2,1,0:T(1,128)}), f32[32,1,7680]{2,1,0:T(1,128)S(1)}, u32[]{:S(2)}, u32[]{:S(2)}) async-start(f32[32,1,7680]{2,1,0:T(1,128)} %reshape.1264), calls=%async_computation.3 | async-start | bytes 1966080 | tf_op jit(solution)/shard_map/all_to_all | solution.py:175
  496.6 5.6 copy.206
  503.0 4.7 copy.208
  507.7 16.0 %all-to-all-done.3 = f32[32,1,7680]{2,1,0:T(1,128)S(1)} async-done(((f32[32,1,7680]{2,1,0:T(1,128)}), f32[32,1,7680]{2,1,0:T(1,128)S(1)}, u32[]{:S(2)}, u32[]{:S(2)}) %all-to-all-start.3) | async-done | bytes 983072 | tf_op jit(solution)/shard_map/all_to_all | solution.py:175
  523.6 3.0 reduce.19
  526.7 12.3 %reshape.1265 = f32[128,3,16,2,20]{4,3,2,1,0:T(2,128)} reshape(f32[32,7680]{1,0:T(8,128)S(1)} %reduce.19) | data formatting | bytes 1966080
  539.0 3.3 copy.201
  543.5 13.1 %fusion.13 = f32[1024,16,20,4,1]{0,2,4,3,1:T(8,128)S(1)} fusion(f32[96,16,20,2,4]{2,1,4,3,0:T(8,128)S(1)} %bitcast.354, f32[1024,1,96]{0,2,1:T(8,128)S(1)} %copy-done.7, f32[1024,1,96]{0,2,1:T(8,128)S(1)} %copy-done.5), kind=kOutput, calls=%fused_computation.17 | convolution fusion | flops 3020095488 | bytes 7012352 | tf_op jit(solution)/shard_map/macpb,pmq->abcq/dot_general | solution.py:179
  557.9 3.7 copy.207
  (122 shorter events, 35.1 us)
Async XLA Ops:
  7.2 277.8 %copy-start = (bf16[20,20]{1,0:T(8,128)(2,1)S(1)}, bf16[20,20]{1,0:T(8,128)(2,1)}, u32[]{:S(2)}) copy-start(bf16[20,20]{1,0:T(8,128)(2,1)} %param.8) | copy-start | bytes 2404
  8.9 0.8 copy-start.4
  8.9 0.9 copy-start.6
  28.2 38.6 %all-to-all-start = ((f32[32,1,7680]{2,1,0:T(1,128)}), f32[32,1,7680]{2,1,0:T(1,128)S(1)}, u32[]{:S(2)}, u32[]{:S(2)}) async-start(f32[32,1,7680]{2,1,0:T(1,128)} %reshape.1258), calls=%async_computation | async-start | bytes 1966080 | tf_op jit(solution)/shard_map/all_to_all | solution.py:161
  39.5 128.6 %all-reduce.5.cloned.1.call-start = ((), (), s32[]{:S(2)}) async-start(), calls=%async_computation.4 | async-start | bytes 2949120
  40.0 47.9 %copy-start.13 = (f32[6,8,2,128]{3,1,2,0:T(8,128)}, f32[6,8,2,128]{3,1,2,0:T(8,128)S(1)}, u32[]{:S(2)}) copy-start(f32[6,8,2,128]{3,1,2,0:T(8,128)S(1)} %copy.429) | copy-start | bytes 147460
  66.7 0.9 copy-start.1
  100.3 3.1 copy-start.21
  169.3 2.8 copy-start.11
  213.3 37.5 %all-to-all-start.1 = ((f32[32,1,7680]{2,1,0:T(1,128)}), f32[32,1,7680]{2,1,0:T(1,128)}, u32[]{:S(2)}, u32[]{:S(2)}) async-start(f32[32,1,7680]{2,1,0:T(1,128)} %reshape.1260), calls=%async_computation.1 | async-start | bytes 1966080 | tf_op jit(solution)/shard_map/all_to_all | solution.py:175
  226.0 45.6 %copy-start.8 = (f32[1,96,1024]{2,1,0:T(8,128)}, f32[1,96,1024]{2,1,0:T(8,128)S(1)}, u32[]{:S(2)}) copy-start(f32[1,96,1024]{2,1,0:T(8,128)S(1)} %get-tuple-element.60) | copy-start | bytes 1179652
  270.5 1.1 copy-start.10
  271.7 13.3 %copy-start.18 = (bf16[16,4,20,1024]{3,1,2,0:T(4,128)(2,1)S(1)}, bf16[16,4,20,1024]{3,1,2,0:T(4,128)(2,1)}, u32[]{:S(2)}) copy-start(bf16[16,4,20,1024]{3,1,2,0:T(4,128)(2,1)} %param.6) | copy-start | bytes 7864324
  271.7 13.3 %copy-start.19 = (bf16[16,4,20,1024]{3,1,2,0:T(4,128)(2,1)S(1)}, bf16[16,4,20,1024]{3,1,2,0:T(4,128)(2,1)}, u32[]{:S(2)}) copy-start(bf16[16,4,20,1024]{3,1,2,0:T(4,128)(2,1)} %param.5) | copy-start | bytes 7864324
  271.7 13.3 %copy-start.20 = (f32[20]{0:T(128)S(1)}, f32[20]{0:T(128)}, u32[]{:S(2)}) copy-start(f32[20]{0:T(128)} %param.9) | copy-start | bytes 244
  285.0 9.5 %copy-start.9 = (f32[1,96,1024]{2,1,0:T(8,128)S(1)}, f32[1,96,1024]{2,1,0:T(8,128)}, u32[]{:S(2)}) copy-start(f32[1,96,1024]{2,1,0:T(8,128)} %copy-done.8) | copy-start | bytes 1179652
  292.9 1.7 copy-start.2
  301.0 15.6 %copy-start.15 = (f32[2,128,2,24]{1,3,0,2:T(8,128)S(1)}, f32[2,128,2,24]{1,3,0,2:T(8,128)}, u32[]{:S(2)}) copy-start(f32[2,128,2,24]{1,3,0,2:T(8,128)} %get-tuple-element.50) | copy-start | bytes 147460
  301.0 15.7 %copy-start.17 = (f32[2,16,2,24]{3,2,1,0:T(2,128)S(1)}, f32[2,16,2,24]{3,2,1,0:T(2,128)}, u32[]{:S(2)}) copy-start(f32[2,16,2,24]{3,2,1,0:T(2,128)} %get-tuple-element.52) | copy-start | bytes 18436
  310.9 32.4 %all-to-all-start.2 = ((f32[32,1,7680]{2,1,0:T(1,128)}), f32[32,1,7680]{2,1,0:T(1,128)}, u32[]{:S(2)}, u32[]{:S(2)}) async-start(f32[32,1,7680]{2,1,0:T(1,128)} %reshape.1262), calls=%async_computation.2 | async-start | bytes 1966080 | tf_op jit(solution)/shard_map/all_to_all | solution.py:161
  316.5 125.2 %all-reduce.7.cloned.1.call-start = ((), (), s32[]{:S(2)}) async-start(), calls=%async_computation.5 | async-start | bytes 2949120
  373.7 4.1 copy-start.16
  373.7 4.2 copy-start.14
  475.0 21.6 %copy-start.12 = (f32[3,3,20,1,24]{4,2,3,0,1:T(8,128)S(1)}, f32[3,3,20,1,24]{4,2,3,0,1:T(8,128)}, u32[]{:S(2)}) copy-start(f32[3,3,20,1,24]{4,2,3,0,1:T(8,128)} %copy-done.11) | copy-start | bytes 51844
  486.1 37.5 %all-to-all-start.3 = ((f32[32,1,7680]{2,1,0:T(1,128)}), f32[32,1,7680]{2,1,0:T(1,128)S(1)}, u32[]{:S(2)}, u32[]{:S(2)}) async-start(f32[32,1,7680]{2,1,0:T(1,128)} %reshape.1264), calls=%async_computation.3 | async-start | bytes 1966080 | tf_op jit(solution)/shard_map/all_to_all | solution.py:175
  542.3 1.1 copy-start.5
  542.3 1.1 copy-start.7
  543.5 13.1 %copy-start.3 = (bf16[16,4,20,1024]{3,2,1,0:T(8,128)(2,1)S(1)}, bf16[16,4,20,1024]{3,2,1,0:T(8,128)(2,1)}, u32[]{:S(2)}) copy-start(bf16[16,4,20,1024]{3,2,1,0:T(8,128)(2,1)} %copy-done.2) | copy-start | bytes 7864324
Sparse Core Ops, SparseCore 0:
  102.8 65.2 all-reduce.4
  377.9 63.8 all-reduce.6
where the time goes:
time: 575 us; the launch traced here: 569 us
  waiting for transfers between devices  212 us (37%)
  local copies, waits for them, and re-layouts  169 us (29%)
  matrix products  75.3 us (13%)
  starting transfers between devices  37.7 us (7%)
  other arithmetic  29.6 us (5%)
  blocking collectives  29.2 us (5%)
  between operations  15.8 us (3%)
    unnamed x4, waiting for transfers between devices  127 us
    unnamed x65, local copies, waits for them, and re-layouts  107 us
    all_to_all x2, waiting for transfers between devices, analyze(): lax.all_to_all(spectrum_stack, 'gy', split_axis=0, concat_axis=4, tiled=T...  43.7 us
    all_to_all x2, waiting for transfers between devices, synthesize(): lax.all_to_all(spectrum_stack, 'gy', split_axis=4, concat_axis=0, tiled=T...  40.7 us
    dot_general x8, matrix products, along_last(): product = jnp.dot(flat, table, precision=HIGHEST_PRECISION)  35.8 us
    all_gather x2, blocking collectives, synthesize(): spectrum_stack = lax.all_gather(spectrum_stack, 'gx', axis=1, tiled=True)  29.2 us
    dot_general x2, matrix products, synthesize(): jnp.einsum('macpb,pmq->abcq', spectrum_stack, outward, precision=HIGHEST_...  26.3 us
    all_to_all x2, starting transfers between devices, synthesize(): lax.all_to_all(spectrum_stack, 'gy', split_axis=4, concat_axis=0, tiled=T...  20.5 us
  transfers between devices with their start and end apart: 6, of which 6 were waited for; matrix products, arithmetic and copies ran while one was open for 4% of the time, Pallas kernels for 0%

commit v1 on v0

v1 whole, which is shorter than its diff:
```python
import math

import jax
import jax.numpy as jnp
import numpy as np
from jax import lax
from jax.experimental import pallas as pl
from jax.experimental.pallas import tpu as pltpu
from jax.sharding import PartitionSpec as P

NX = 128
NY = 128
NZ = 64
NT = 16
C = 20
KX = 24
KY = 24
KZ = 12
KT = 8

GX = 8
GY = 32
XL = NX // GX
YL = NY // GY
KYL = KY // GX
ML = KZ * KT // GY
XC = XL * C
CELLS = XL * C * YL
Q = NZ * NT
N = 2 * ML * GY
LT = 8
G = 4
CG = C // G
KC = CG * KX
MODES = KYL * ML
ROWS = G * 2 * MODES

GELU_SCALE = math.sqrt(2.0 / math.pi)
GELU_CUBIC = 0.044715
F32 = jnp.float32
BF16 = jnp.bfloat16
SCALE = 1.0 / (NX * NY)


def signed(count):
    j = np.arange(count)
    return np.where(j < count // 2, j, j - count)


def halves(table):
    table = np.asarray(table, np.float32)
    high = table.astype(jnp.bfloat16)
    low = (table - high.astype(np.float32)).astype(jnp.bfloat16)
    return high, low


def zt_tables():
    q = np.arange(Q)
    m = (np.arange(GY)[None, :] * ML + np.arange(ML)[:, None]).reshape(-1)
    fz, kt = signed(KZ)[m // KT], m % KT
    phase = (fz[None, :] * (q // NT)[:, None] * NT + kt[None, :] * (q % NT)[:, None] * NZ) % Q
    angles = phase * (2.0 * math.pi / Q)
    weights = np.where(kt == 0, 1.0, 2.0) / Q
    analysis = np.concatenate([np.cos(angles), -np.sin(angles)], axis=1)
    synthesis = analysis * np.concatenate([weights, weights])[None, :]
    return analysis.astype(np.float32), synthesis.astype(np.float32)


def three_rows(table):
    high, low = halves(table)
    return np.concatenate([high, high, low], axis=0)


def y_table():
    ky = (np.arange(GX)[None, :] * KYL + np.arange(KYL)[:, None]).reshape(-1)
    f = signed(KY)[ky]
    n = np.arange(NY)
    angles = ((f[:, None] * n[None, :]) % NY) * (2.0 * math.pi / NY)
    c, s = np.cos(angles), np.sin(angles)
    t = np.zeros((2, KY, GY, 2, YL))
    c4, s4 = c.reshape(KY, GY, YL), s.reshape(KY, GY, YL)
    t[0, :, :, 0], t[0, :, :, 1] = c4, s4
    t[1, :, :, 0], t[1, :, :, 1] = -s4, c4
    return t.reshape(2 * KY, GY * 2 * YL)


def x_table():
    f, x = signed(KX), np.arange(XL)
    angles = ((f[None, :] * x[:, None]) % NX) * (2.0 * math.pi / NX)
    t = np.zeros((XL, C, 2, G, 128))
    for c in range(C):
        g, j = divmod(c, CG)
        t[:, c, 0, g, j * KX : (j + 1) * KX] = np.cos(angles)
        t[:, c, 1, g, j * KX : (j + 1) * KX] = np.sin(angles)
    return t.reshape(XC, 2, G * 128)


def twiddle_table():
    f, a = signed(KX), np.arange(GX)
    angles = ((f[None, :] * a[:, None] * XL) % NX) * (2.0 * math.pi / NX)
    t = np.zeros((GX, 8, G, 128), np.float32)
    for j in range(CG):
        t[:, 0, :, j * KX : (j + 1) * KX] = np.cos(angles)[:, None]
        t[:, 1, :, j * KX : (j + 1) * KX] = np.sin(angles)[:, None]
    return t.reshape(GX, 8, G * 128)


def group_tables():
    gather = np.zeros((CG, 128, 128), np.float32)
    spread = np.zeros((128, CG, 128), np.float32)
    eye = np.eye(KX, dtype=np.float32)
    for o in range(CG):
        for i in range(CG):
            gather[o, i * KX : (i + 1) * KX, o * KX : (o + 1) * KX] = eye
            spread[o * KX : (o + 1) * KX, o, i * KX : (i + 1) * KX] = eye
    return gather.reshape(CG * 128, 128), spread.reshape(128, CG * 128)


def mm(a, b):
    return jnp.dot(a, b, preferred_element_type=F32)


def split(v):
    high = v.astype(BF16)
    return high, (v - high.astype(F32)).astype(BF16)


def call(body, outs, *args, scratch=()):
    return pl.pallas_call(
        body,
        out_shape=outs,
        scratch_shapes=list(scratch),
        compiler_params=pltpu.CompilerParams(vmem_limit_bytes=56 * 2**20),
    )(*args)


def shape(*dims, dtype=F32):
    return jax.ShapeDtypeStruct(dims, dtype)


def pack_modes(c_ref, o_ref):
    for y in range(YL):
        blocks = []
        for t in range(2):
            v = c_ref[t, pl.ds(y, XC, stride=YL), :]
            vt = v.T
            for k in range(4 if t == 0 else 2):
                blocks.append(vt[k * GY : (k + 1) * GY])
        for part in range(2):
            row = jnp.concatenate(
                blocks[part * ML : (part + 1) * ML] + [jnp.zeros((GY, LT * 128 - ML * XC), F32)], axis=1
            )
            for lt in range(LT):
                o_ref[pl.ds(lt * 8 + part * YL + y, GY, stride=64), :] = row[:, lt * 128 : (lt + 1) * 128]


def unpack_modes(r_ref, g_ref):
    for y in range(YL):
        blocks = []
        for part in range(2):
            row = jnp.concatenate(
                [r_ref[pl.ds(lt * 8 + part * YL + y, GY, stride=64), :] for lt in range(LT)], axis=1
            )
            for m in range(ML):
                blocks.append(row[:, m * XC : (m + 1) * XC])
        top = jnp.concatenate(blocks[:4], axis=0)
        low = jnp.concatenate(blocks[4:] + [jnp.zeros((64, XC), F32)], axis=0)
        g_ref[0, pl.ds(y, XC, stride=YL), :] = top.T
        g_ref[1, pl.ds(y, XC, stride=YL), :] = low.T


def analyze_kernel(f_ref, t_ref, o_ref, c_ref):
    def body(i, _):
        v = jnp.concatenate([f_ref[i * 4 + k].reshape(C * YL, Q) for k in range(4)], axis=0)
        r = mm(v, t_ref[...])
        rows = pl.ds(pl.multiple_of(i * 320, 8), 320)
        c_ref[0, rows, :] = r[:, :128]
        c_ref[1, rows, :64] = r[:, 128:]
        return 0

    lax.fori_loop(0, 4, body, 0, unroll=True)
    pack_modes(c_ref, o_ref)


def forward_kernel(r_ref, f_ref, d_ref, w_ref, b_ref, s_ref, t_ref, out_ref, pre_ref, o_ref, g_ref, c_ref, sp_ref):
    unpack_modes(r_ref, g_ref)

    def body(i, _):
        rows = pl.ds(pl.multiple_of(i * 320, 8), 320)
        gh0, gl0 = split(g_ref[0, rows, :])
        gh1, gl1 = split(g_ref[1, rows, :])
        gh1, gl1 = gh1[:, :64], gl1[:, :64]
        lhs = jnp.concatenate([gh0, gh1, gl0, gl1, gh0, gh1], axis=1)
        sp_ref[...] = mm(lhs, s_ref[...])
        for k in range(2):
            x = i * 4 + 2 * k
            fv = jnp.concatenate([f_ref[x + h].reshape(C * YL, Q) for h in range(2)], axis=0)
            dv = jnp.concatenate([d_ref[x + h].reshape(C * YL, Q) for h in range(2)], axis=0)
            before = sp_ref[k * 160 : (k + 1) * 160, :] + mm(w_ref[...], fv) + b_ref[...]
            square = before * before
            tangent = jnp.tanh(before * (GELU_SCALE + (GELU_SCALE * GELU_CUBIC) * square))
            half = 0.5 + 0.5 * tangent
            result = before * half
            slope = half + result * (1.0 - tangent) * (GELU_SCALE + (3.0 * GELU_SCALE * GELU_CUBIC) * square)
            result = result.astype(BF16)
            pre = (dv.astype(F32) * slope).astype(BF16)
            for h in range(2):
                out_ref[x + h] = result[h * 80 : (h + 1) * 80].reshape(C, YL, Q)
            pre_ref[pl.ds(pl.multiple_of(x * 80, 16), 160), :] = pre
        r = mm(pre_ref[rows, :], t_ref[...])
        c_ref[0, rows, :] = r[:, :128]
        c_ref[1, rows, :64] = r[:, 128:]
        return 0

    lax.fori_loop(0, 4, body, 0)
    pack_modes(c_ref, o_ref)


def backward_kernel(r_ref, pre_ref, w_ref, s_ref, out_ref, g_ref, sp_ref):
    unpack_modes(r_ref, g_ref)

    def body(i, _):
        rows = pl.ds(pl.multiple_of(i * 320, 8), 320)
        gh0, gl0 = split(g_ref[0, rows, :])
        gh1, gl1 = split(g_ref[1, rows, :])
        gh1, gl1 = gh1[:, :64], gl1[:, :64]
        lhs = jnp.concatenate([gh0, gh1, gl0, gl1, gh0, gh1], axis=1)
        sp_ref[...] = mm(lhs, s_ref[...])
        for k in range(2):
            x = i * 4 + 2 * k
            pv = pre_ref[pl.ds(pl.multiple_of(x * 80, 16), 160), :]
            total = (sp_ref[k * 160 : (k + 1) * 160, :] + mm(w_ref[...], pv)).astype(BF16)
            for h in range(2):
                out_ref[x + h] = total[h * 80 : (h + 1) * 80].reshape(C, YL, Q)
        return 0

    lax.fori_loop(0, 4, body, 0)


def inward_kernel(r_ref, yh_ref, yl_ref, xh_ref, xl_ref, tw_ref, o_ref):
    tiles = []
    for lt in range(LT):
        v = r_ref[:, lt * 8 : (lt + 1) * 8, :].reshape(GY * 8, 128)
        vh, vl = split(v)
        tiles.append(mm(yh_ref[...], vh) + (mm(yh_ref[...], vl) + mm(yl_ref[...], vh)))
    row = jnp.concatenate(tiles, axis=1)
    y1 = jnp.concatenate([row[:, m * XC : (m + 1) * XC] for m in range(ML)], axis=0)
    vh, vl = split(y1)
    p = mm(vh, xh_ref[...]) + (mm(vl, xh_ref[...]) + mm(vh, xl_ref[...]))
    tc, ts = tw_ref[0:1, :], tw_ref[1:2, :]
    for m in range(ML):
        re, im = p[m * 48 : m * 48 + 24], p[m * 48 + 24 : m * 48 + 48]
        real = re[:, :512] + im[:, 512:]
        imag = im[:, :512] - re[:, 512:]
        parts = (real * tc + imag * ts, imag * tc - real * ts)
        for part in range(2):
            for ky in range(KYL):
                for g in range(G):
                    o_ref[pl.ds(g * 18 + part * 9 + ky * ML + m, GX, stride=ROWS), :] = parts[part][
                        ky * 8 : (ky + 1) * 8, g * 128 : (g + 1) * 128
                    ]


def outward_kernel(z_ref, xh_ref, xl_ref, y_ref, tw_ref, o_ref):
    tc, ts = tw_ref[0:1, :], tw_ref[1:2, :]
    rows = []
    for m in range(ML):
        parts = []
        for part in range(2):
            parts.append(
                jnp.concatenate(
                    [
                        jnp.concatenate(
                            [
                                z_ref[pl.ds(g * 18 + part * 9 + ky * ML + m, GX, stride=ROWS), :]
                                for g in range(G)
                            ],
                            axis=1,
                        )
                        for ky in range(KYL)
                    ],
                    axis=0,
                )
            )
        re, im = parts
        rows += [re * tc - im * ts, re * ts + im * tc]
    v = jnp.concatenate(rows, axis=0)
    vh, vl = split(v)
    p = mm(vh, xh_ref[...]) + (mm(vl, xh_ref[...]) + mm(vh, xl_ref[...]))
    tops, lows = [], []
    for m in range(ML):
        re, im = p[m * 48 : m * 48 + 24], p[m * 48 + 24 : m * 48 + 48]
        tops.append(re[:, :XC] - im[:, 384 : 384 + XC])
        lows.append(re[:, 384 : 384 + XC] + im[:, :XC])
    pad = [jnp.zeros((24, LT * 128 - ML * XC), F32)]
    v = jnp.concatenate([jnp.concatenate(tops + pad, axis=1), jnp.concatenate(lows + pad, axis=1)], axis=0)
    vh, vl = split(v)
    v3 = jnp.concatenate([vh, vl, vh], axis=0)
    for lt in range(LT):
        o = mm(y_ref[...], v3[:, lt * 128 : (lt + 1) * 128])
        o_ref[:, lt * 8 : (lt + 1) * 8, :] = o.reshape(GY, 8, 128)


def part_rows(ref, g, part):
    return ref[g * 18 + part * 9 : g * 18 + part * 9 + 9, :]


def send_all(o_ref, r_ref):
    for a in range(GX):
        o_ref[a] = r_ref[...]


def mix_kernel(q_ref, w_ref, e_ref, u_ref, o_ref, l_ref, r_ref):
    total = q_ref[0]
    for a in range(1, GX):
        total = total + q_ref[a]
    u_ref[...] = total
    us = [[part_rows(u_ref, g, part) for part in range(2)] for g in range(G)]
    l_ref[...] = jnp.zeros_like(l_ref)
    for o in range(C):
        real = imag = None
        for g in range(G):
            wr, wi = w_ref[o, g, 0], w_ref[o, g, 1]
            ur, ui = us[g]
            a, b = wr * ur - wi * ui, wr * ui + wi * ur
            real, imag = (a, b) if real is None else (real + a, imag + b)
        gi, oi = divmod(o, CG)
        l_ref[gi * 32 : gi * 32 + 9, oi * 128 : (oi + 1) * 128] = real
        l_ref[gi * 32 + 16 : gi * 32 + 25, oi * 128 : (oi + 1) * 128] = imag
    vh, vl = split(l_ref[...])
    v = (mm(vh, e_ref[...]) + mm(vl, e_ref[...])) * SCALE
    for g in range(G):
        for part in range(2):
            r_ref[g * 18 + part * 9 : g * 18 + part * 9 + 9, :] = v[g * 32 + part * 16 : g * 32 + part * 16 + 9]
    send_all(o_ref, r_ref)


def unmix_kernel(q_ref, w_ref, e_ref, s_ref, o_ref, l_ref, r_ref):
    total = q_ref[0]
    for a in range(1, GX):
        total = total + q_ref[a]
    r_ref[...] = total * SCALE
    l_ref[...] = jnp.zeros_like(l_ref)
    for g in range(G):
        for part in range(2):
            l_ref[g * 32 + part * 16 : g * 32 + part * 16 + 9, :] = part_rows(r_ref, g, part)
    vh, vl = split(l_ref[...])
    s_ref[...] = mm(vh, e_ref[...]) + mm(vl, e_ref[...])
    acc = [[None, None] for _ in range(G)]
    for o in range(C):
        gi, oi = divmod(o, CG)
        gr = s_ref[gi * 32 : gi * 32 + 9, oi * 128 : (oi + 1) * 128]
        gm = s_ref[gi * 32 + 16 : gi * 32 + 25, oi * 128 : (oi + 1) * 128]
        for g in range(G):
            wr, wi = w_ref[o, g, 0], w_ref[o, g, 1]
            a, b = wr * gr + wi * gm, wr * gm - wi * gr
            acc[g] = [a, b] if acc[g][0] is None else [acc[g][0] + a, acc[g][1] + b]
    for g in range(G):
        for part in range(2):
            r_ref[g * 18 + part * 9 : g * 18 + part * 9 + 9, :] = acc[g][part]
    send_all(o_ref, r_ref)


def outer_kernel(u_ref, s_ref, o_ref):
    us = [[part_rows(u_ref, g, part) for part in range(2)] for g in range(G)]
    for o in range(C):
        gi, oi = divmod(o, CG)
        gr = s_ref[gi * 32 : gi * 32 + 9, oi * 128 : (oi + 1) * 128]
        gm = s_ref[gi * 32 + 16 : gi * 32 + 25, oi * 128 : (oi + 1) * 128]
        for g in range(G):
            ur, ui = us[g]
            o_ref[o, g, 0] = gr * ur + gm * ui
            o_ref[o, g, 1] = gm * ur - gr * ui


def per_device(field, cotangent, spectral_weight, pointwise_weight, channel_bias):
    analysis, synthesis = zt_tables()
    toward = jnp.asarray(analysis.astype(jnp.bfloat16))
    toward_back = jnp.asarray(synthesis.astype(jnp.bfloat16))
    outward = jnp.asarray(three_rows(synthesis.T))
    outward_back = jnp.asarray(three_rows(analysis.T))
    ytab = y_table()
    y_in = [jnp.asarray(t) for t in halves(ytab)]
    yh, yl = halves(ytab.T)
    y_out = jnp.asarray(np.concatenate([yh, yh, yl], axis=1))
    xtab = x_table()
    x_in = [jnp.asarray(t) for t in halves(xtab.reshape(XC, 2 * G * 128))]
    xt = np.zeros((G * 128, 2, 384))
    xt[:, :, :XC] = np.transpose(xtab, (2, 1, 0))
    x_out = [jnp.asarray(t) for t in halves(xt.reshape(G * 128, 768))]
    gather, spread = group_tables()
    gather, spread = jnp.asarray(gather.astype(jnp.bfloat16)), jnp.asarray(spread.astype(jnp.bfloat16))
    twiddle = lax.dynamic_index_in_dim(jnp.asarray(twiddle_table()), lax.axis_index("gx"), 0, keepdims=False)

    f = jnp.transpose(field, (0, 2, 1, 3))
    d = jnp.transpose(cotangent, (0, 2, 1, 3))
    eye = jnp.eye(2, dtype=BF16)
    eye_y = jnp.eye(YL, dtype=BF16)
    mix_in = jnp.einsum("hk,io,yw->hoykiw", eye, pointwise_weight, eye_y).reshape(160, 160)
    mix_back = jnp.einsum("hk,io,yw->hiykow", eye, pointwise_weight, eye_y).reshape(160, 160)
    bias = jnp.broadcast_to(channel_bias[None, :, None], (2, C, YL)).reshape(160, 1)
    w = spectral_weight.reshape(2, G, CG, C, KX, KYL, ML)
    w = jnp.transpose(w, (3, 1, 0, 5, 6, 2, 4)).reshape(C, G, 2, MODES, KC)
    w = jnp.pad(w, ((0, 0),) * 4 + ((0, 128 - KC),))

    def over_y(v):
        return lax.all_to_all(v.reshape(GY, 64, 128), "gy", split_axis=0, concat_axis=0, tiled=True)

    def over_x(v):
        return lax.all_to_all(v.reshape(GX, ROWS, 128), "gx", split_axis=0, concat_axis=0, tiled=True)

    def inward(v):
        return over_x(call(inward_kernel, shape(GX * ROWS, 128), over_y(v), *y_in, *x_in, twiddle))

    def spread_out(v):
        v = over_x(v).reshape(GX * ROWS, 128)
        v = call(outward_kernel, shape(GY, 64, 128), v, *x_out, y_out, twiddle)
        return over_y(v).reshape(GY * 64, 128)

    cells = pltpu.VMEM((2, CELLS, 128), F32)
    part = pltpu.VMEM((320, Q), F32)
    rows = pltpu.VMEM((ROWS, 128), F32)
    v = call(analyze_kernel, shape(GY * 64, 128), f, toward, scratch=[cells])
    v = inward(v)
    u, v = call(
        mix_kernel, (shape(ROWS, 128), shape(GX, ROWS, 128)), v, w, gather,
        scratch=[pltpu.VMEM((128, CG * 128), F32), rows],
    )
    v = spread_out(v)
    output, pre, v = call(
        forward_kernel,
        (shape(XL, C, YL, Q, dtype=BF16), shape(CELLS, Q, dtype=BF16), shape(GY * 64, 128)),
        v, f, d, mix_in, bias, outward, toward_back,
        scratch=[cells, cells, part],
    )
    v = inward(v)
    s, v = call(
        unmix_kernel, (shape(128, CG * 128), shape(GX, ROWS, 128)), v, w, spread,
        scratch=[pltpu.VMEM((128, 128), F32), rows],
    )
    gw = call(outer_kernel, shape(C, G, 2, MODES, 128), u, s)
    gw = gw[..., :KC].reshape(C, G, 2, KYL, ML, CG, KX)
    grad_weight = jnp.transpose(gw, (2, 1, 5, 0, 6, 3, 4)).reshape(2, C, C, KX, KYL, ML)
    v = spread_out(v)
    grad_field = call(
        backward_kernel, shape(XL, C, YL, Q, dtype=BF16), v, pre, mix_back, outward_back,
        scratch=[cells, part],
    )
    return (jnp.transpose(output, (0, 2, 1, 3)), jnp.transpose(grad_field, (0, 2, 1, 3)), grad_weight)


def solution(mesh):
    grid = P("gx", "gy", None, None)
    modes = P(None, None, None, None, "gx", "gy")
    return jax.shard_map(
        per_device,
        mesh=mesh,
        in_specs=(grid, grid, modes, P(), P()),
        out_specs=(grid, grid, modes),
        check_vma=False,
    )
```

time: 575 us -> 245 us (0.43)
  waiting for transfers between devices: 212 us -> 61.6 us
  local copies, waits for them, and re-layouts: 169 us -> 36.6 us
  matrix products: 75.3 us -> 0 us
  Pallas kernels: 0 us -> 48.6 us
  blocking collectives: 29.2 us -> 70 us
  other arithmetic: 29.6 us -> 0.41 us
  between operations: 15.8 us -> 0.71 us
  starting transfers between devices: 37.7 us -> 26 us
    unnamed x4 -> x0, waiting for transfers between devices: 127 us -> none
    unnamed x65 -> x12, local copies, waits for them, and re-layouts: 107 us -> 3.65 us
    dot_general x14 -> x0, matrix products: 75.3 us -> none  [the longest x8 35.8 us: along_last(): product = jnp.dot(flat, table, precision=HIGHEST_PRECISION)]
    all_to_all x0 -> x4, blocking collectives: none -> 70 us  [the longest x3 36.6 us: over_x(): lax.all_to_all(v.reshape(GX, ROWS, 128), 'gx', split_axis=0, concat_axis=...]
    pallas_call x0 -> x10, Pallas kernels: none -> 48.6 us  [call(): pl.pallas_call(body, out_shape=outs, scratch_shapes=list(scratch), compil...]
    all_gather x2 -> x0, blocking collectives: 29.2 us -> none  [synthesize(): spectrum_stack = lax.all_gather(spectrum_stack, 'gx', axis=1, tiled=True)]
    all_to_all x4, waiting for transfers between devices: 84.4 us -> 61.6 us  [the longest x3 61.6 us: over_y(): lax.all_to_all(v.reshape(GY, 64, 128), 'gy', split_axis=0, concat_axis=0,...]
    all_to_all x9 -> x0, local copies, waits for them, and re-layouts: 19.1 us -> none  [the longest x5 10.2 us: analyze(): lax.all_to_all(spectrum_stack, 'gy', split_axis=0, concat_axis=4, tiled=T...]
  transfers between devices with their start and end apart: 6 -> 4, of which waited for: 6 -> 3; matrix products, arithmetic and copies ran while one was open for 4% -> 14% of each run, Pallas kernels for 0% -> 1%
where the time goes in v1:
time: 245 us; the launch traced here: 244 us
  blocking collectives  70 us (29%)
  waiting for transfers between devices  61.6 us (25%)
  Pallas kernels  48.6 us (20%)
  local copies, waits for them, and re-layouts  36.6 us (15%)
  starting transfers between devices  26 us (11%)
    all_to_all x3, waiting for transfers between devices, over_y(): lax.all_to_all(v.reshape(GY, 64, 128), 'gy', split_axis=0, concat_axis=0,...  61.6 us
    pallas_call x10, Pallas kernels, call(): pl.pallas_call(body, out_shape=outs, scratch_shapes=list(scratch), compil...  48.6 us
    all_to_all x3, blocking collectives, over_x(): lax.all_to_all(v.reshape(GX, ROWS, 128), 'gx', split_axis=0, concat_axis=...  36.6 us
    all_to_all x1, blocking collectives, over_y(): lax.all_to_all(v.reshape(GY, 64, 128), 'gy', split_axis=0, concat_axis=0,...  33.3 us
    all_to_all x3, starting transfers between devices, over_y(): lax.all_to_all(v.reshape(GY, 64, 128), 'gy', split_axis=0, concat_axis=0,...  21.7 us
    transpose x1, local copies, waits for them, and re-layouts, per_device(): jnp.transpose(gw, (2, 1, 5, 0, 6, 3, 4)).reshape(2, C, C, KX, KYL, ML)  6.41 us
    reshape x1, local copies, waits for them, and re-layouts, per_device(): w = spectral_weight.reshape(2, G, CG, C, KX, KYL, ML)  5.7 us
  transfers between devices with their start and end apart: 4, of which 3 were waited for; matrix products, arithmetic and copies ran while one was open for 14% of the time, Pallas kernels for 1%

profile of v1, /device:TPU:32, one launch (start us, length us, event | category | flops | bytes accessed | tf_op | source)
XLA Modules:
  0.0 243.9 jit_solution(4521420339733368998)
XLA Ops:
  0.6 4.5 %shard_map.202 = f32[2048,128]{1,0:T(8,128)} custom-call(bf16[16,20,4,1024]{3,2,1,0:T(4,128)(2,1)} %bitcast.31, bf16[1024,192]{1,0:T(8,128)(2,1)} %constant.43.clone.t_ref), custom_call_target="tpu_custom_call" | custom-call | tf_op jit(solution)/shard_map/pallas_call | solution.py:129
  5.2 11.4 %all-to-all-start = ((f32[32,64,128]{2,1,0:T(8,128)}), f32[32,64,128]{2,1,0:T(8,128)S(1)}, u32[]{:S(2)}, u32[]{:S(2)}) async-start(f32[32,64,128]{2,1,0:T(8,128)} %bitcast.35), calls=%async_computation | async-start | bytes 2097152 | tf_op jit(solution)/shard_map/all_to_all | solution.py:407
  16.5 1.3 dynamic-slice_bitcast_fusion.tw_ref
  17.9 27.2 %all-to-all-done.r_ref = f32[32,64,128]{2,1,0:T(8,128)S(1)} async-done(((f32[32,64,128]{2,1,0:T(8,128)}), f32[32,64,128]{2,1,0:T(8,128)S(1)}, u32[]{:S(2)}, u32[]{:S(2)}) %all-to-all-start) | async-done | bytes 1048608 | tf_op jit(solution)/shard_map/all_to_all | solution.py:407
  45.1 0.0 copy-start.1
  45.1 1.0 copy-done.1
  46.0 3.3 %shard_map.203 = f32[576,128]{1,0:T(8,128)} custom-call(f32[32,64,128]{2,1,0:T(8,128)} %copy-done.1, bf16[48,256]{1,0:T(8,128)(2,1)} %constant.47.clone.yh_ref, bf16[48,256]{1,0:T(8,128)(2,1)} %constant.48.clone.yl_ref, bf16[320,1024]{1,0:T(8,128)(2,1)} %constant.50.clone.xh_ref, bf16[320,1024]{1,0:T(8,128)(2,1)} %constant.51.clone.xl_ref, ...), custom_call_target="tpu_custom_call" | custom-call | tf_op jit(solution)/shard_map/pallas_call | solution.py:129
  49.3 4.3 %all-to-all-start.1 = ((f32[8,72,128]{2,1,0:T(8,128)}), f32[8,72,128]{2,1,0:T(8,128)S(1)}, u32[]{:S(2)}, u32[]{:S(2)}) async-start(f32[8,72,128]{2,1,0:T(8,128)} %bitcast.43), calls=%async_computation.1 | async-start | bytes 589824 | tf_op jit(solution)/shard_map/all_to_all | solution.py:410
  53.6 5.7 %copy.37 = f32[2,4,5,20,24,3,3]{4,2,0,6,5,1,3:T(8,128)} copy(f32[2,4,5,20,24,3,3]{4,0,6,5,3,2,1:T(2,128)} %bitcast.37) | data formatting | bytes 1382400 | tf_op jit(solution)/shard_map/reshape | solution.py:402
  59.3 4.3 %reshape.55 = f32[20,4,2,9,120]{4,2,3,1,0:T(2,128)S(1)} reshape(f32[20,4,2,3,3,5,24]{6,5,2,4,3,1,0:T(8,128)} %bitcast.30) | data formatting | bytes 1382400 | tf_op jit(solution)/shard_map/reshape | solution.py:403
  63.6 0.2 copy.31
  63.8 1.3 pad.4.w_ref
  65.1 0.0 all-to-all-done.1.q_ref
  65.1 0.0 copy-start.3
  65.1 0.7 copy-done.3
  65.8 2.6 %shard_map.204 = (f32[72,128]{1,0:T(8,128)}, f32[8,72,128]{2,1,0:T(8,128)}) custom-call(f32[8,72,128]{2,1,0:T(8,128)} %copy-done.3, f32[20,4,2,9,128]{4,3,2,1,0:T(8,128)} %pad.4.w_ref, bf16[640,128]{1,0:T(8,128)(2,1)} %constant.54.clone.e_ref), custom_call_target="tpu_custom_call" | custom-call | tf_op jit(solution)/shard_map/pallas_call | solution.py:129
  68.4 12.8 %all_to_all.40 = f32[8,72,128]{2,1,0:T(8,128)} all-to-all(f32[8,72,128]{2,1,0:T(8,128)} %get-tuple-element.10), channel_id=1, replica_groups=mesh['gx'=8,'gy'=32] {'gx'}, dimensions={0} | all-to-all | bytes 589824 | tf_op jit(solution)/shard_map/all_to_all | solution.py:410
  81.2 0.0 copy-start.5
  81.2 0.0 copy-start.4
  81.2 3.6 %shard_map.205 = f32[32,64,128]{2,1,0:T(8,128)} custom-call(f32[576,128]{1,0:T(8,128)} %bitcast.42, bf16[512,768]{1,0:T(8,128)(2,1)} %constant.52.clone.xh_ref, bf16[512,768]{1,0:T(8,128)(2,1)} %constant.53.clone.xl_ref, bf16[256,144]{1,0:T(8,128)(2,1)} %constant.49.clone.y_ref, f32[8,512]{1,0:T(8,128)} %dynamic-slice_bitcast_fusion.tw_ref), custom_call_target="tpu_custom_call" | custom-call | tf_op jit(solution)/shard_map/pallas_call | solution.py:129
  84.8 5.2 %all-to-all-start.3 = ((f32[32,64,128]{2,1,0:T(8,128)}), f32[32,64,128]{2,1,0:T(8,128)S(1)}, u32[]{:S(2)}, u32[]{:S(2)}) async-start(f32[32,64,128]{2,1,0:T(8,128)} %shard_map.205), calls=%async_computation.3 | async-start | bytes 2097152 | tf_op jit(solution)/shard_map/all_to_all | solution.py:407
  90.0 0.0 copy-done.5
  90.0 0.1 broadcast_in_dim.2
  90.0 0.7 reshape.67.b_ref
  90.8 0.1 broadcast_multiply_fusion
  90.8 0.0 copy-done.4
  90.8 0.3 multiply_bitcast_fusion
  91.2 2.4 copy.32
  93.5 3.3 %reshape.58.w_ref = bf16[160,160]{1,0:T(8,128)(2,1)} reshape(bf16[2,20,4,2,20,4]{5,4,3,2,1,0:T(8,128)(2,1)} %copy.32) | data formatting | bytes 102400 | tf_op jit(solution)/shard_map/reshape | solution.py:399
  96.8 21.7 %all-to-all-done.3 = f32[32,64,128]{2,1,0:T(8,128)S(1)} async-done(((f32[32,64,128]{2,1,0:T(8,128)}), f32[32,64,128]{2,1,0:T(8,128)S(1)}, u32[]{:S(2)}, u32[]{:S(2)}) %all-to-all-start.3) | async-done | bytes 1048608 | tf_op jit(solution)/shard_map/all_to_all | solution.py:407
  118.6 0.0 copy-start.2
  118.6 1.0 copy-done.2
  119.6 14.3 %shard_map.206 = (bf16[16,20,4,1024]{3,2,1,0:T(4,128)(2,1)}, bf16[1280,1024]{1,0:T(8,128)(2,1)}, f32[2048,128]{1,0:T(8,128)}) custom-call(f32[2048,128]{1,0:T(8,128)} %bitcast.36, bf16[16,20,4,1024]{3,2,1,0:T(4,128)(2,1)} %bitcast.32, bf16[16,20,4,1024]{3,2,1,0:T(4,128)(2,1)} %bitcast.40, bf16[160,160]{1,0:T(8,128)(2,1)} %reshape.58.w_ref, ...), custom_call_target="tpu_custom_call" | custom-call | tf_op jit(solution)/shard_map/pallas_call | solution.py:129
  133.8 33.3 %all_to_all.41.r_ref = f32[32,64,128]{2,1,0:T(8,128)} all-to-all(f32[32,64,128]{2,1,0:T(8,128)} %bitcast.45), channel_id=1, replica_groups=mesh['gx'=8,'gy'=32] {'gy'}, dimensions={0} | all-to-all | bytes 2097152 | tf_op jit(solution)/shard_map/all_to_all | solution.py:407
  167.2 3.3 %shard_map.207 = f32[576,128]{1,0:T(8,128)} custom-call(f32[32,64,128]{2,1,0:T(8,128)} %all_to_all.41.r_ref, bf16[48,256]{1,0:T(8,128)(2,1)} %constant.47.clone.yh_ref, bf16[48,256]{1,0:T(8,128)(2,1)} %constant.48.clone.yl_ref, bf16[320,1024]{1,0:T(8,128)(2,1)} %constant.50.clone.xh_ref, bf16[320,1024]{1,0:T(8,128)(2,1)} %constant.51.clone.xl_ref, ...), custom_call_target="tpu_custom_call" | custom-call | tf_op jit(solution)/shard_map/pallas_call | solution.py:129
  170.5 11.9 %all_to_all.42.q_ref = f32[8,72,128]{2,1,0:T(8,128)} all-to-all(f32[8,72,128]{2,1,0:T(8,128)} %bitcast.44), channel_id=1, replica_groups=mesh['gx'=8,'gy'=32] {'gx'}, dimensions={0} | all-to-all | bytes 589824 | tf_op jit(solution)/shard_map/all_to_all | solution.py:410
  182.4 2.6 %shard_map.208 = (f32[128,640]{1,0:T(8,128)}, f32[8,72,128]{2,1,0:T(8,128)}) custom-call(f32[8,72,128]{2,1,0:T(8,128)} %all_to_all.42.q_ref, f32[20,4,2,9,128]{4,3,2,1,0:T(8,128)} %pad.4.w_ref, bf16[128,640]{1,0:T(8,128)(2,1)} %constant.55.clone.e_ref), custom_call_target="tpu_custom_call" | custom-call | tf_op jit(solution)/shard_map/pallas_call | solution.py:129
  185.0 11.9 %all_to_all.43 = f32[8,72,128]{2,1,0:T(8,128)} all-to-all(f32[8,72,128]{2,1,0:T(8,128)} %get-tuple-element.13), channel_id=1, replica_groups=mesh['gx'=8,'gy'=32] {'gx'}, dimensions={0} | all-to-all | bytes 589824 | tf_op jit(solution)/shard_map/all_to_all | solution.py:410
  196.9 3.7 %shard_map.209 = f32[32,64,128]{2,1,0:T(8,128)} custom-call(f32[576,128]{1,0:T(8,128)} %bitcast.41, bf16[512,768]{1,0:T(8,128)(2,1)} %constant.52.clone.xh_ref, bf16[512,768]{1,0:T(8,128)(2,1)} %constant.53.clone.xl_ref, bf16[256,144]{1,0:T(8,128)(2,1)} %constant.49.clone.y_ref, f32[8,512]{1,0:T(8,128)} %dynamic-slice_bitcast_fusion.tw_ref), custom_call_target="tpu_custom_call" | custom-call | tf_op jit(solution)/shard_map/pallas_call | solution.py:129
  200.6 5.2 %all-to-all-start.7 = ((f32[32,64,128]{2,1,0:T(8,128)}), f32[32,64,128]{2,1,0:T(8,128)S(1)}, u32[]{:S(2)}, u32[]{:S(2)}) async-start(f32[32,64,128]{2,1,0:T(8,128)} %shard_map.209), calls=%async_computation.7 | async-start | bytes 2097152 | tf_op jit(solution)/shard_map/all_to_all | solution.py:407
  205.8 2.1 reshape.64.w_ref
  207.9 2.2 shard_map.211
  210.1 1.7 copy.34
  211.8 3.6 %reshape.65 = f32[20,4,2,3,3,5,24]{6,5,2,4,3,1,0:T(8,128)} reshape(f32[20,4,2,9,120]{4,2,3,1,0:T(2,128)S(1)} %copy.34) | data formatting | bytes 1382400 | tf_op jit(solution)/shard_map/reshape | solution.py:442
  215.4 6.4 %copy.35 = f32[2,4,5,20,24,3,3]{4,0,6,5,3,2,1:T(2,128)} copy(f32[2,4,5,20,24,3,3]{4,2,0,6,5,1,3:T(8,128)} %bitcast.29) | data formatting | bytes 1382400 | tf_op jit(solution)/shard_map/transpose | solution.py:443
  221.8 12.6 %all-to-all-done.7 = f32[32,64,128]{2,1,0:T(8,128)S(1)} async-done(((f32[32,64,128]{2,1,0:T(8,128)}), f32[32,64,128]{2,1,0:T(8,128)S(1)}, u32[]{:S(2)}, u32[]{:S(2)}) %all-to-all-start.7) | async-done | bytes 1048608 | tf_op jit(solution)/shard_map/all_to_all | solution.py:407
  234.4 1.0 copy-done
  235.4 8.5 %shard_map.210 = bf16[16,20,4,1024]{3,2,1,0:T(4,128)(2,1)} custom-call(f32[2048,128]{1,0:T(8,128)} %bitcast.34, bf16[1280,1024]{1,0:T(8,128)(2,1)} %get-tuple-element.14.pre_ref, bf16[160,160]{1,0:T(8,128)(2,1)} %reshape.64.w_ref, bf16[576,1024]{1,0:T(8,128)(2,1)} %constant.46.clone.s_ref), custom_call_target="tpu_custom_call" | custom-call | tf_op jit(solution)/shard_map/pallas_call | solution.py:129
  (3 shorter events, 0.0 us)
Async XLA Ops:
  5.2 39.9 %all-to-all-start = ((f32[32,64,128]{2,1,0:T(8,128)}), f32[32,64,128]{2,1,0:T(8,128)S(1)}, u32[]{:S(2)}, u32[]{:S(2)}) async-start(f32[32,64,128]{2,1,0:T(8,128)} %bitcast.35), calls=%async_computation | async-start | bytes 2097152 | tf_op jit(solution)/shard_map/all_to_all | solution.py:407
  45.1 1.0 copy-start.1
  49.3 15.7 %all-to-all-start.1 = ((f32[8,72,128]{2,1,0:T(8,128)}), f32[8,72,128]{2,1,0:T(8,128)S(1)}, u32[]{:S(2)}, u32[]{:S(2)}) async-start(f32[8,72,128]{2,1,0:T(8,128)} %bitcast.43), calls=%async_computation.1 | async-start | bytes 589824 | tf_op jit(solution)/shard_map/all_to_all | solution.py:410
  65.1 0.7 copy-start.3
  81.2 8.8 %copy-start.5 = (f32[20]{0:T(128)S(1)}, f32[20]{0:T(128)}, u32[]{:S(2)}) copy-start(f32[20]{0:T(128)} %param.23) | copy-start | bytes 244
  81.2 9.7 %copy-start.4 = (bf16[20,20]{1,0:T(8,128)(2,1)S(1)}, bf16[20,20]{1,0:T(8,128)(2,1)}, u32[]{:S(2)}) copy-start(bf16[20,20]{1,0:T(8,128)(2,1)} %param.22) | copy-start | bytes 2404
  84.8 33.8 %all-to-all-start.3 = ((f32[32,64,128]{2,1,0:T(8,128)}), f32[32,64,128]{2,1,0:T(8,128)S(1)}, u32[]{:S(2)}, u32[]{:S(2)}) async-start(f32[32,64,128]{2,1,0:T(8,128)} %shard_map.205), calls=%async_computation.3 | async-start | bytes 2097152 | tf_op jit(solution)/shard_map/all_to_all | solution.py:407
  118.6 1.0 copy-start.2
  200.6 33.8 %all-to-all-start.7 = ((f32[32,64,128]{2,1,0:T(8,128)}), f32[32,64,128]{2,1,0:T(8,128)S(1)}, u32[]{:S(2)}, u32[]{:S(2)}) async-start(f32[32,64,128]{2,1,0:T(8,128)} %shard_map.209), calls=%async_computation.7 | async-start | bytes 2097152 | tf_op jit(solution)/shard_map/all_to_all | solution.py:407
  234.4 1.0 copy-start

commit v2 on v1

--- a/solution.py
+++ b/solution.py
@@ -28,7 +28,8 @@
 CELLS = XL * C * YL
 Q = NZ * NT
 N = 2 * ML * GY
-LT = 8
+LT = 7
+CHUNK = 60
 G = 4
 CG = C // G
 KC = CG * KX
@@ -81,7 +82,7 @@
     c4, s4 = c.reshape(KY, GY, YL), s.reshape(KY, GY, YL)
     t[0, :, :, 0], t[0, :, :, 1] = c4, s4
     t[1, :, :, 0], t[1, :, :, 1] = -s4, c4
-    return t.reshape(2 * KY, GY * 2 * YL)
+    return np.transpose(t, (0, 1, 3, 4, 2)).reshape(2 * KY, 2 * YL * GY)
 
 
 def x_table():
@@ -125,17 +126,49 @@
     return high, (v - high.astype(F32)).astype(BF16)
 
 
-def call(body, outs, *args, scratch=()):
+def call(body, outs, *args, scratch=(), mib=12):
     return pl.pallas_call(
         body,
         out_shape=outs,
         scratch_shapes=list(scratch),
-        compiler_params=pltpu.CompilerParams(vmem_limit_bytes=56 * 2**20),
+        compiler_params=pltpu.CompilerParams(vmem_limit_bytes=mib * 2**20),
     )(*args)
 
 
 def shape(*dims, dtype=F32):
     return jax.ShapeDtypeStruct(dims, dtype)
+
+
+def held(*dims, dtype=F32):
+    return pltpu.VMEM(dims, dtype)
+
+
+def pin(*values):
+    return [pltpu.with_memory_space_constraint(v, pltpu.VMEM) for v in values]
+
+
+def far(*values):
+    return [pltpu.with_memory_space_constraint(v, pltpu.HBM) for v in values]
+
+
+def fetch_kernel(*refs):
+    count = len(refs) // 2
+    sems = refs[-1]
+    copies = [pltpu.make_async_copy(refs[i], refs[count + i], sems.at[i]) for i in range(count)]
+    for copy in copies:
+        copy.start()
+    for copy in copies:
+        copy.wait()
+
+
+def fetch(*arrays):
+    return pl.pallas_call(
+        fetch_kernel,
+        out_shape=tuple(held(*a.shape, dtype=a.dtype) for a in arrays),
+        in_specs=[pl.BlockSpec(memory_space=pltpu.HBM)] * len(arrays),
+        scratch_shapes=[pltpu.SemaphoreType.DMA((len(arrays),))],
+        compiler_params=pltpu.CompilerParams(vmem_limit_bytes=2**20),
+    )(*far(*arrays))
 
 
 def pack_modes(c_ref, o_ref):
@@ -146,20 +179,22 @@
             vt = v.T
             for k in range(4 if t == 0 else 2):
                 blocks.append(vt[k * GY : (k + 1) * GY])
-        for part in range(2):
-            row = jnp.concatenate(
-                blocks[part * ML : (part + 1) * ML] + [jnp.zeros((GY, LT * 128 - ML * XC), F32)], axis=1
-            )
+        rows = [jnp.concatenate(blocks[part * ML : (part + 1) * ML], axis=1) for part in range(2)]
+        for part in range(2):
             for lt in range(LT):
-                o_ref[pl.ds(lt * 8 + part * YL + y, GY, stride=64), :] = row[:, lt * 128 : (lt + 1) * 128]
+                o_ref[pl.ds(lt * 8 + part * YL + y, GY, stride=CHUNK), :] = rows[part][:, lt * 128 : (lt + 1) * 128]
+        o_ref[pl.ds(LT * 8 + y, GY, stride=CHUNK), :] = jnp.concatenate([r[:, LT * 128 :] for r in rows], axis=1)
 
 
 def unpack_modes(r_ref, g_ref):
     for y in range(YL):
         blocks = []
+        last = r_ref[pl.ds(LT * 8 + y, GY, stride=CHUNK), :]
         for part in range(2):
             row = jnp.concatenate(
-                [r_ref[pl.ds(lt * 8 + part * YL + y, GY, stride=64), :] for lt in range(LT)], axis=1
+                [r_ref[pl.ds(lt * 8 + part * YL + y, GY, stride=CHUNK), :] for lt in range(LT)]
+                + [last[:, part * 64 : part * 64 + 64]],
+                axis=1,
             )
             for m in range(ML):
                 blocks.append(row[:, m * XC : (m + 1) * XC])
@@ -169,83 +204,144 @@
         g_ref[1, pl.ds(y, XC, stride=YL), :] = low.T
 
 
-def analyze_kernel(f_ref, t_ref, o_ref, c_ref):
+def analyze_kernel(f_ref, table_ref, o_ref, c_ref, v_ref, t_ref, sems):
+    table = pltpu.make_async_copy(table_ref, t_ref, sems.at[4])
+    table.start()
+    copies = [pltpu.make_async_copy(f_ref.at[pl.ds(i * 4, 4)], v_ref.at[pl.ds(i * 4, 4)], sems.at[i]) for i in range(4)]
+    for copy in copies:
+        copy.start()
+    table.wait()
+    for i in range(4):
+        copies[i].wait()
+        v = jnp.concatenate([v_ref[i * 4 + k].reshape(C * YL, Q) for k in range(4)], axis=0)
+        r = mm(v, t_ref[...])
+        c_ref[0, i * 320 : (i + 1) * 320, :] = r[:, :128]
+        c_ref[1, i * 320 : (i + 1) * 320, :64] = r[:, 128:]
+    pack_modes(c_ref, o_ref)
+
+
+def widen(table, e_ref, et_ref, mask_ref):
+    tall = mm(e_ref[...], table).astype(BF16)
+    return mm(tall, et_ref[...]).astype(BF16) * mask_ref[...]
+
+
+def linear_kernel(f_ref, d_ref, w_ref, b_ref, e_ref, et_ref, mask_ref, lin_ref, row_ref):
+    mix = widen(w_ref[...], e_ref, et_ref, mask_ref)
+    bias = jnp.sum(e_ref[...].astype(F32) * b_ref[...], axis=1, keepdims=True)
+
     def body(i, _):
-        v = jnp.concatenate([f_ref[i * 4 + k].reshape(C * YL, Q) for k in range(4)], axis=0)
-        r = mm(v, t_ref[...])
-        rows = pl.ds(pl.multiple_of(i * 320, 8), 320)
-        c_ref[0, rows, :] = r[:, :128]
-        c_ref[1, rows, :64] = r[:, 128:]
+        x = 2 * i
+        rows = pl.ds(pl.multiple_of(i * 160, 16), 160)
+        fv = jnp.concatenate([f_ref[x + h].reshape(C * YL, Q) for h in range(2)], axis=0)
+        lin_ref[rows, :] = mm(mix, fv) + bias
+        row_ref[rows, :] = jnp.concatenate([d_ref[x + h].reshape(C * YL, Q) for h in range(2)], axis=0)
         return 0
 
-    lax.fori_loop(0, 4, body, 0, unroll=True)
-    pack_modes(c_ref, o_ref)
-
-
-def forward_kernel(r_ref, f_ref, d_ref, w_ref, b_ref, s_ref, t_ref, out_ref, pre_ref, o_ref, g_ref, c_ref, sp_ref):
+    lax.fori_loop(0, XL // 2, body, 0)
+
+
+def linear_back_kernel(p_ref, w_ref, e_ref, et_ref, mask_ref, lin_ref):
+    mix = widen(w_ref[...], e_ref, et_ref, mask_ref)
+
+    def body(i, _):
+        rows = pl.ds(pl.multiple_of(i * 160, 16), 160)
+        lin_ref[rows, :] = mm(mix, p_ref[rows, :])
+        return 0
+
+    lax.fori_loop(0, XL // 2, body, 0)
+
+
+def synthesis_rows(g_ref, rows):
+    gh0, gl0 = split(g_ref[0, rows, :])
+    gh1, gl1 = split(g_ref[1, rows, :])
+    gh1, gl1 = gh1[:, :64], gl1[:, :64]
+    return jnp.concatenate([gh0, gh1, gl0, gl1, gh0, gh1], axis=1)
+
+
+def pieces(source, target, sems):
+    return [
+        pltpu.make_async_copy(source.at[pl.ds(i * n, n)], target.at[pl.ds(i * n, n)], sems.at[i])
+        for n in [source.shape[0] // 4]
+        for i in range(4)
+    ]
+
+
+def forward_kernel(
+    r_ref, lin_hbm, d_hbm, s_ref, t_hbm, out_hbm, pre_hbm, o_ref,
+    g_ref, c_ref, lin_ref, d_ref, sp_ref, t_ref, out_ref, pre_ref, sems, sem,
+):
+    table = pltpu.make_async_copy(t_hbm, t_ref, sem)
+    lin_in, d_in = pieces(lin_hbm, lin_ref, sems.at[0]), pieces(d_hbm, d_ref, sems.at[1])
+    out_out, pre_out = pieces(out_ref, out_hbm, sems.at[2]), pieces(pre_ref, pre_hbm, sems.at[3])
+    for i in range(4):
+        lin_in[i].start()
+        d_in[i].start()
+        if i == 0:
+            table.start()
     unpack_modes(r_ref, g_ref)
-
-    def body(i, _):
-        rows = pl.ds(pl.multiple_of(i * 320, 8), 320)
-        gh0, gl0 = split(g_ref[0, rows, :])
-        gh1, gl1 = split(g_ref[1, rows, :])
-        gh1, gl1 = gh1[:, :64], gl1[:, :64]
-        lhs = jnp.concatenate([gh0, gh1, gl0, gl1, gh0, gh1], axis=1)
-        sp_ref[...] = mm(lhs, s_ref[...])
-        for k in range(2):
-            x = i * 4 + 2 * k
-            fv = jnp.concatenate([f_ref[x + h].reshape(C * YL, Q) for h in range(2)], axis=0)
-            dv = jnp.concatenate([d_ref[x + h].reshape(C * YL, Q) for h in range(2)], axis=0)
-            before = sp_ref[k * 160 : (k + 1) * 160, :] + mm(w_ref[...], fv) + b_ref[...]
+    table.wait()
+    for i in range(4):
+        rows = slice(i * 320, (i + 1) * 320)
+        sp_ref[...] = mm(synthesis_rows(g_ref, rows), s_ref[...])
+        lin_in[i].wait()
+        d_in[i].wait()
+
+        def body(k, _, i=i):
+            at = pl.ds(pl.multiple_of(i * 320 + k * 80, 16), 80)
+            before = sp_ref[pl.ds(pl.multiple_of(k * 80, 16), 80), :] + lin_ref[at, :]
             square = before * before
             tangent = jnp.tanh(before * (GELU_SCALE + (GELU_SCALE * GELU_CUBIC) * square))
             half = 0.5 + 0.5 * tangent
             result = before * half
             slope = half + result * (1.0 - tangent) * (GELU_SCALE + (3.0 * GELU_SCALE * GELU_CUBIC) * square)
-            result = result.astype(BF16)
-            pre = (dv.astype(F32) * slope).astype(BF16)
-            for h in range(2):
-                out_ref[x + h] = result[h * 80 : (h + 1) * 80].reshape(C, YL, Q)
-            pre_ref[pl.ds(pl.multiple_of(x * 80, 16), 160), :] = pre
+            pre_ref[at, :] = (d_ref[at, :].astype(F32) * slope).astype(BF16)
+            out_ref[i * 4 + k] = result.astype(BF16).reshape(C, YL, Q)
+            return 0
+
+        lax.fori_loop(0, 4, body, 0)
+        out_out[i].start()
+        pre_out[i].start()
         r = mm(pre_ref[rows, :], t_ref[...])
         c_ref[0, rows, :] = r[:, :128]
         c_ref[1, rows, :64] = r[:, 128:]
-        return 0
-
-    lax.fori_loop(0, 4, body, 0)
     pack_modes(c_ref, o_ref)
-
-
-def backward_kernel(r_ref, pre_ref, w_ref, s_ref, out_ref, g_ref, sp_ref):
+    for i in range(4):
+        out_out[i].wait()
+        pre_out[i].wait()
+
+
+def backward_kernel(r_ref, lin_hbm, s_ref, out_hbm, g_ref, sp_ref, lin_ref, out_ref, sems):
+    lin_in, out_out = pieces(lin_hbm, lin_ref, sems.at[0]), pieces(out_ref, out_hbm, sems.at[1])
+    for i in range(4):
+        lin_in[i].start()
     unpack_modes(r_ref, g_ref)
-
-    def body(i, _):
-        rows = pl.ds(pl.multiple_of(i * 320, 8), 320)
-        gh0, gl0 = split(g_ref[0, rows, :])
-        gh1, gl1 = split(g_ref[1, rows, :])
-        gh1, gl1 = gh1[:, :64], gl1[:, :64]
-        lhs = jnp.concatenate([gh0, gh1, gl0, gl1, gh0, gh1], axis=1)
-        sp_ref[...] = mm(lhs, s_ref[...])
-        for k in range(2):
-            x = i * 4 + 2 * k
-            pv = pre_ref[pl.ds(pl.multiple_of(x * 80, 16), 160), :]
-            total = (sp_ref[k * 160 : (k + 1) * 160, :] + mm(w_ref[...], pv)).astype(BF16)
-            for h in range(2):
-                out_ref[x + h] = total[h * 80 : (h + 1) * 80].reshape(C, YL, Q)
-        return 0
-
-    lax.fori_loop(0, 4, body, 0)
-
-
-def inward_kernel(r_ref, yh_ref, yl_ref, xh_ref, xl_ref, tw_ref, o_ref):
+    for i in range(4):
+        rows = slice(i * 320, (i + 1) * 320)
+        sp_ref[...] = mm(synthesis_rows(g_ref, rows), s_ref[...])
+        lin_in[i].wait()
+        for k in range(4):
+            total = sp_ref[k * 80 : (k + 1) * 80, :] + lin_ref[i * 320 + k * 80 : i * 320 + (k + 1) * 80, :]
+            out_ref[i * 4 + k] = total.astype(BF16).reshape(C, YL, Q)
+        out_out[i].start()
+    for i in range(4):
+        out_out[i].wait()
+
+
+def inward_kernel(r_ref, yh_ref, yl_ref, xh_ref, xl_ref, tw_ref, o_ref, copy=None):
+    columns = []
+    for lt in range(LT):
+        columns.append([r_ref[pl.ds(lt * 8 + k, GY, stride=CHUNK), :] for k in range(8)])
+    last = [r_ref[pl.ds(LT * 8 + k, GY, stride=CHUNK), :] for k in range(YL)]
+    columns.append([v[:, :64] for v in last] + [v[:, 64:] for v in last])
     tiles = []
-    for lt in range(LT):
-        v = r_ref[:, lt * 8 : (lt + 1) * 8, :].reshape(GY * 8, 128)
-        vh, vl = split(v)
+    for column in columns:
+        vh, vl = split(jnp.concatenate(column, axis=0))
         tiles.append(mm(yh_ref[...], vh) + (mm(yh_ref[...], vl) + mm(yl_ref[...], vh)))
     row = jnp.concatenate(tiles, axis=1)
     y1 = jnp.concatenate([row[:, m * XC : (m + 1) * XC] for m in range(ML)], axis=0)
     vh, vl = split(y1)
+    if copy is not None:
+        copy.wait()
     p = mm(vh, xh_ref[...]) + (mm(vl, xh_ref[...]) + mm(vh, xl_ref[...]))
     tc, ts = tw_ref[0:1, :], tw_ref[1:2, :]
     for m in range(ML):
@@ -259,6 +355,12 @@
                     o_ref[pl.ds(g * 18 + part * 9 + ky * ML + m, GX, stride=ROWS), :] = parts[part][
                         ky * 8 : (ky + 1) * 8, g * 128 : (g + 1) * 128
                     ]
+
+
+def first_inward_kernel(r_ref, yh_ref, yl_ref, xh_ref, xl_hbm, tw_ref, o_ref, xl_ref, sem):
+    copy = pltpu.make_async_copy(xl_hbm, xl_ref, sem)
+    copy.start()
+    inward_kernel(r_ref, yh_ref, yl_ref, xh_ref, xl_ref, tw_ref, o_ref, copy)
 
 
 def outward_kernel(z_ref, xh_ref, xl_ref, y_ref, tw_ref, o_ref):
@@ -292,13 +394,18 @@
         re, im = p[m * 48 : m * 48 + 24], p[m * 48 + 24 : m * 48 + 48]
         tops.append(re[:, :XC] - im[:, 384 : 384 + XC])
         lows.append(re[:, 384 : 384 + XC] + im[:, :XC])
-    pad = [jnp.zeros((24, LT * 128 - ML * XC), F32)]
-    v = jnp.concatenate([jnp.concatenate(tops + pad, axis=1), jnp.concatenate(lows + pad, axis=1)], axis=0)
+    v = jnp.concatenate([jnp.concatenate(tops, axis=1), jnp.concatenate(lows, axis=1)], axis=0)
     vh, vl = split(v)
     v3 = jnp.concatenate([vh, vl, vh], axis=0)
     for lt in range(LT):
         o = mm(y_ref[...], v3[:, lt * 128 : (lt + 1) * 128])
-        o_ref[:, lt * 8 : (lt + 1) * 8, :] = o.reshape(GY, 8, 128)
+        for k in range(8):
+            o_ref[pl.ds(lt * 8 + k, GY, stride=CHUNK), :] = o[k * GY : (k + 1) * GY]
+    o = mm(y_ref[...], v3[:, LT * 128 :])
+    for k in range(YL):
+        o_ref[pl.ds(LT * 8 + k, GY, stride=CHUNK), :] = jnp.concatenate(
+            [o[k * GY : (k + 1) * GY], o[(YL + k) * GY : (YL + k + 1) * GY]], axis=1
+        )
 
 
 def part_rows(ref, g, part):
@@ -394,58 +501,88 @@
 
     f = jnp.transpose(field, (0, 2, 1, 3))
     d = jnp.transpose(cotangent, (0, 2, 1, 3))
-    eye = jnp.eye(2, dtype=BF16)
-    eye_y = jnp.eye(YL, dtype=BF16)
-    mix_in = jnp.einsum("hk,io,yw->hoykiw", eye, pointwise_weight, eye_y).reshape(160, 160)
-    mix_back = jnp.einsum("hk,io,yw->hiykow", eye, pointwise_weight, eye_y).reshape(160, 160)
-    bias = jnp.broadcast_to(channel_bias[None, :, None], (2, C, YL)).reshape(160, 1)
+    row_channel = (np.arange(160) // YL) % C
+    pick = (row_channel[:, None] == np.arange(C)[None, :]).astype(jnp.bfloat16)
+    cell = (np.arange(160) // (C * YL)) * YL + np.arange(160) % YL
+    wide = [jnp.asarray(v) for v in (pick, pick.T, (cell[:, None] == cell[None, :]).astype(jnp.bfloat16))]
     w = spectral_weight.reshape(2, G, CG, C, KX, KYL, ML)
     w = jnp.transpose(w, (3, 1, 0, 5, 6, 2, 4)).reshape(C, G, 2, MODES, KC)
     w = jnp.pad(w, ((0, 0),) * 4 + ((0, 128 - KC),))
 
+    hbm, vmem = pl.BlockSpec(memory_space=pltpu.HBM), pl.BlockSpec(memory_space=pltpu.VMEM)
+
     def over_y(v):
-        return lax.all_to_all(v.reshape(GY, 64, 128), "gy", split_axis=0, concat_axis=0, tiled=True)
+        return lax.all_to_all(v.reshape(GY, 1, CHUNK * 128), "gy", split_axis=0, concat_axis=0, tiled=True).reshape(
+            GY * CHUNK, 128
+        )
 
     def over_x(v):
         return lax.all_to_all(v.reshape(GX, ROWS, 128), "gx", split_axis=0, concat_axis=0, tiled=True)
 
-    def inward(v):
-        return over_x(call(inward_kernel, shape(GX * ROWS, 128), over_y(v), *y_in, *x_in, twiddle))
-
-    def spread_out(v):
-        v = over_x(v).reshape(GX * ROWS, 128)
-        v = call(outward_kernel, shape(GY, 64, 128), v, *x_out, y_out, twiddle)
-        return over_y(v).reshape(GY * 64, 128)
+    def outward_part(v):
+        return call(outward_kernel, shape(GY * CHUNK, 128), over_x(v).reshape(GX * ROWS, 128), *x_out, y_out, twiddle)
 
     cells = pltpu.VMEM((2, CELLS, 128), F32)
-    part = pltpu.VMEM((320, Q), F32)
     rows = pltpu.VMEM((ROWS, 128), F32)
-    v = call(analyze_kernel, shape(GY * 64, 128), f, toward, scratch=[cells])
-    v = inward(v)
+    full, full16 = pltpu.VMEM((CELLS, Q), F32), pltpu.VMEM((CELLS, Q), BF16)
+    native = pltpu.VMEM((XL, C, YL, Q), BF16)
+    grid, grid16 = pltpu.HBM((CELLS, Q), F32), pltpu.HBM((CELLS, Q), BF16)
+    v = pl.pallas_call(
+        analyze_kernel,
+        out_shape=shape(GY * CHUNK, 128),
+        in_specs=[hbm] * 2,
+        scratch_shapes=[cells, native, pltpu.VMEM((Q, N), BF16), pltpu.SemaphoreType.DMA((5,))],
+        compiler_params=pltpu.CompilerParams(vmem_limit_bytes=12 * 2**20),
+    )(*far(f, toward))
+    v, tables = lax.optimization_barrier((v, (*y_in, x_in[0], gather)))
+    v, w, (*inner, gather) = lax.optimization_barrier((over_y(v), w, fetch(*tables)))
+    v = pl.pallas_call(
+        first_inward_kernel,
+        out_shape=shape(GX * ROWS, 128),
+        in_specs=[vmem] * 4 + [hbm, vmem],
+        scratch_shapes=[pltpu.VMEM((XC, 2 * G * 128), BF16), pltpu.SemaphoreType.DMA(())],
+        compiler_params=pltpu.CompilerParams(vmem_limit_bytes=12 * 2**20),
+    )(v, *pin(*inner), *far(x_in[1]), twiddle)
     u, v = call(
-        mix_kernel, (shape(ROWS, 128), shape(GX, ROWS, 128)), v, w, gather,
+        mix_kernel, (shape(ROWS, 128), shape(GX, ROWS, 128)), over_x(v), w, *pin(gather),
         scratch=[pltpu.VMEM((128, CG * 128), F32), rows],
     )
-    v = spread_out(v)
-    output, pre, v = call(
+    v, f, d, table = lax.optimization_barrier((outward_part(v), f, d, outward))
+    lin, d = call(
+        linear_kernel, (grid, grid16), f, d, pointwise_weight.T, channel_bias.reshape(1, C), *wide, mib=18
+    )
+    v, lin, d, (table,) = lax.optimization_barrier((over_y(v), lin, d, fetch(table)))
+    output, pre, v = pl.pallas_call(
         forward_kernel,
-        (shape(XL, C, YL, Q, dtype=BF16), shape(CELLS, Q, dtype=BF16), shape(GY * 64, 128)),
-        v, f, d, mix_in, bias, outward, toward_back,
-        scratch=[cells, cells, part],
-    )
-    v = inward(v)
+        out_shape=(shape(XL, C, YL, Q, dtype=BF16), grid16, shape(GY * CHUNK, 128)),
+        in_specs=[vmem, hbm, hbm, vmem, hbm],
+        out_specs=(hbm, hbm, vmem),
+        scratch_shapes=[
+            cells, cells, full, full16, pltpu.VMEM((320, Q), F32), pltpu.VMEM((Q, N), BF16), native, full16,
+            pltpu.SemaphoreType.DMA((4, 4)), pltpu.SemaphoreType.DMA(()),
+        ],
+        compiler_params=pltpu.CompilerParams(vmem_limit_bytes=28 * 2**20),
+    )(v, *far(lin, d), *pin(table), *far(toward_back))
+    v = call(inward_kernel, shape(GX * ROWS, 128), over_y(v), *y_in, *x_in, twiddle)
+    v = over_x(v)
     s, v = call(
         unmix_kernel, (shape(128, CG * 128), shape(GX, ROWS, 128)), v, w, spread,
         scratch=[pltpu.VMEM((128, 128), F32), rows],
     )
+    v, s, pre, table = lax.optimization_barrier((outward_part(v), s, pre, outward_back))
+    lin = call(linear_back_kernel, grid, pre, pointwise_weight, *wide, mib=14)
     gw = call(outer_kernel, shape(C, G, 2, MODES, 128), u, s)
     gw = gw[..., :KC].reshape(C, G, 2, KYL, ML, CG, KX)
     grad_weight = jnp.transpose(gw, (2, 1, 5, 0, 6, 3, 4)).reshape(2, C, C, KX, KYL, ML)
-    v = spread_out(v)
-    grad_field = call(
-        backward_kernel, shape(XL, C, YL, Q, dtype=BF16), v, pre, mix_back, outward_back,
-        scratch=[cells, part],
-    )
+    v, lin, (table,) = lax.optimization_barrier((over_y(v), lin, fetch(table)))
+    grad_field = pl.pallas_call(
+        backward_kernel,
+        out_shape=shape(XL, C, YL, Q, dtype=BF16),
+        in_specs=[vmem, hbm, vmem],
+        out_specs=hbm,
+        scratch_shapes=[cells, pltpu.VMEM((320, Q), F32), full, native, pltpu.SemaphoreType.DMA((2, 4))],
+        compiler_params=pltpu.CompilerParams(vmem_limit_bytes=18 * 2**20),
+    )(v, *far(lin), *pin(table))
     return (jnp.transpose(output, (0, 2, 1, 3)), jnp.transpose(grad_field, (0, 2, 1, 3)), grad_weight)
 
 

time: 245 us -> 208 us (0.85)
  waiting for transfers between devices: 61.6 us -> 37.6 us
  Pallas kernels: 48.6 us -> 41.7 us
  local copies, waits for them, and re-layouts: 36.6 us -> 30.3 us
  blocking collectives: 70 us -> 74.5 us
  starting transfers between devices: 26 us -> 21.9 us
    pallas_call x10 -> x8, Pallas kernels: 48.6 us -> 16.3 us  [call(): pl.pallas_call(body, out_shape=outs, scratch_shapes=list(scratch), compil...]
    pallas_call x0 -> x7, Pallas kernels: none -> 25.4 us  [the longest x1 10.1 us: per_device(): pl.pallas_call(forward_kernel, out_shape=(shape(XL, C, YL, Q, dtype=BF16)...]
    all_to_all x4 -> x3, waiting for transfers between devices: 61.6 us -> 37.6 us  [over_y(): lax.all_to_all(v.reshape(GY, 1, CHUNK * 128), 'gy', split_axis=0, concat_...]
    all_to_all x3 -> x4, blocking collectives: 36.6 us -> 42.8 us  [over_x(): lax.all_to_all(v.reshape(GX, ROWS, 128), 'gx', split_axis=0, concat_axis=...]
    reshape x3 -> x0, local copies, waits for them, and re-layouts: 6.1 us -> none  [the longest x1 3.29 us: per_device(): jnp.einsum('hk,io,yw->hoykiw', eye, pointwise_weight, eye_y)]
    all_to_all x4 -> x3, starting transfers between devices: 26 us -> 21.9 us  [over_y(): lax.all_to_all(v.reshape(GY, 1, CHUNK * 128), 'gy', split_axis=0, concat_...]
  transfers between devices with their start and end apart: 4 -> 3, of which waited for: 3 -> 3; matrix products, arithmetic and copies ran while one was open for 14% -> 12% of each run, Pallas kernels for 1% -> 7%
where the time goes in v2:
time: 208 us; the launch traced here: 207 us
  blocking collectives  74.5 us (36%)
  Pallas kernels  41.7 us (20%)
  waiting for transfers between devices  37.6 us (18%)
  local copies, waits for them, and re-layouts  30.3 us (15%)
  starting transfers between devices  21.9 us (11%)
    all_to_all x4, blocking collectives, over_x(): lax.all_to_all(v.reshape(GX, ROWS, 128), 'gx', split_axis=0, concat_axis=...  42.8 us
    all_to_all x3, waiting for transfers between devices, over_y(): lax.all_to_all(v.reshape(GY, 1, CHUNK * 128), 'gy', split_axis=0, concat_...  37.6 us
    all_to_all x1, blocking collectives, over_y(): lax.all_to_all(v.reshape(GY, 1, CHUNK * 128), 'gy', split_axis=0, concat_...  31.7 us
    all_to_all x3, starting transfers between devices, over_y(): lax.all_to_all(v.reshape(GY, 1, CHUNK * 128), 'gy', split_axis=0, concat_...  21.9 us
    pallas_call x8, Pallas kernels, call(): pl.pallas_call(body, out_shape=outs, scratch_shapes=list(scratch), compil...  16.3 us
    pallas_call x1, Pallas kernels, per_device(): pl.pallas_call(forward_kernel, out_shape=(shape(XL, C, YL, Q, dtype=BF16)...  10.1 us
    transpose x1, local copies, waits for them, and re-layouts, per_device(): jnp.transpose(gw, (2, 1, 5, 0, 6, 3, 4)).reshape(2, C, C, KX, KYL, ML)  6.56 us
    reshape x1, local copies, waits for them, and re-layouts, per_device(): w = spectral_weight.reshape(2, G, CG, C, KX, KYL, ML)  5.73 us
  transfers between devices with their start and end apart: 3, of which 3 were waited for; matrix products, arithmetic and copies ran while one was open for 12% of the time, Pallas kernels for 7%

profile of v2, /device:TPU:32, one launch (start us, length us, event | category | flops | bytes accessed | tf_op | source)
XLA Modules:
  0.0 207.0 jit_solution(11984538181900796428)
XLA Ops:
  0.6 4.6 %shard_map.229 = f32[1920,128]{1,0:T(8,128)} custom-call(bf16[16,20,4,1024]{3,2,1,0:T(4,128)(2,1)} %bitcast.31, bf16[1024,192]{1,0:T(8,128)(2,1)} %constant.49.clone.table_ref), custom_call_target="tpu_custom_call" | custom-call | tf_op jit(solution)/shard_map/pallas_call | solution.py:530
  5.2 11.4 %all-to-all-start = ((f32[32,1,7680]{2,1,0:T(1,128)}), f32[32,1,7680]{2,1,0:T(1,128)S(1)}, u32[]{:S(2)}, u32[]{:S(2)}) async-start(f32[32,1,7680]{2,1,0:T(1,128)} %bitcast.1), calls=%async_computation | async-start | bytes 1966080 | tf_op jit(solution)/shard_map/all_to_all | solution.py:515
  16.6 5.7 %copy.47 = f32[2,4,5,20,24,3,3]{4,2,0,6,5,1,3:T(8,128)} copy(f32[2,4,5,20,24,3,3]{4,0,6,5,3,2,1:T(2,128)} %bitcast.48) | data formatting | bytes 1382400 | tf_op jit(solution)/shard_map/reshape | solution.py:508
  22.4 4.3 %reshape.60 = f32[20,4,2,9,120]{4,2,3,1,0:T(2,128)S(1)} reshape(f32[20,4,2,3,3,5,24]{6,5,2,4,3,1,0:T(8,128)} %bitcast.47) | data formatting | bytes 1382400 | tf_op jit(solution)/shard_map/reshape | solution.py:509
  26.6 1.2 copy.39
  27.9 1.5 pad.4.w_ref
  29.3 1.2 shard_map.230
  30.5 0.7 dynamic-slice_bitcast_fusion.tw_ref
  31.3 12.5 %all-to-all-done = f32[32,1,7680]{2,1,0:T(1,128)S(1)} async-done(((f32[32,1,7680]{2,1,0:T(1,128)}), f32[32,1,7680]{2,1,0:T(1,128)S(1)}, u32[]{:S(2)}, u32[]{:S(2)}) %all-to-all-start) | async-done | bytes 983072 | tf_op jit(solution)/shard_map/all_to_all | solution.py:515
  43.8 2.1 shard_map.231
  45.9 12.0 %all_to_all.40.q_ref = f32[8,72,128]{2,1,0:T(8,128)S(1)} all-to-all(f32[8,72,128]{2,1,0:T(8,128)S(1)} %bitcast.42), channel_id=1, replica_groups=mesh['gx'=8,'gy'=32] {'gx'}, dimensions={0} | all-to-all | bytes 589824 | tf_op jit(solution)/shard_map/all_to_all | solution.py:520
  57.9 0.5 shard_map.232
  58.3 0.0 copy-start.18
  58.4 10.3 %all_to_all.41 = f32[8,72,128]{2,1,0:T(8,128)S(1)} all-to-all(f32[8,72,128]{2,1,0:T(8,128)S(1)} %get-tuple-element.57), channel_id=1, replica_groups=mesh['gx'=8,'gy'=32] {'gx'}, dimensions={0} | all-to-all | bytes 589824 | tf_op jit(solution)/shard_map/all_to_all | solution.py:520
  68.6 0.0 copy-done.1
  68.6 2.1 %shard_map.233 = f32[1920,128]{1,0:T(8,128)} custom-call(f32[576,128]{1,0:T(8,128)S(1)} %bitcast.40, bf16[512,768]{1,0:T(8,128)(2,1)S(1)} %copy-done.3, bf16[512,768]{1,0:T(8,128)(2,1)S(1)} %copy-done.1, bf16[256,144]{1,0:T(8,128)(2,1)S(1)} %copy-done.9, f32[8,512]{1,0:T(8,128)S(1)} %dynamic-slice_bitcast_fusion.tw_ref), custom_call_target="tpu_custom_call" | custom-call | tf_op jit(solution)/shard_map/pallas_call | solution.py:130
  70.7 5.3 %all-to-all-start.3 = ((f32[32,1,7680]{2,1,0:T(1,128)}), f32[32,1,7680]{2,1,0:T(1,128)S(1)}, u32[]{:S(2)}, u32[]{:S(2)}) async-start(f32[32,1,7680]{2,1,0:T(1,128)} %bitcast.9), calls=%async_computation.3 | async-start | bytes 1966080 | tf_op jit(solution)/shard_map/all_to_all | solution.py:515
  76.0 0.1 copy.41
  76.1 1.3 shard_map.235.s_ref
  77.5 0.0 copy-start
  77.5 1.7 copy-done
  79.2 1.7 copy-done.5
  80.9 0.9 copy-done.11
  81.8 5.5 %shard_map.234 = (f32[1280,1024]{1,0:T(8,128)}, bf16[1280,1024]{1,0:T(8,128)(2,1)}) custom-call(bf16[16,20,4,1024]{3,2,1,0:T(4,128)(2,1)S(1)} %bitcast.32, bf16[16,20,4,1024]{3,2,1,0:T(4,128)(2,1)S(1)} %bitcast.38, bf16[20,20]{1,0:T(8,128)(2,1)S(1)} %bitcast.44, f32[1,20]{1,0:T(1,128)S(1)} %bitcast.45, bf16[160,20]{1,0:T(8,128)(2,1)S(1)} %copy-done.14, ...), custom_call_target="tpu_custom_call" | custom-call | tf_op jit(solution)/shard_map/pallas_call | solution.py:130
  87.3 16.0 %all-to-all-done.3 = f32[32,1,7680]{2,1,0:T(1,128)S(1)} async-done(((f32[32,1,7680]{2,1,0:T(1,128)}), f32[32,1,7680]{2,1,0:T(1,128)S(1)}, u32[]{:S(2)}, u32[]{:S(2)}) %all-to-all-start.3) | async-done | bytes 983072 | tf_op jit(solution)/shard_map/all_to_all | solution.py:515
  103.3 10.1 %shard_map.236 = (bf16[16,20,4,1024]{3,2,1,0:T(4,128)(2,1)}, bf16[1280,1024]{1,0:T(8,128)(2,1)}, f32[1920,128]{1,0:T(8,128)S(1)}) custom-call(f32[1920,128]{1,0:T(8,128)S(1)} %bitcast.35, f32[1280,1024]{1,0:T(8,128)} %get-tuple-element.65.lin_hbm, bf16[1280,1024]{1,0:T(8,128)(2,1)} %get-tuple-element.66.d_hbm, bf16[576,1024]{1,0:T(8,128)(2,1)S(1)} %shard_map.235.s_ref, ...), custom_call_target="tpu_custom_call" | custom-call | tf_op jit(solution)/shard_map/pallas_call | solution.py:555
  113.4 0.0 copy-start.13
  113.4 31.7 %all_to_all.42 = f32[32,1,7680]{2,1,0:T(1,128)S(1)} all-to-all(f32[32,1,7680]{2,1,0:T(1,128)S(1)} %bitcast.43), channel_id=1, replica_groups=mesh['gx'=8,'gy'=32] {'gy'}, dimensions={0} | all-to-all | bytes 1966080 | tf_op jit(solution)/shard_map/all_to_all | solution.py:515
  145.2 0.0 copy-done.8
  145.2 0.0 copy-start.2
  145.2 0.0 copy-start.4
  145.2 0.0 copy-start.10
  145.2 1.0 shard_map.237
  146.2 10.3 %all_to_all.43.q_ref = f32[8,72,128]{2,1,0:T(8,128)S(1)} all-to-all(f32[8,72,128]{2,1,0:T(8,128)S(1)} %bitcast.41), channel_id=1, replica_groups=mesh['gx'=8,'gy'=32] {'gx'}, dimensions={0} | all-to-all | bytes 589824 | tf_op jit(solution)/shard_map/all_to_all | solution.py:520
  156.5 0.5 shard_map.238
  157.0 10.3 %all_to_all.44 = f32[8,72,128]{2,1,0:T(8,128)S(1)} all-to-all(f32[8,72,128]{2,1,0:T(8,128)S(1)} %get-tuple-element.70), channel_id=1, replica_groups=mesh['gx'=8,'gy'=32] {'gx'}, dimensions={0} | all-to-all | bytes 589824 | tf_op jit(solution)/shard_map/all_to_all | solution.py:520
  167.3 2.1 %shard_map.239 = f32[1920,128]{1,0:T(8,128)} custom-call(f32[576,128]{1,0:T(8,128)S(1)} %bitcast.39, bf16[512,768]{1,0:T(8,128)(2,1)S(1)} %copy-done.4, bf16[512,768]{1,0:T(8,128)(2,1)S(1)} %copy-done.2, bf16[256,144]{1,0:T(8,128)(2,1)S(1)} %copy-done.10, f32[8,512]{1,0:T(8,128)S(1)} %dynamic-slice_bitcast_fusion.tw_ref), custom_call_target="tpu_custom_call" | custom-call | tf_op jit(solution)/shard_map/pallas_call | solution.py:130
  169.4 5.3 %all-to-all-start.7 = ((f32[32,1,7680]{2,1,0:T(1,128)}), f32[32,1,7680]{2,1,0:T(1,128)S(1)}, u32[]{:S(2)}, u32[]{:S(2)}) async-start(f32[32,1,7680]{2,1,0:T(1,128)} %bitcast.18), calls=%async_computation.7 | async-start | bytes 1966080 | tf_op jit(solution)/shard_map/all_to_all | solution.py:515
  174.6 1.3 shard_map.241.s_ref
  175.9 0.0 copy-done.19
  175.9 0.1 shard_map.243
  176.1 1.2 copy.44
  177.3 4.5 %reshape.72 = f32[20,4,2,3,3,5,24]{6,5,2,4,3,1,0:T(8,128)} reshape(f32[20,4,2,9,120]{4,2,3,1,0:T(2,128)} %copy.44) | data formatting | bytes 1382400 | tf_op jit(solution)/shard_map/reshape | solution.py:575
  181.8 6.6 %copy.45 = f32[2,4,5,20,24,3,3]{4,0,6,5,3,2,1:T(2,128)} copy(f32[2,4,5,20,24,3,3]{4,2,0,6,5,1,3:T(8,128)} %bitcast.46) | data formatting | bytes 1382400 | tf_op jit(solution)/shard_map/transpose | solution.py:576
  188.4 0.0 copy-done.7
  188.4 4.5 %shard_map.240.lin_hbm = f32[1280,1024]{1,0:T(8,128)} custom-call(bf16[1280,1024]{1,0:T(8,128)(2,1)S(1)} %copy-done.7, bf16[20,20]{1,0:T(8,128)(2,1)S(1)} %copy-done.21, bf16[160,20]{1,0:T(8,128)(2,1)S(1)} %copy-done.14, bf16[20,160]{1,0:T(8,128)(2,1)S(1)} %copy-done.17, bf16[160,160]{1,0:T(8,128)(2,1)S(1)} %copy-done.12), custom_call_target="tpu_custom_call" | custom-call | tf_op jit(solution)/shard_map/pallas_call | solution.py:130
  192.9 9.0 %all-to-all-done.7 = f32[32,1,7680]{2,1,0:T(1,128)S(1)} async-done(((f32[32,1,7680]{2,1,0:T(1,128)}), f32[32,1,7680]{2,1,0:T(1,128)S(1)}, u32[]{:S(2)}, u32[]{:S(2)}) %all-to-all-start.7) | async-done | bytes 983072 | tf_op jit(solution)/shard_map/all_to_all | solution.py:515
  201.9 4.9 %shard_map.242 = bf16[16,20,4,1024]{3,2,1,0:T(4,128)(2,1)} custom-call(f32[1920,128]{1,0:T(8,128)S(1)} %bitcast.34, f32[1280,1024]{1,0:T(8,128)} %shard_map.240.lin_hbm, bf16[576,1024]{1,0:T(8,128)(2,1)S(1)} %shard_map.241.s_ref), custom_call_target="tpu_custom_call" | custom-call | tf_op jit(solution)/shard_map/pallas_call | solution.py:578
  (33 shorter events, 0.1 us)
Async XLA Ops:
  5.2 38.6 %all-to-all-start = ((f32[32,1,7680]{2,1,0:T(1,128)}), f32[32,1,7680]{2,1,0:T(1,128)S(1)}, u32[]{:S(2)}, u32[]{:S(2)}) async-start(f32[32,1,7680]{2,1,0:T(1,128)} %bitcast.1), calls=%async_computation | async-start | bytes 1966080 | tf_op jit(solution)/shard_map/all_to_all | solution.py:515
  43.8 24.8 %copy-start.1 = (bf16[512,768]{1,0:T(8,128)(2,1)S(1)}, bf16[512,768]{1,0:T(8,128)(2,1)}, u32[]{:S(2)}) copy-start(bf16[512,768]{1,0:T(8,128)(2,1)} %constant.59.clone.xl_ref) | copy-start | bytes 2359300
  43.8 24.8 %copy-start.3 = (bf16[512,768]{1,0:T(8,128)(2,1)S(1)}, bf16[512,768]{1,0:T(8,128)(2,1)}, u32[]{:S(2)}) copy-start(bf16[512,768]{1,0:T(8,128)(2,1)} %constant.58.clone.xh_ref) | copy-start | bytes 2359300
  43.8 24.8 %copy-start.9 = (bf16[256,144]{1,0:T(8,128)(2,1)S(1)}, bf16[256,144]{1,0:T(8,128)(2,1)}, u32[]{:S(2)}) copy-start(bf16[256,144]{1,0:T(8,128)(2,1)} %constant.55.clone.y_ref) | copy-start | bytes 221188
  58.3 12.4 %copy-start.18 = (f32[72,128]{1,0:T(8,128)}, f32[72,128]{1,0:T(8,128)S(1)}, u32[]{:S(2)}) copy-start(f32[72,128]{1,0:T(8,128)S(1)} %get-tuple-element.79.u_ref) | copy-start | bytes 110596
  68.6 7.4 %copy-start.20 = (bf16[20,20]{1,0:T(8,128)(2,1)S(1)}, bf16[20,20]{1,0:T(8,128)(2,1)}, u32[]{:S(2)}) copy-start(bf16[20,20]{1,0:T(8,128)(2,1)} %w_ref.1) | copy-start | bytes 2404
  70.7 6.7 %copy-start.14 = (bf16[160,20]{1,0:T(8,128)(2,1)S(1)}, bf16[160,20]{1,0:T(8,128)(2,1)}, u32[]{:S(2)}) copy-start(bf16[160,20]{1,0:T(8,128)(2,1)} %constant.63.clone.e_ref) | copy-start | bytes 19204
  70.7 6.7 %copy-start.17 = (bf16[20,160]{1,0:T(8,128)(2,1)S(1)}, bf16[20,160]{1,0:T(8,128)(2,1)}, u32[]{:S(2)}) copy-start(bf16[20,160]{1,0:T(8,128)(2,1)} %constant.64.clone.et_ref) | copy-start | bytes 19204
  70.7 6.7 %copy-start.22 = (f32[20]{0:T(128)S(1)}, f32[20]{0:T(128)}, u32[]{:S(2)}) copy-start(f32[20]{0:T(128)} %param.26) | copy-start | bytes 244
  70.7 32.6 %all-to-all-start.3 = ((f32[32,1,7680]{2,1,0:T(1,128)}), f32[32,1,7680]{2,1,0:T(1,128)S(1)}, u32[]{:S(2)}, u32[]{:S(2)}) async-start(f32[32,1,7680]{2,1,0:T(1,128)} %bitcast.9), calls=%async_computation.3 | async-start | bytes 1966080 | tf_op jit(solution)/shard_map/all_to_all | solution.py:515
  77.5 1.7 copy-start
  79.2 1.7 copy-start.5
  80.9 0.9 copy-start.11
  103.3 41.9 %copy-start.6 = (bf16[320,1024]{1,0:T(8,128)(2,1)S(1)}, bf16[320,1024]{1,0:T(8,128)(2,1)}, u32[]{:S(2)}) copy-start(bf16[320,1024]{1,0:T(8,128)(2,1)} %constant.56.clone.refs_2_.xh_ref) | copy-start | bytes 1966084
  103.3 41.9 %copy-start.8 = (bf16[320,1024]{1,0:T(8,128)(2,1)S(1)}, bf16[320,1024]{1,0:T(8,128)(2,1)}, u32[]{:S(2)}) copy-start(bf16[320,1024]{1,0:T(8,128)(2,1)} %constant.57.clone.xl_hbm.xl_ref) | copy-start | bytes 1966084
  103.3 41.9 %copy-start.15 = (bf16[48,256]{1,0:T(8,128)(2,1)S(1)}, bf16[48,256]{1,0:T(8,128)(2,1)}, u32[]{:S(2)}) copy-start(bf16[48,256]{1,0:T(8,128)(2,1)} %constant.54.clone.refs_1_.yl_ref) | copy-start | bytes 73732
  103.3 41.9 %copy-start.16 = (bf16[48,256]{1,0:T(8,128)(2,1)S(1)}, bf16[48,256]{1,0:T(8,128)(2,1)}, u32[]{:S(2)}) copy-start(bf16[48,256]{1,0:T(8,128)(2,1)} %constant.53.clone.refs_0_.yh_ref) | copy-start | bytes 73732
  113.4 43.0 %copy-start.13 = (bf16[128,640]{1,0:T(8,128)(2,1)S(1)}, bf16[128,640]{1,0:T(8,128)(2,1)}, u32[]{:S(2)}) copy-start(bf16[128,640]{1,0:T(8,128)(2,1)} %constant.61.clone.e_ref) | copy-start | bytes 491524
  145.2 22.1 %copy-start.2 = (bf16[512,768]{1,0:T(8,128)(2,1)S(1)}, bf16[512,768]{1,0:T(8,128)(2,1)}, u32[]{:S(2)}) copy-start(bf16[512,768]{1,0:T(8,128)(2,1)} %constant.59.clone.xl_ref) | copy-start | bytes 2359300
  145.2 22.0 %copy-start.4 = (bf16[512,768]{1,0:T(8,128)(2,1)S(1)}, bf16[512,768]{1,0:T(8,128)(2,1)}, u32[]{:S(2)}) copy-start(bf16[512,768]{1,0:T(8,128)(2,1)} %constant.58.clone.xh_ref) | copy-start | bytes 2359300
  145.2 22.0 %copy-start.10 = (bf16[256,144]{1,0:T(8,128)(2,1)S(1)}, bf16[256,144]{1,0:T(8,128)(2,1)}, u32[]{:S(2)}) copy-start(bf16[256,144]{1,0:T(8,128)(2,1)} %constant.55.clone.y_ref) | copy-start | bytes 221188
  169.4 6.6 %copy-start.19 = (f32[72,128]{1,0:T(8,128)S(1)}, f32[72,128]{1,0:T(8,128)}, u32[]{:S(2)}) copy-start(f32[72,128]{1,0:T(8,128)} %copy-done.18) | copy-start | bytes 110596
  169.4 32.5 %all-to-all-start.7 = ((f32[32,1,7680]{2,1,0:T(1,128)}), f32[32,1,7680]{2,1,0:T(1,128)S(1)}, u32[]{:S(2)}, u32[]{:S(2)}) async-start(f32[32,1,7680]{2,1,0:T(1,128)} %bitcast.18), calls=%async_computation.7 | async-start | bytes 1966080 | tf_op jit(solution)/shard_map/all_to_all | solution.py:515
  181.8 6.6 %copy-start.7 = (bf16[1280,1024]{1,0:T(8,128)(2,1)S(1)}, bf16[1280,1024]{1,0:T(8,128)(2,1)}, u32[]{:S(2)}) copy-start(bf16[1280,1024]{1,0:T(8,128)(2,1)} %get-tuple-element.74.p_ref) | copy-start | bytes 7864324
  181.8 6.6 %copy-start.12 = (bf16[160,160]{1,0:T(8,128)(2,1)S(1)}, bf16[160,160]{1,0:T(8,128)(2,1)}, u32[]{:S(2)}) copy-start(bf16[160,160]{1,0:T(8,128)(2,1)} %constant.65.clone.mask_ref) | copy-start | bytes 153604
  181.8 6.6 %copy-start.21 = (bf16[20,20]{1,0:T(8,128)(2,1)S(1)}, bf16[20,20]{1,0:T(8,128)(2,1)}, u32[]{:S(2)}) copy-start(bf16[20,20]{1,0:T(8,128)(2,1)} %w_ref.1) | copy-start | bytes 2404

commit v3 on v2

v3 whole, which is shorter than its diff:
```python
import math

import jax
import jax.numpy as jnp
import numpy as np
from jax import lax
from jax.experimental import pallas as pl
from jax.experimental.pallas import tpu as pltpu
from jax.sharding import PartitionSpec as P

NX = 128
NY = 128
NZ = 64
NT = 16
C = 20
KX = 24
KY = 24
KZ = 12
KT = 8

GX = 8
GY = 32
XL = NX // GX
YL = NY // GY
KYL = KY // GX
ML = KZ * KT // GY
XC = XL * C
CELLS = XL * C * YL
Q = NZ * NT
N = 2 * ML * GY
HALF = C // 2
HC = XL * HALF
KEEP = HC * YL
SWAP = KEEP * 3 // 2
LT = 6
CHUNK = LT * 8
G = 4
CG = C // G
KC = CG * KX
MODES = KYL * ML
ROWS = G * 2 * MODES
XROWS = ROWS // 2

GELU_SCALE = math.sqrt(2.0 / math.pi)
GELU_CUBIC = 0.044715
F32 = jnp.float32
BF16 = jnp.bfloat16
SCALE = 1.0 / (NX * NY)


def signed(count):
    j = np.arange(count)
    return np.where(j < count // 2, j, j - count)


def halves(table):
    table = np.asarray(table, np.float32)
    high = table.astype(jnp.bfloat16)
    low = (table - high.astype(np.float32)).astype(jnp.bfloat16)
    return high, low


def zt_tables():
    q = np.arange(Q)
    m = (np.arange(GY)[None, :] * ML + np.arange(ML)[:, None]).reshape(-1)
    fz, kt = signed(KZ)[m // KT], m % KT
    phase = (fz[None, :] * (q // NT)[:, None] * NT + kt[None, :] * (q % NT)[:, None] * NZ) % Q
    angles = phase * (2.0 * math.pi / Q)
    weights = np.where(kt == 0, 1.0, 2.0) / Q
    analysis = np.concatenate([np.cos(angles), -np.sin(angles)], axis=1)
    synthesis = analysis * np.concatenate([weights, weights])[None, :]
    return analysis.astype(np.float32), synthesis.astype(np.float32)


def three_rows(table):
    high, low = halves(table)
    return np.concatenate([high, high, low], axis=0)


def y_table():
    ky = (np.arange(GX)[None, :] * KYL + np.arange(KYL)[:, None]).reshape(-1)
    f = signed(KY)[ky]
    n = np.arange(NY)
    angles = ((f[:, None] * n[None, :]) % NY) * (2.0 * math.pi / NY)
    c, s = np.cos(angles), np.sin(angles)
    t = np.zeros((2, KY, GY, 2, YL))
    c4, s4 = c.reshape(KY, GY, YL), s.reshape(KY, GY, YL)
    t[0, :, :, 0], t[0, :, :, 1] = c4, s4
    t[1, :, :, 0], t[1, :, :, 1] = -s4, c4
    return np.transpose(t, (0, 1, 3, 4, 2)).reshape(2 * KY, 2 * YL * GY)


def x_tables():
    f = signed(KX)
    t = np.zeros((GX, 2, XL, HALF, 2, 2, 128))
    for a in range(GX):
        for side in range(2):
            cells = XL * (a ^ side) + np.arange(XL)
            angles = ((f[None, :] * cells[:, None]) % NX) * (2.0 * math.pi / NX)
            for c in range(HALF):
                g, j = divmod(c, CG)
                t[a, side, :, c, 0, g, j * KX : (j + 1) * KX] = np.cos(angles)
                t[a, side, :, c, 1, g, j * KX : (j + 1) * KX] = np.sin(angles)
    turned = np.zeros((GX, 256, 2, 384))
    turned[..., :XC] = np.transpose(t, (0, 5, 6, 4, 1, 2, 3)).reshape(GX, 256, 2, XC)
    return t.reshape(GX, XC, 512), turned.reshape(GX, 256, 768)


def group_tables():
    gather = np.zeros((CG, 128, 128), np.float32)
    spread = np.zeros((128, CG, 128), np.float32)
    eye = np.eye(KX, dtype=np.float32)
    for o in range(CG):
        for i in range(CG):
            gather[o, i * KX : (i + 1) * KX, o * KX : (o + 1) * KX] = eye
            spread[o * KX : (o + 1) * KX, o, i * KX : (i + 1) * KX] = eye
    return gather.reshape(CG * 128, 128), spread.reshape(128, CG * 128)


def mm(a, b):
    return jnp.dot(a, b, preferred_element_type=F32)


def split(v):
    high = v.astype(BF16)
    return high, (v - high.astype(F32)).astype(BF16)


def call(body, outs, *args, scratch=(), mib=12):
    return pl.pallas_call(
        body,
        out_shape=outs,
        scratch_shapes=list(scratch),
        compiler_params=pltpu.CompilerParams(vmem_limit_bytes=mib * 2**20),
    )(*args)


def shape(*dims, dtype=F32):
    return jax.ShapeDtypeStruct(dims, dtype)


def far(*values):
    return [pltpu.with_memory_space_constraint(v, pltpu.HBM) for v in values]


def halves_of_rows(core, x):
    own = pl.ds(pl.multiple_of(x * 80 + core * 40, 8), 40)
    other = pl.ds(pl.multiple_of(x * 80 + (1 - core) * 40, 8), 40)
    return own, other


def part_with(core, c_ref, keep_ref, send_ref):
    late = []
    for x in range(XL):
        own, other = halves_of_rows(core, x)
        keep_ref[0, x * 40 : x * 40 + 40, :] = c_ref[0, own, :]
        keep_ref[1, x * 40 : x * 40 + 40, :] = c_ref[1, own, :]
        send_ref[x * 40 : x * 40 + 40, :] = c_ref[0, other, :]
        late.append(c_ref[1, other, :][:, :64])
    for x in range(XL // 2):
        send_ref[KEEP + x * 40 : KEEP + x * 40 + 40, :] = jnp.concatenate([late[x], late[x + XL // 2]], axis=1)


def join(core, keep_ref, recv_ref, g_ref):
    for x in range(XL):
        own, other = halves_of_rows(core, x)
        g_ref[0, own, :] = keep_ref[0, x * 40 : x * 40 + 40, :]
        g_ref[1, own, :] = keep_ref[1, x * 40 : x * 40 + 40, :]
        g_ref[0, other, :] = recv_ref[x * 40 : x * 40 + 40, :]
    for x in range(XL // 2):
        both = recv_ref[KEEP + x * 40 : KEEP + x * 40 + 40, :]
        for h in range(2):
            g_ref[1, halves_of_rows(core, x + h * XL // 2)[1], :64] = both[:, h * 64 : h * 64 + 64]


def load_tables(me_ref, high_hbm, low_hbm, high_ref, low_ref, sems):
    me = me_ref[0]
    copies = [
        pltpu.make_async_copy(high_hbm.at[me], high_ref, sems.at[0]),
        pltpu.make_async_copy(low_hbm.at[me], low_ref, sems.at[1]),
    ]
    for copy in copies:
        copy.start()
    return copies


def contract_kernel(me_ref, keep_ref, recv_ref, high_hbm, low_hbm, o_ref, high_ref, low_ref, sems):
    copies = load_tables(me_ref, high_hbm, low_hbm, high_ref, low_ref, sems)
    rows = []
    for y in range(YL):
        both = recv_ref[pl.ds(KEEP + y, HC // 2, stride=YL), :]
        first = jnp.concatenate(
            [keep_ref[0, pl.ds(y, HC, stride=YL), :], recv_ref[pl.ds(y, HC, stride=YL), :]], axis=0
        )
        second = jnp.concatenate(
            [keep_ref[1, pl.ds(y, HC, stride=YL), :][:, :64], both[:, :64], both[:, 64:]], axis=0
        )
        rows += [first.T, second.T]
    vh, vl = split(jnp.concatenate(rows, axis=0))
    for copy in copies:
        copy.wait()
    p = mm(vh, high_ref[...]) + (mm(vl, high_ref[...]) + mm(vh, low_ref[...]))
    for y in range(YL):
        for m in range(ML):
            at = y * N + m * GY
            re, im = p[at : at + GY], p[at + N // 2 : at + N // 2 + GY]
            parts = (re[:, :256] + im[:, 256:], im[:, :256] - re[:, 256:])
            for part in range(2):
                for g in range(2):
                    o_ref[pl.ds((m * 2 + g) * 8 + part * YL + y, GY, stride=CHUNK), :] = parts[part][
                        :, g * 128 : (g + 1) * 128
                    ]


def expand_kernel(me_ref, r_ref, high_hbm, low_hbm, keep_ref, send_ref, high_ref, low_ref, sems):
    copies = load_tables(me_ref, high_hbm, low_hbm, high_ref, low_ref, sems)
    rows = []
    for y in range(YL):
        for part in range(2):
            for m in range(ML):
                rows.append(
                    jnp.concatenate(
                        [
                            r_ref[pl.ds((m * 2 + g) * 8 + part * YL + y, GY, stride=CHUNK), :]
                            for g in range(2)
                        ],
                        axis=1,
                    )
                )
    vh, vl = split(jnp.concatenate(rows, axis=0))
    for copy in copies:
        copy.wait()
    p = mm(vh, high_ref[...]) + (mm(vl, high_ref[...]) + mm(vh, low_ref[...]))
    for y in range(YL):
        re, im = p[y * N : y * N + N // 2], p[y * N + N // 2 : y * N + N]
        real = re[:, :XC] - im[:, 384 : 384 + XC]
        imag = re[:, 384 : 384 + XC] + im[:, :XC]
        first = jnp.concatenate([real, imag[:GY]], axis=0).T
        second = imag[GY:].T
        keep_ref[0, pl.ds(y, HC, stride=YL), :] = first[:HC]
        keep_ref[1, pl.ds(y, HC, stride=YL), :] = jnp.concatenate(
            [second[:HC], jnp.zeros((HC, 64), F32)], axis=1
        )
        send_ref[pl.ds(y, HC, stride=YL), :] = first[HC:]
        send_ref[pl.ds(KEEP + y, HC // 2, stride=YL), :] = jnp.concatenate(
            [second[HC : HC + HC // 2], second[HC + HC // 2 :]], axis=1
        )


def analyze_kernel(me_ref, f_ref, table_ref, keep_ref, send_ref, c_ref, v_ref, t_ref, sems):
    table = pltpu.make_async_copy(table_ref, t_ref, sems.at[4])
    table.start()
    copies = [pltpu.make_async_copy(f_ref.at[pl.ds(i * 4, 4)], v_ref.at[pl.ds(i * 4, 4)], sems.at[i]) for i in range(4)]
    for copy in copies:
        copy.start()
    table.wait()
    for i in range(4):
        copies[i].wait()
        v = jnp.concatenate([v_ref[i * 4 + k].reshape(C * YL, Q) for k in range(4)], axis=0)
        r = mm(v, t_ref[...])
        c_ref[0, i * 320 : (i + 1) * 320, :] = r[:, :128]
        c_ref[1, i * 320 : (i + 1) * 320, :64] = r[:, 128:]
    part_with(me_ref[0] % 2, c_ref, keep_ref, send_ref)


def widen(table, e_ref, et_ref, mask_ref):
    tall = mm(e_ref[...], table).astype(BF16)
    return mm(tall, et_ref[...]).astype(BF16) * mask_ref[...]


def linear_kernel(f_ref, d_ref, w_ref, b_ref, e_ref, et_ref, mask_ref, lin_ref, row_ref):
    mix = widen(w_ref[...], e_ref, et_ref, mask_ref)
    bias = jnp.sum(e_ref[...].astype(F32) * b_ref[...], axis=1, keepdims=True)

    def body(i, _):
        x = 2 * i
        rows = pl.ds(pl.multiple_of(i * 160, 16), 160)
        fv = jnp.concatenate([f_ref[x + h].reshape(C * YL, Q) for h in range(2)], axis=0)
        lin_ref[rows, :] = mm(mix, fv) + bias
        row_ref[rows, :] = jnp.concatenate([d_ref[x + h].reshape(C * YL, Q) for h in range(2)], axis=0)
        return 0

    lax.fori_loop(0, XL // 2, body, 0)


def linear_back_kernel(p_ref, w_ref, e_ref, et_ref, mask_ref, lin_ref):
    mix = widen(w_ref[...], e_ref, et_ref, mask_ref)

    def body(i, _):
        rows = pl.ds(pl.multiple_of(i * 160, 16), 160)
        lin_ref[rows, :] = mm(mix, p_ref[rows, :])
        return 0

    lax.fori_loop(0, XL // 2, body, 0)


def synthesis_rows(g_ref, rows):
    gh0, gl0 = split(g_ref[0, rows, :])
    gh1, gl1 = split(g_ref[1, rows, :])
    gh1, gl1 = gh1[:, :64], gl1[:, :64]
    return jnp.concatenate([gh0, gh1, gl0, gl1, gh0, gh1], axis=1)


def pieces(source, target, sems):
    return [
        pltpu.make_async_copy(source.at[pl.ds(i * n, n)], target.at[pl.ds(i * n, n)], sems.at[i])
        for n in [source.shape[0] // 4]
        for i in range(4)
    ]


def forward_kernel(
    me_ref, keep_ref, recv_ref, lin_ref, d_hbm, s_ref, t_ref, out_hbm, pre_hbm, keep_out, send_ref,
    g_ref, c_ref, d_ref, sp_ref, out_ref, pre_ref, sems,
):
    d_in = pieces(d_hbm, d_ref, sems.at[2])
    for copy in d_in:
        copy.start()
    out_out, pre_out = pieces(out_ref, out_hbm, sems.at[0]), pieces(pre_ref, pre_hbm, sems.at[1])
    core = me_ref[0] % 2
    join(core, keep_ref, recv_ref, g_ref)
    for i in range(4):
        rows = slice(i * 320, (i + 1) * 320)
        sp_ref[...] = mm(synthesis_rows(g_ref, rows), s_ref[...])
        d_in[i].wait()

        def body(k, _, i=i):
            at = pl.ds(pl.multiple_of(i * 320 + k * 80, 16), 80)
            before = sp_ref[pl.ds(pl.multiple_of(k * 80, 16), 80), :] + lin_ref[at, :]
            square = before * before
            tangent = jnp.tanh(before * (GELU_SCALE + (GELU_SCALE * GELU_CUBIC) * square))
            half = 0.5 + 0.5 * tangent
            result = before * half
            slope = half + result * (1.0 - tangent) * (GELU_SCALE + (3.0 * GELU_SCALE * GELU_CUBIC) * square)
            pre_ref[at, :] = (d_ref[at, :].astype(F32) * slope).astype(BF16)
            out_ref[i * 4 + k] = result.astype(BF16).reshape(C, YL, Q)
            return 0

        lax.fori_loop(0, 4, body, 0)
        out_out[i].start()
        pre_out[i].start()
        r = mm(pre_ref[rows, :], t_ref[...])
        c_ref[0, rows, :] = r[:, :128]
        c_ref[1, rows, :64] = r[:, 128:]
    part_with(core, c_ref, keep_out, send_ref)
    for i in range(4):
        out_out[i].wait()
        pre_out[i].wait()


def backward_kernel(me_ref, keep_ref, recv_ref, lin_ref, s_ref, out_hbm, g_ref, sp_ref, out_ref, sems):
    out_out = pieces(out_ref, out_hbm, sems)
    join(me_ref[0] % 2, keep_ref, recv_ref, g_ref)
    for i in range(4):
        rows = slice(i * 320, (i + 1) * 320)
        sp_ref[...] = mm(synthesis_rows(g_ref, rows), s_ref[...])
        for k in range(4):
            total = sp_ref[k * 80 : (k + 1) * 80, :] + lin_ref[i * 320 + k * 80 : i * 320 + (k + 1) * 80, :]
            out_ref[i * 4 + k] = total.astype(BF16).reshape(C, YL, Q)
        out_out[i].start()
    for i in range(4):
        out_out[i].wait()


def inward_kernel(r_ref, yh_ref, yl_ref, o_ref):
    columns = []
    for lt in range(LT):
        columns.append(
            jnp.concatenate([r_ref[pl.ds(lt * 8 + k, GY, stride=CHUNK), :] for k in range(8)], axis=0)
        )
    vh, vl = split(jnp.concatenate(columns, axis=1))
    p = mm(yh_ref[...], vh) + (mm(yh_ref[...], vl) + mm(yl_ref[...], vh))
    for lt in range(LT):
        m, g = divmod(lt, 2)
        for part in range(2):
            for ky in range(KYL):
                o_ref[pl.ds(g * 18 + part * 9 + ky * ML + m, GX, stride=XROWS), :] = p[
                    part * 24 + ky * 8 : part * 24 + ky * 8 + 8, lt * 128 : (lt + 1) * 128
                ]


def outward_kernel(z_ref, y_ref, o_ref):
    columns = []
    for lt in range(LT):
        m, g = divmod(lt, 2)
        columns.append(
            jnp.concatenate(
                [
                    z_ref[pl.ds(g * 18 + part * 9 + ky * ML + m, GX, stride=XROWS), :]
                    for part in range(2)
                    for ky in range(KYL)
                ],
                axis=0,
            )
        )
    vh, vl = split(jnp.concatenate(columns, axis=1))
    o = mm(y_ref[...], jnp.concatenate([vh, vl, vh], axis=0))
    for lt in range(LT):
        for k in range(8):
            o_ref[pl.ds(lt * 8 + k, GY, stride=CHUNK), :] = o[k * GY : (k + 1) * GY, lt * 128 : (lt + 1) * 128]


def part_rows(ref, g, part):
    return ref[g * 18 + part * 9 : g * 18 + part * 9 + 9, :]


def send_all(o_ref, r_ref):
    for a in range(GX):
        core = a % 2
        o_ref[a * XROWS : (a + 1) * XROWS, :] = r_ref[core * XROWS : (core + 1) * XROWS, :]


def sum_chips(q_ref, core):
    return sum(q_ref[a * XROWS : (a + 1) * XROWS, :] for a in range(core, GX, 2))


def mix_kernel(q_ref, w_ref, e_ref, u_ref, o_ref, l_ref, r_ref):
    for core in range(2):
        u_ref[core * XROWS : (core + 1) * XROWS, :] = sum_chips(q_ref, core)
    us = [[part_rows(u_ref, g, part) for part in range(2)] for g in range(G)]
    l_ref[...] = jnp.zeros_like(l_ref)
    for o in range(C):
        real = imag = None
        for g in range(G):
            wr, wi = w_ref[o, g, 0], w_ref[o, g, 1]
            ur, ui = us[g]
            a, b = wr * ur - wi * ui, wr * ui + wi * ur
            real, imag = (a, b) if real is None else (real + a, imag + b)
        gi, oi = divmod(o, CG)
        l_ref[gi * 32 : gi * 32 + 9, oi * 128 : (oi + 1) * 128] = real
        l_ref[gi * 32 + 16 : gi * 32 + 25, oi * 128 : (oi + 1) * 128] = imag
    vh, vl = split(l_ref[...])
    v = (mm(vh, e_ref[...]) + mm(vl, e_ref[...])) * SCALE
    for g in range(G):
        for part in range(2):
            r_ref[g * 18 + part * 9 : g * 18 + part * 9 + 9, :] = v[g * 32 + part * 16 : g * 32 + part * 16 + 9]
    send_all(o_ref, r_ref)


def unmix_kernel(q_ref, w_ref, e_ref, s_ref, o_ref, l_ref, r_ref):
    for core in range(2):
        r_ref[core * XROWS : (core + 1) * XROWS, :] = sum_chips(q_ref, core) * SCALE
    l_ref[...] = jnp.zeros_like(l_ref)
    for g in range(G):
        for part in range(2):
            l_ref[g * 32 + part * 16 : g * 32 + part * 16 + 9, :] = part_rows(r_ref, g, part)
    vh, vl = split(l_ref[...])
    s_ref[...] = mm(vh, e_ref[...]) + mm(vl, e_ref[...])
    acc = [[None, None] for _ in range(G)]
    for o in range(C):
        gi, oi = divmod(o, CG)
        gr = s_ref[gi * 32 : gi * 32 + 9, oi * 128 : (oi + 1) * 128]
        gm = s_ref[gi * 32 + 16 : gi * 32 + 25, oi * 128 : (oi + 1) * 128]
        for g in range(G):
            wr, wi = w_ref[o, g, 0], w_ref[o, g, 1]
            a, b = wr * gr + wi * gm, wr * gm - wi * gr
            acc[g] = [a, b] if acc[g][0] is None else [acc[g][0] + a, acc[g][1] + b]
    for g in range(G):
        for part in range(2):
            r_ref[g * 18 + part * 9 : g * 18 + part * 9 + 9, :] = acc[g][part]
    send_all(o_ref, r_ref)


def outer_kernel(u_ref, s_ref, o_ref):
    us = [[part_rows(u_ref, g, part) for part in range(2)] for g in range(G)]
    for o in range(C):
        gi, oi = divmod(o, CG)
        gr = s_ref[gi * 32 : gi * 32 + 9, oi * 128 : (oi + 1) * 128]
        gm = s_ref[gi * 32 + 16 : gi * 32 + 25, oi * 128 : (oi + 1) * 128]
        for g in range(G):
            ur, ui = us[g]
            o_ref[o, g, 0] = gr * ur + gm * ui
            o_ref[o, g, 1] = gm * ur - gr * ui


def per_device(field, cotangent, spectral_weight, pointwise_weight, channel_bias):
    analysis, synthesis = zt_tables()
    toward = jnp.asarray(analysis.astype(jnp.bfloat16))
    toward_back = jnp.asarray(synthesis.astype(jnp.bfloat16))
    outward = jnp.asarray(three_rows(synthesis.T))
    outward_back = jnp.asarray(three_rows(analysis.T))
    ytab = y_table()
    y_in = [jnp.asarray(t) for t in halves(ytab)]
    yh, yl = halves(ytab.T)
    y_out = jnp.asarray(np.concatenate([yh, yh, yl], axis=1))
    xtab, xturned = x_tables()
    x_in = [jnp.asarray(t) for t in halves(xtab)]
    x_out = [jnp.asarray(t) for t in halves(xturned)]
    me = jnp.full((1,), lax.axis_index("gx"), jnp.int32)
    gather, spread = group_tables()
    gather, spread = jnp.asarray(gather.astype(jnp.bfloat16)), jnp.asarray(spread.astype(jnp.bfloat16))
    f = jnp.transpose(field, (0, 2, 1, 3))
    d = jnp.transpose(cotangent, (0, 2, 1, 3))
    row_channel = (np.arange(160) // YL) % C
    pick = (row_channel[:, None] == np.arange(C)[None, :]).astype(jnp.bfloat16)
    cell = (np.arange(160) // (C * YL)) * YL + np.arange(160) % YL
    wide = [jnp.asarray(v) for v in (pick, pick.T, (cell[:, None] == cell[None, :]).astype(jnp.bfloat16))]
    w = spectral_weight.reshape(2, G, CG, C, KX, KYL, ML)
    w = jnp.transpose(w, (3, 1, 0, 5, 6, 2, 4)).reshape(C, G, 2, MODES, KC)
    w = jnp.pad(w, ((0, 0),) * 4 + ((0, 128 - KC),))

    hbm, vmem = pl.BlockSpec(memory_space=pltpu.HBM), pl.BlockSpec(memory_space=pltpu.VMEM)
    smem = pl.BlockSpec(memory_space=pltpu.SMEM)

    def over_y(v):
        return lax.all_to_all(v.reshape(GY, 1, CHUNK * 128), "gy", split_axis=0, concat_axis=0, tiled=True).reshape(
            GY * CHUNK, 128
        )

    def over_x(v):
        return lax.all_to_all(v.reshape(GX, 1, XROWS * 128), "gx", split_axis=0, concat_axis=0, tiled=True).reshape(
            GX * XROWS, 128
        )

    def swap(v):
        return lax.ppermute(v, "gx", [(a, a ^ 1) for a in range(GX)])

    def kernel(body, outs, in_specs, *args, scratch, mib, out_specs=vmem):
        return pl.pallas_call(
            body,
            out_shape=outs,
            in_specs=in_specs,
            out_specs=out_specs,
            scratch_shapes=scratch,
            compiler_params=pltpu.CompilerParams(vmem_limit_bytes=mib * 2**20),
        )(*args)

    def contract(keep, send):
        return kernel(
            contract_kernel, shape(GY * CHUNK, 128), [smem, vmem, vmem, hbm, hbm],
            me, keep, swap(send), *far(*x_in), mib=16,
            scratch=[pltpu.VMEM((XC, 512), BF16)] * 2 + [pltpu.SemaphoreType.DMA((2,))],
        )

    def expand(v):
        keep, send = kernel(
            expand_kernel, (shape(2, KEEP, 128), shape(SWAP, 128)), [smem, vmem, hbm, hbm],
            me, v, *far(*x_out), mib=16, out_specs=(vmem, vmem),
            scratch=[pltpu.VMEM((256, 768), BF16)] * 2 + [pltpu.SemaphoreType.DMA((2,))],
        )
        return keep, swap(send)

    def outward_part(v):
        return call(outward_kernel, shape(GY * CHUNK, 128), over_x(v), y_out)

    cells = pltpu.VMEM((2, CELLS, 128), F32)
    rows = pltpu.VMEM((ROWS, 128), F32)
    part = pltpu.VMEM((320, Q), F32)
    full16 = pltpu.VMEM((CELLS, Q), BF16)
    native = pltpu.VMEM((XL, C, YL, Q), BF16)
    grid, grid16 = pltpu.HBM((CELLS, Q), F32), pltpu.HBM((CELLS, Q), BF16)
    kept, sent = shape(2, KEEP, 128), shape(SWAP, 128)
    keep, send = kernel(
        analyze_kernel, (kept, sent), [smem, hbm, hbm], me, *far(f, toward), mib=16, out_specs=(vmem, vmem),
        scratch=[cells, native, pltpu.VMEM((Q, N), BF16), pltpu.SemaphoreType.DMA((5,))],
    )
    v, w = lax.optimization_barrier((over_y(contract(keep, send)), w))
    v = call(inward_kernel, shape(GX * XROWS, 128), v, *y_in)
    u, v = call(
        mix_kernel, (shape(ROWS, 128), shape(GX * XROWS, 128)), over_x(v), w, gather,
        scratch=[pltpu.VMEM((128, CG * 128), F32), rows],
    )
    v, f, d = lax.optimization_barrier((outward_part(v), f, d))
    lin, d = call(
        linear_kernel, (grid, grid16), f, d, pointwise_weight.T, channel_bias.reshape(1, C), *wide, mib=18
    )
    v, lin, d = lax.optimization_barrier((over_y(v), lin, d))
    output, pre, keep, send = kernel(
        forward_kernel, (shape(XL, C, YL, Q, dtype=BF16), grid16, kept, sent), [smem] + [vmem] * 3 + [hbm, vmem, vmem],
        me, *expand(v), lin, *far(d), outward, toward_back, mib=28, out_specs=(hbm, hbm, vmem, vmem),
        scratch=[cells, cells, full16, part, native, full16, pltpu.SemaphoreType.DMA((3, 4))],
    )
    v = call(inward_kernel, shape(GX * XROWS, 128), over_y(contract(keep, send)), *y_in)
    s, v = call(
        unmix_kernel, (shape(128, CG * 128), shape(GX * XROWS, 128)), over_x(v), w, spread,
        scratch=[pltpu.VMEM((128, 128), F32), rows],
    )
    v, s, pre = lax.optimization_barrier((outward_part(v), s, pre))
    lin = call(linear_back_kernel, grid, pre, pointwise_weight, *wide, mib=14)
    gw = call(outer_kernel, shape(C, G, 2, MODES, 128), u, s)
    gw = gw[..., :KC].reshape(C, G, 2, KYL, ML, CG, KX)
    grad_weight = jnp.transpose(gw, (2, 1, 5, 0, 6, 3, 4)).reshape(2, C, C, KX, KYL, ML)
    v, lin, grad_weight = lax.optimization_barrier((over_y(v), lin, grad_weight))
    grad_field = kernel(
        backward_kernel, shape(XL, C, YL, Q, dtype=BF16), [smem] + [vmem] * 4,
        me, *expand(v), lin, outward_back, mib=18, out_specs=hbm,
        scratch=[cells, part, native, pltpu.SemaphoreType.DMA((4,))],
    )
    return (jnp.transpose(output, (0, 2, 1, 3)), jnp.transpose(grad_field, (0, 2, 1, 3)), grad_weight)


def solution(mesh):
    grid = P("gx", "gy", None, None)
    modes = P(None, None, None, None, "gx", "gy")
    return jax.shard_map(
        per_device,
        mesh=mesh,
        in_specs=(grid, grid, modes, P(), P()),
        out_specs=(grid, grid, modes),
        check_vma=False,
    )
```

time: 208 us -> 199 us (0.957)
  blocking collectives: 74.5 us -> 64.8 us
  local copies, waits for them, and re-layouts: 30.3 us -> 24.5 us
  waiting for transfers between devices: 37.6 us -> 41.8 us
    ppermute x0 -> x4, waiting for transfers between devices: none -> 7.28 us  [swap(): return lax.ppermute(v, 'gx', [(a, a ^ 1) for a in range(GX)])]
    all_to_all x4, blocking collectives: 42.8 us -> 36.6 us  [over_x(): lax.all_to_all(v.reshape(GX, 1, XROWS * 128), 'gx', split_axis=0, concat_...]
    all_to_all x1, blocking collectives: 31.7 us -> 28.1 us  [over_y(): lax.all_to_all(v.reshape(GY, 1, CHUNK * 128), 'gy', split_axis=0, concat_...]
    all_to_all x3, waiting for transfers between devices: 37.6 us -> 34.5 us  [over_y(): lax.all_to_all(v.reshape(GY, 1, CHUNK * 128), 'gy', split_axis=0, concat_...]
    pallas_call x7, Pallas kernels: 25.4 us -> 28 us  [kernel(): pl.pallas_call(body, out_shape=outs, in_specs=in_specs, out_specs=out_spe...]
    pallas_call x8 -> x9, Pallas kernels: 16.3 us -> 14.7 us  [call(): pl.pallas_call(body, out_shape=outs, scratch_shapes=list(scratch), compil...]
    unnamed x47 -> x37, local copies, waits for them, and re-layouts: 4.55 us -> 3.67 us
  transfers between devices with their start and end apart: 3 -> 7, of which waited for: 3 -> 7; matrix products, arithmetic and copies ran while one was open for 12% -> 11% of each run, Pallas kernels for 7% -> 5%
where the time goes in v3:
time: 199 us; the launch traced here: 197 us
  blocking collectives  64.8 us (33%)
  Pallas kernels  42.7 us (21%)
  waiting for transfers between devices  41.8 us (21%)
  local copies, waits for them, and re-layouts  24.5 us (12%)
  starting transfers between devices  22.3 us (11%)
    all_to_all x4, blocking collectives, over_x(): lax.all_to_all(v.reshape(GX, 1, XROWS * 128), 'gx', split_axis=0, concat_...  36.6 us
    all_to_all x3, waiting for transfers between devices, over_y(): lax.all_to_all(v.reshape(GY, 1, CHUNK * 128), 'gy', split_axis=0, concat_...  34.5 us
    all_to_all x1, blocking collectives, over_y(): lax.all_to_all(v.reshape(GY, 1, CHUNK * 128), 'gy', split_axis=0, concat_...  28.1 us
    pallas_call x7, Pallas kernels, kernel(): pl.pallas_call(body, out_shape=outs, in_specs=in_specs, out_specs=out_spe...  28 us
    all_to_all x3, starting transfers between devices, over_y(): lax.all_to_all(v.reshape(GY, 1, CHUNK * 128), 'gy', split_axis=0, concat_...  21.6 us
    pallas_call x9, Pallas kernels, call(): pl.pallas_call(body, out_shape=outs, scratch_shapes=list(scratch), compil...  14.7 us
    ppermute x4, waiting for transfers between devices, swap(): return lax.ppermute(v, 'gx', [(a, a ^ 1) for a in range(GX)])  7.28 us
    transpose x1, local copies, waits for them, and re-layouts, per_device(): jnp.transpose(gw, (2, 1, 5, 0, 6, 3, 4)).reshape(2, C, C, KX, KYL, ML)  6.56 us
  transfers between devices with their start and end apart: 7, of which 7 were waited for; matrix products, arithmetic and copies ran while one was open for 11% of the time, Pallas kernels for 5%

profile of v3, /device:TPU:32, one launch (start us, length us, event | category | flops | bytes accessed | tf_op | source)
XLA Modules:
  0.0 197.2 jit_solution(14961053083203973665)
XLA Ops:
  0.6 3.4 %shard_map.220 = (f32[2,640,128]{2,1,0:T(8,128)S(1)}, f32[960,128]{1,0:T(8,128)S(1)}) custom-call(s32[1]{0:T(128)} %bitcast.me_ref, bf16[16,20,4,1024]{3,2,1,0:T(4,128)(2,1)} %bitcast.34, bf16[1024,192]{1,0:T(8,128)(2,1)} %constant.41.clone.table_ref), custom_call_target="tpu_custom_call" | custom-call | tf_op jit(solution)/shard_map/pallas_call | solution.py:519
  4.1 0.1 collective-permute-start
  4.2 1.9 collective-permute-done.recv_ref
  6.0 3.5 %shard_map.221 = f32[1536,128]{1,0:T(8,128)} custom-call(s32[1]{0:T(128)} %bitcast.me_ref, f32[2,640,128]{2,1,0:T(8,128)S(1)} %get-tuple-element.33.keep_ref, f32[960,128]{1,0:T(8,128)S(1)} %collective-permute-done.recv_ref, bf16[8,320,512]{2,1,0:T(8,128)(2,1)} %constant.48.clone.high_hbm, bf16[8,320,512]{2,1,0:T(8,128)(2,1)} %constant.49.clone.low_hbm), custom_call_target="tpu_custom_call" | custom-call | tf_op jit(solution)/shard_map/pallas_call | solution.py:519
  9.5 11.4 %all-to-all-start = ((f32[32,1,6144]{2,1,0:T(1,128)}), f32[32,1,6144]{2,1,0:T(1,128)S(1)}, u32[]{:S(2)}, u32[]{:S(2)}) async-start(f32[32,1,6144]{2,1,0:T(1,128)} %bitcast.2), calls=%async_computation | async-start | bytes 1572864 | tf_op jit(solution)/shard_map/all_to_all | solution.py:506
  20.9 5.7 %copy.50 = f32[2,4,5,20,24,3,3]{4,2,0,6,5,1,3:T(8,128)} copy(f32[2,4,5,20,24,3,3]{4,0,6,5,3,2,1:T(2,128)} %bitcast.55) | data formatting | bytes 1382400 | tf_op jit(solution)/shard_map/reshape | solution.py:498
  26.7 4.3 %reshape.72 = f32[20,4,2,9,120]{4,2,3,1,0:T(2,128)S(1)} reshape(f32[20,4,2,3,3,5,24]{6,5,2,4,3,1,0:T(8,128)} %bitcast.54) | data formatting | bytes 1382400 | tf_op jit(solution)/shard_map/reshape | solution.py:499
  30.9 0.0 copy-start.13
  31.0 0.0 copy-start.14
  31.0 0.2 copy.38
  31.2 0.1 pad.4.w_ref
  31.3 12.9 %all-to-all-done = f32[32,1,6144]{2,1,0:T(1,128)S(1)} async-done(((f32[32,1,6144]{2,1,0:T(1,128)}), f32[32,1,6144]{2,1,0:T(1,128)S(1)}, u32[]{:S(2)}, u32[]{:S(2)}) %all-to-all-start) | async-done | bytes 786464 | tf_op jit(solution)/shard_map/all_to_all | solution.py:506
  44.2 0.5 shard_map.222
  44.8 0.0 copy-start.9
  44.8 10.5 %all_to_all.40 = f32[8,1,4608]{2,1,0:T(1,128)S(1)} all-to-all(f32[8,1,4608]{2,1,0:T(1,128)S(1)} %bitcast.47), channel_id=1, replica_groups=mesh['gx'=8,'gy'=32] {'gx'}, dimensions={0} | all-to-all | bytes 294912 | tf_op jit(solution)/shard_map/all_to_all | solution.py:511
  55.4 0.5 shard_map.223
  55.8 8.7 %all_to_all.41 = f32[8,1,4608]{2,1,0:T(1,128)S(1)} all-to-all(f32[8,1,4608]{2,1,0:T(1,128)S(1)} %bitcast.50), channel_id=1, replica_groups=mesh['gx'=8,'gy'=32] {'gx'}, dimensions={0} | all-to-all | bytes 294912 | tf_op jit(solution)/shard_map/all_to_all | solution.py:511
  64.5 1.3 shard_map.224
  65.8 5.1 %all-to-all-start.3 = ((f32[32,1,6144]{2,1,0:T(1,128)}), f32[32,1,6144]{2,1,0:T(1,128)S(1)}, u32[]{:S(2)}, u32[]{:S(2)}) async-start(f32[32,1,6144]{2,1,0:T(1,128)} %bitcast.11), calls=%async_computation.3 | async-start | bytes 1572864 | tf_op jit(solution)/shard_map/all_to_all | solution.py:506
  70.9 0.1 copy.42
  71.1 1.7 copy-done.1
  72.8 1.7 copy-done.3
  74.5 5.5 %shard_map.225 = (f32[1280,1024]{1,0:T(8,128)}, bf16[1280,1024]{1,0:T(8,128)(2,1)}) custom-call(bf16[16,20,4,1024]{3,2,1,0:T(4,128)(2,1)S(1)} %bitcast.35, bf16[16,20,4,1024]{3,2,1,0:T(4,128)(2,1)S(1)} %bitcast.42, bf16[20,20]{1,0:T(8,128)(2,1)S(1)} %bitcast.51, f32[1,20]{1,0:T(1,128)S(1)} %bitcast.52, bf16[160,20]{1,0:T(8,128)(2,1)S(1)} %copy-done.12, ...), custom_call_target="tpu_custom_call" | custom-call | tf_op jit(solution)/shard_map/pallas_call | solution.py:130
  80.0 13.9 %all-to-all-done.3 = f32[32,1,6144]{2,1,0:T(1,128)S(1)} async-done(((f32[32,1,6144]{2,1,0:T(1,128)}), f32[32,1,6144]{2,1,0:T(1,128)S(1)}, u32[]{:S(2)}, u32[]{:S(2)}) %all-to-all-start.3) | async-done | bytes 786464 | tf_op jit(solution)/shard_map/all_to_all | solution.py:506
  93.9 2.8 %shard_map.226 = (f32[2,640,128]{2,1,0:T(8,128)S(1)}, f32[960,128]{1,0:T(8,128)S(1)}) custom-call(s32[1]{0:T(128)} %bitcast.me_ref, f32[1536,128]{1,0:T(8,128)S(1)} %bitcast.38, bf16[8,256,768]{2,1,0:T(8,128)(2,1)} %constant.50.clone.high_hbm, bf16[8,256,768]{2,1,0:T(8,128)(2,1)} %constant.51.clone.low_hbm), custom_call_target="tpu_custom_call" | custom-call | tf_op jit(solution)/shard_map/pallas_call | solution.py:519
  96.7 0.3 collective-permute-start.1
  97.0 1.9 collective-permute-done.1.recv_ref
  98.9 9.4 %shard_map.227 = (bf16[16,20,4,1024]{3,2,1,0:T(4,128)(2,1)}, bf16[1280,1024]{1,0:T(8,128)(2,1)}, f32[2,640,128]{2,1,0:T(8,128)S(1)}, f32[960,128]{1,0:T(8,128)S(1)}) custom-call(s32[1]{0:T(128)} %bitcast.me_ref, f32[2,640,128]{2,1,0:T(8,128)S(1)} %get-tuple-element.44.keep_ref, f32[960,128]{1,0:T(8,128)S(1)} %collective-permute-done.1.recv_ref, ...), custom_call_target="tpu_custom_call" | custom-call | tf_op jit(solution)/shard_map/pallas_call | solution.py:519
  108.3 0.2 collective-permute-start.2
  108.5 1.7 collective-permute-done.2.recv_ref
  110.3 2.6 %shard_map.228 = f32[1536,128]{1,0:T(8,128)S(1)} custom-call(s32[1]{0:T(128)} %bitcast.me_ref, f32[2,640,128]{2,1,0:T(8,128)S(1)} %get-tuple-element.49.keep_ref, f32[960,128]{1,0:T(8,128)S(1)} %collective-permute-done.2.recv_ref, bf16[8,320,512]{2,1,0:T(8,128)(2,1)} %constant.48.clone.high_hbm, bf16[8,320,512]{2,1,0:T(8,128)(2,1)} %constant.49.clone.low_hbm), custom_call_target="tpu_custom_call" | custom-call | tf_op jit(solution)/shard_map/pallas_call | solution.py:519
  112.9 28.1 %all_to_all.42 = f32[32,1,6144]{2,1,0:T(1,128)S(1)} all-to-all(f32[32,1,6144]{2,1,0:T(1,128)S(1)} %bitcast.39), channel_id=1, replica_groups=mesh['gx'=8,'gy'=32] {'gy'}, dimensions={0} | all-to-all | bytes 1572864 | tf_op jit(solution)/shard_map/all_to_all | solution.py:506
  141.1 0.5 shard_map.229
  141.6 8.7 %all_to_all.43 = f32[8,1,4608]{2,1,0:T(1,128)S(1)} all-to-all(f32[8,1,4608]{2,1,0:T(1,128)S(1)} %bitcast.45), channel_id=1, replica_groups=mesh['gx'=8,'gy'=32] {'gx'}, dimensions={0} | all-to-all | bytes 294912 | tf_op jit(solution)/shard_map/all_to_all | solution.py:511
  150.3 0.5 shard_map.230
  150.8 8.7 %all_to_all.44 = f32[8,1,4608]{2,1,0:T(1,128)S(1)} all-to-all(f32[8,1,4608]{2,1,0:T(1,128)S(1)} %bitcast.49), channel_id=1, replica_groups=mesh['gx'=8,'gy'=32] {'gx'}, dimensions={0} | all-to-all | bytes 294912 | tf_op jit(solution)/shard_map/all_to_all | solution.py:511
  159.5 1.3 shard_map.231
  160.8 5.1 %all-to-all-start.7 = ((f32[32,1,6144]{2,1,0:T(1,128)}), f32[32,1,6144]{2,1,0:T(1,128)S(1)}, u32[]{:S(2)}, u32[]{:S(2)}) async-start(f32[32,1,6144]{2,1,0:T(1,128)} %bitcast.22), calls=%async_computation.7 | async-start | bytes 1572864 | tf_op jit(solution)/shard_map/all_to_all | solution.py:506
  165.9 0.1 shard_map.233
  166.0 0.4 copy.47
  166.4 3.6 %reshape.88 = f32[20,4,2,3,3,5,24]{6,5,2,4,3,1,0:T(8,128)} reshape(f32[20,4,2,9,120]{4,2,3,1,0:T(2,128)S(1)} %copy.47) | data formatting | bytes 1382400 | tf_op jit(solution)/shard_map/reshape | solution.py:581
  170.0 6.6 %copy.48 = f32[2,4,5,20,24,3,3]{4,0,6,5,3,2,1:T(2,128)} copy(f32[2,4,5,20,24,3,3]{4,2,0,6,5,1,3:T(8,128)} %bitcast.53) | data formatting | bytes 1382400 | tf_op jit(solution)/shard_map/transpose | solution.py:582
  176.6 4.5 %shard_map.232.lin_ref = f32[1280,1024]{1,0:T(8,128)} custom-call(bf16[1280,1024]{1,0:T(8,128)(2,1)S(1)} %copy-done.4, bf16[20,20]{1,0:T(8,128)(2,1)S(1)} %copy-done.16, bf16[160,20]{1,0:T(8,128)(2,1)S(1)} %copy-done.12, bf16[20,160]{1,0:T(8,128)(2,1)S(1)} %copy-done.15, bf16[160,160]{1,0:T(8,128)(2,1)S(1)} %copy-done.9), custom_call_target="tpu_custom_call" | custom-call | tf_op jit(solution)/shard_map/pallas_call | solution.py:130
  181.1 7.7 %all-to-all-done.7 = f32[32,1,6144]{2,1,0:T(1,128)S(1)} async-done(((f32[32,1,6144]{2,1,0:T(1,128)}), f32[32,1,6144]{2,1,0:T(1,128)S(1)}, u32[]{:S(2)}, u32[]{:S(2)}) %all-to-all-start.7) | async-done | bytes 786464 | tf_op jit(solution)/shard_map/all_to_all | solution.py:506
  188.9 2.8 %shard_map.234 = (f32[2,640,128]{2,1,0:T(8,128)S(1)}, f32[960,128]{1,0:T(8,128)S(1)}) custom-call(s32[1]{0:T(128)} %bitcast.me_ref, f32[1536,128]{1,0:T(8,128)S(1)} %bitcast.37, bf16[8,256,768]{2,1,0:T(8,128)(2,1)} %constant.50.clone.high_hbm, bf16[8,256,768]{2,1,0:T(8,128)(2,1)} %constant.51.clone.low_hbm), custom_call_target="tpu_custom_call" | custom-call | tf_op jit(solution)/shard_map/pallas_call | solution.py:519
  191.7 0.1 collective-permute-start.3
  191.8 1.9 collective-permute-done.3.recv_ref
  193.7 3.3 %shard_map.235 = bf16[16,20,4,1024]{3,2,1,0:T(4,128)(2,1)} custom-call(s32[1]{0:T(128)} %bitcast.me_ref, f32[2,640,128]{2,1,0:T(8,128)S(1)} %get-tuple-element.59.keep_ref, f32[960,128]{1,0:T(8,128)S(1)} %collective-permute-done.3.recv_ref, f32[1280,1024]{1,0:T(8,128)S(1)} %copy-done, bf16[576,1024]{1,0:T(8,128)(2,1)S(1)} %copy-done.5), custom_call_target="tpu_custom_call" | custom-call | tf_op jit(solution)/shard_map/pallas_call | solution.py:519
  (31 shorter events, 0.1 us)
Async XLA Ops:
  4.1 2.0 collective-permute-start
  9.5 34.7 %all-to-all-start = ((f32[32,1,6144]{2,1,0:T(1,128)}), f32[32,1,6144]{2,1,0:T(1,128)S(1)}, u32[]{:S(2)}, u32[]{:S(2)}) async-start(f32[32,1,6144]{2,1,0:T(1,128)} %bitcast.2), calls=%async_computation | async-start | bytes 1572864 | tf_op jit(solution)/shard_map/all_to_all | solution.py:506
  30.9 13.3 %copy-start.13 = (bf16[48,256]{1,0:T(8,128)(2,1)S(1)}, bf16[48,256]{1,0:T(8,128)(2,1)}, u32[]{:S(2)}) copy-start(bf16[48,256]{1,0:T(8,128)(2,1)} %constant.46.clone.yl_ref) | copy-start | bytes 73732
  31.0 13.3 %copy-start.14 = (bf16[48,256]{1,0:T(8,128)(2,1)S(1)}, bf16[48,256]{1,0:T(8,128)(2,1)}, u32[]{:S(2)}) copy-start(bf16[48,256]{1,0:T(8,128)(2,1)} %constant.45.clone.yh_ref) | copy-start | bytes 73732
  31.0 24.4 %copy-start.11 = (bf16[640,128]{1,0:T(8,128)(2,1)S(1)}, bf16[640,128]{1,0:T(8,128)(2,1)}, u32[]{:S(2)}) copy-start(bf16[640,128]{1,0:T(8,128)(2,1)} %constant.52.clone.e_ref) | copy-start | bytes 491524
  31.2 33.3 %copy-start.7 = (bf16[256,144]{1,0:T(8,128)(2,1)S(1)}, bf16[256,144]{1,0:T(8,128)(2,1)}, u32[]{:S(2)}) copy-start(bf16[256,144]{1,0:T(8,128)(2,1)} %constant.47.clone.y_ref) | copy-start | bytes 221188
  44.7 26.2 %copy-start.16 = (bf16[20,20]{1,0:T(8,128)(2,1)S(1)}, bf16[20,20]{1,0:T(8,128)(2,1)}, u32[]{:S(2)}) copy-start(bf16[20,20]{1,0:T(8,128)(2,1)} %w_ref.1) | copy-start | bytes 2404
  44.8 26.3 %copy-start.9 = (bf16[160,160]{1,0:T(8,128)(2,1)S(1)}, bf16[160,160]{1,0:T(8,128)(2,1)}, u32[]{:S(2)}) copy-start(bf16[160,160]{1,0:T(8,128)(2,1)} %constant.56.clone.mask_ref) | copy-start | bytes 153604
  44.8 26.3 %copy-start.12 = (bf16[160,20]{1,0:T(8,128)(2,1)S(1)}, bf16[160,20]{1,0:T(8,128)(2,1)}, u32[]{:S(2)}) copy-start(bf16[160,20]{1,0:T(8,128)(2,1)} %constant.54.clone.e_ref) | copy-start | bytes 19204
  44.8 26.2 %copy-start.15 = (bf16[20,160]{1,0:T(8,128)(2,1)S(1)}, bf16[20,160]{1,0:T(8,128)(2,1)}, u32[]{:S(2)}) copy-start(bf16[20,160]{1,0:T(8,128)(2,1)} %constant.55.clone.et_ref) | copy-start | bytes 19204
  44.8 26.2 %copy-start.17 = (f32[20]{0:T(128)S(1)}, f32[20]{0:T(128)}, u32[]{:S(2)}) copy-start(f32[20]{0:T(128)} %param.25) | copy-start | bytes 244
  65.8 28.1 %all-to-all-start.3 = ((f32[32,1,6144]{2,1,0:T(1,128)}), f32[32,1,6144]{2,1,0:T(1,128)S(1)}, u32[]{:S(2)}, u32[]{:S(2)}) async-start(f32[32,1,6144]{2,1,0:T(1,128)} %bitcast.11), calls=%async_computation.3 | async-start | bytes 1572864 | tf_op jit(solution)/shard_map/all_to_all | solution.py:506
  71.0 1.7 copy-start.1
  72.8 1.7 copy-start.3
  93.9 5.0 %copy-start.2 = (f32[1280,1024]{1,0:T(8,128)S(1)}, f32[1280,1024]{1,0:T(8,128)}, u32[]{:S(2)}) copy-start(f32[1280,1024]{1,0:T(8,128)} %get-tuple-element.46.lin_ref) | copy-start | bytes 15728644
  93.9 5.0 %copy-start.6 = (bf16[576,1024]{1,0:T(8,128)(2,1)S(1)}, bf16[576,1024]{1,0:T(8,128)(2,1)}, u32[]{:S(2)}) copy-start(bf16[576,1024]{1,0:T(8,128)(2,1)} %constant.43.clone.s_ref) | copy-start | bytes 3538948
  93.9 5.0 %copy-start.8 = (bf16[1024,192]{1,0:T(8,128)(2,1)S(1)}, bf16[1024,192]{1,0:T(8,128)(2,1)}, u32[]{:S(2)}) copy-start(bf16[1024,192]{1,0:T(8,128)(2,1)} %constant.42.clone.t_ref) | copy-start | bytes 1179652
  96.7 2.1 %collective-permute-start.1 = (f32[960,128]{1,0:T(8,128)S(1)}, f32[960,128]{1,0:T(8,128)S(1)}, u32[]{:S(2)}, u32[]{:S(2)}) collective-permute-start(f32[960,128]{1,0:T(8,128)S(1)} %get-tuple-element.45), channel_id=1, source_target_pairs={{0,32},{32,0},{64,96},{96,64},{128,160},{160,128},{192,224},{224,1... | collective-permute-start | bytes 1474568 | tf_op jit(solution)/shard_map/ppermute | solution.py:516
  108.3 2.0 collective-permute-start.2
  112.9 37.4 %copy-start.10 = (bf16[128,640]{1,0:T(8,128)(2,1)S(1)}, bf16[128,640]{1,0:T(8,128)(2,1)}, u32[]{:S(2)}) copy-start(bf16[128,640]{1,0:T(8,128)(2,1)} %constant.53.clone.e_ref) | copy-start | bytes 491524
  160.8 28.1 %all-to-all-start.7 = ((f32[32,1,6144]{2,1,0:T(1,128)}), f32[32,1,6144]{2,1,0:T(1,128)S(1)}, u32[]{:S(2)}, u32[]{:S(2)}) async-start(f32[32,1,6144]{2,1,0:T(1,128)} %bitcast.22), calls=%async_computation.7 | async-start | bytes 1572864 | tf_op jit(solution)/shard_map/all_to_all | solution.py:506
  170.0 6.6 %copy-start.4 = (bf16[1280,1024]{1,0:T(8,128)(2,1)S(1)}, bf16[1280,1024]{1,0:T(8,128)(2,1)}, u32[]{:S(2)}) copy-start(bf16[1280,1024]{1,0:T(8,128)(2,1)} %get-tuple-element.55.p_ref) | copy-start | bytes 7864324
  188.8 4.8 %copy-start = (f32[1280,1024]{1,0:T(8,128)S(1)}, f32[1280,1024]{1,0:T(8,128)}, u32[]{:S(2)}) copy-start(f32[1280,1024]{1,0:T(8,128)} %shard_map.232.lin_ref) | copy-start | bytes 15728644
  188.9 4.8 %copy-start.5 = (bf16[576,1024]{1,0:T(8,128)(2,1)S(1)}, bf16[576,1024]{1,0:T(8,128)(2,1)}, u32[]{:S(2)}) copy-start(bf16[576,1024]{1,0:T(8,128)(2,1)} %constant.44.clone.s_ref) | copy-start | bytes 3538948
  191.7 2.0 collective-permute-start.3

commit v4 on v3

--- a/solution.py
+++ b/solution.py
@@ -33,7 +33,8 @@
 KEEP = HC * YL
 SWAP = KEEP * 3 // 2
 LT = 6
-CHUNK = LT * 8
+WHOLE = 5
+CHUNK = WHOLE * 8 + 5
 G = 4
 CG = C // G
 KC = CG * KX
@@ -103,7 +104,8 @@
                 t[a, side, :, c, 1, g, j * KX : (j + 1) * KX] = np.sin(angles)
     turned = np.zeros((GX, 256, 2, 384))
     turned[..., :XC] = np.transpose(t, (0, 5, 6, 4, 1, 2, 3)).reshape(GX, 256, 2, XC)
-    return t.reshape(GX, XC, 512), turned.reshape(GX, 256, 768)
+    turned = turned.reshape(GX, 2, 128, 768)[:, :, :KC].reshape(GX, 2 * KC, 768)
+    return t.reshape(GX, XC, 512), turned
 
 
 def group_tables():
@@ -173,6 +175,25 @@
             g_ref[1, halves_of_rows(core, x + h * XL // 2)[1], :64] = both[:, h * 64 : h * 64 + 64]
 
 
+def store_rest(o_ref, rests):
+    for j in range(4):
+        o_ref[pl.ds(WHOLE * 8 + j, GY, stride=CHUNK), :] = jnp.concatenate(
+            [rests[2 * j][:, :64], rests[2 * j + 1][:, :64]], axis=1
+        )
+    o_ref[pl.ds(WHOLE * 8 + 4, GY, stride=CHUNK), :] = jnp.concatenate([r[:, 64:80] for r in rests], axis=1)
+
+
+def load_rest(r_ref):
+    halves_of_tiles = [r_ref[pl.ds(WHOLE * 8 + j, GY, stride=CHUNK), :] for j in range(4)]
+    last = r_ref[pl.ds(WHOLE * 8 + 4, GY, stride=CHUNK), :]
+    return [
+        jnp.concatenate(
+            [halves_of_tiles[k // 2][:, k % 2 * 64 : k % 2 * 64 + 64], last[:, k * 16 : k * 16 + 16]], axis=1
+        )
+        for k in range(8)
+    ]
+
+
 def load_tables(me_ref, high_hbm, low_hbm, high_ref, low_ref, sems):
     me = me_ref[0]
     copies = [
@@ -200,33 +221,34 @@
     for copy in copies:
         copy.wait()
     p = mm(vh, high_ref[...]) + (mm(vl, high_ref[...]) + mm(vh, low_ref[...]))
+    rests = [None] * 8
     for y in range(YL):
+        lanes = ([], [])
         for m in range(ML):
             at = y * N + m * GY
             re, im = p[at : at + GY], p[at + N // 2 : at + N // 2 + GY]
             parts = (re[:, :256] + im[:, 256:], im[:, :256] - re[:, 256:])
             for part in range(2):
-                for g in range(2):
-                    o_ref[pl.ds((m * 2 + g) * 8 + part * YL + y, GY, stride=CHUNK), :] = parts[part][
-                        :, g * 128 : (g + 1) * 128
-                    ]
+                lanes[part].extend(parts[part][:, g * 128 : g * 128 + KC] for g in range(2))
+        for part in range(2):
+            row = jnp.concatenate(lanes[part], axis=1)
+            for lt in range(WHOLE):
+                o_ref[pl.ds(lt * 8 + part * YL + y, GY, stride=CHUNK), :] = row[:, lt * 128 : (lt + 1) * 128]
+            rests[part * YL + y] = row[:, WHOLE * 128 :]
+    store_rest(o_ref, rests)
 
 
 def expand_kernel(me_ref, r_ref, high_hbm, low_hbm, keep_ref, send_ref, high_ref, low_ref, sems):
     copies = load_tables(me_ref, high_hbm, low_hbm, high_ref, low_ref, sems)
     rows = []
+    rests = load_rest(r_ref)
     for y in range(YL):
         for part in range(2):
-            for m in range(ML):
-                rows.append(
-                    jnp.concatenate(
-                        [
-                            r_ref[pl.ds((m * 2 + g) * 8 + part * YL + y, GY, stride=CHUNK), :]
-                            for g in range(2)
-                        ],
-                        axis=1,
-                    )
-                )
+            k = part * YL + y
+            row = jnp.concatenate(
+                [r_ref[pl.ds(lt * 8 + k, GY, stride=CHUNK), :] for lt in range(WHOLE)] + [rests[k]], axis=1
+            )
+            rows += [row[:, m * 2 * KC : (m + 1) * 2 * KC] for m in range(ML)]
     vh, vl = split(jnp.concatenate(rows, axis=0))
     for copy in copies:
         copy.wait()
@@ -363,19 +385,21 @@
 
 
 def inward_kernel(r_ref, yh_ref, yl_ref, o_ref):
-    columns = []
-    for lt in range(LT):
-        columns.append(
-            jnp.concatenate([r_ref[pl.ds(lt * 8 + k, GY, stride=CHUNK), :] for k in range(8)], axis=0)
-        )
+    columns = [
+        jnp.concatenate([r_ref[pl.ds(lt * 8 + k, GY, stride=CHUNK), :] for k in range(8)], axis=0)
+        for lt in range(WHOLE)
+    ]
+    columns.append(jnp.concatenate(load_rest(r_ref), axis=0))
     vh, vl = split(jnp.concatenate(columns, axis=1))
     p = mm(yh_ref[...], vh) + (mm(yh_ref[...], vl) + mm(yl_ref[...], vh))
+    blank = jnp.zeros((2 * KY, 128 - KC), F32)
     for lt in range(LT):
         m, g = divmod(lt, 2)
+        tile = jnp.concatenate([p[:, lt * KC : (lt + 1) * KC], blank], axis=1)
         for part in range(2):
             for ky in range(KYL):
-                o_ref[pl.ds(g * 18 + part * 9 + ky * ML + m, GX, stride=XROWS), :] = p[
-                    part * 24 + ky * 8 : part * 24 + ky * 8 + 8, lt * 128 : (lt + 1) * 128
+                o_ref[pl.ds(g * 18 + part * 9 + ky * ML + m, GX, stride=XROWS), :] = tile[
+                    part * 24 + ky * 8 : part * 24 + ky * 8 + 8
                 ]
 
 
@@ -391,13 +415,14 @@
                     for ky in range(KYL)
                 ],
                 axis=0,
-            )
+            )[:, :KC]
         )
     vh, vl = split(jnp.concatenate(columns, axis=1))
     o = mm(y_ref[...], jnp.concatenate([vh, vl, vh], axis=0))
-    for lt in range(LT):
-        for k in range(8):
+    for k in range(8):
+        for lt in range(WHOLE):
             o_ref[pl.ds(lt * 8 + k, GY, stride=CHUNK), :] = o[k * GY : (k + 1) * GY, lt * 128 : (lt + 1) * 128]
+    store_rest(o_ref, [o[k * GY : (k + 1) * GY, WHOLE * 128 :] for k in range(8)])
 
 
 def part_rows(ref, g, part):
@@ -536,7 +561,7 @@
         keep, send = kernel(
             expand_kernel, (shape(2, KEEP, 128), shape(SWAP, 128)), [smem, vmem, hbm, hbm],
             me, v, *far(*x_out), mib=16, out_specs=(vmem, vmem),
-            scratch=[pltpu.VMEM((256, 768), BF16)] * 2 + [pltpu.SemaphoreType.DMA((2,))],
+            scratch=[pltpu.VMEM((2 * KC, 768), BF16)] * 2 + [pltpu.SemaphoreType.DMA((2,))],
         )
         return keep, swap(send)
 

time: 199 us -> 196 us (0.985)
  waiting for transfers between devices: 41.8 us -> 38.8 us
    all_to_all x3, waiting for transfers between devices: 34.5 us -> 31.5 us  [over_y(): lax.all_to_all(v.reshape(GY, 1, CHUNK * 128), 'gy', split_axis=0, concat_...]
where the time goes in v4:
time: 196 us; the launch traced here: 193 us
  blocking collectives  63.7 us (32%)
  Pallas kernels  43.2 us (22%)
  waiting for transfers between devices  38.8 us (20%)
  local copies, waits for them, and re-layouts  24.5 us (12%)
  starting transfers between devices  22 us (11%)
    all_to_all x4, blocking collectives, over_x(): lax.all_to_all(v.reshape(GX, 1, XROWS * 128), 'gx', split_axis=0, concat_...  36.5 us
    all_to_all x3, waiting for transfers between devices, over_y(): lax.all_to_all(v.reshape(GY, 1, CHUNK * 128), 'gy', split_axis=0, concat_...  31.5 us
    pallas_call x7, Pallas kernels, kernel(): pl.pallas_call(body, out_shape=outs, in_specs=in_specs, out_specs=out_spe...  28.7 us
    all_to_all x1, blocking collectives, over_y(): lax.all_to_all(v.reshape(GY, 1, CHUNK * 128), 'gy', split_axis=0, concat_...  27.2 us
    all_to_all x3, starting transfers between devices, over_y(): lax.all_to_all(v.reshape(GY, 1, CHUNK * 128), 'gy', split_axis=0, concat_...  21.3 us
    pallas_call x9, Pallas kernels, call(): pl.pallas_call(body, out_shape=outs, scratch_shapes=list(scratch), compil...  14.5 us
    ppermute x4, waiting for transfers between devices, swap(): return lax.ppermute(v, 'gx', [(a, a ^ 1) for a in range(GX)])  7.28 us
    transpose x1, local copies, waits for them, and re-layouts, per_device(): jnp.transpose(gw, (2, 1, 5, 0, 6, 3, 4)).reshape(2, C, C, KX, KYL, ML)  6.56 us
  transfers between devices with their start and end apart: 7, of which 7 were waited for; matrix products, arithmetic and copies ran while one was open for 11% of the time, Pallas kernels for 5%

profile of v4, /device:TPU:32, one launch (start us, length us, event | category | flops | bytes accessed | tf_op | source)
XLA Modules:
  0.0 193.3 jit_solution(10895150379436348287)
XLA Ops:
  0.6 3.4 %shard_map.220 = (f32[2,640,128]{2,1,0:T(8,128)S(1)}, f32[960,128]{1,0:T(8,128)S(1)}) custom-call(s32[1]{0:T(128)} %bitcast.me_ref, bf16[16,20,4,1024]{3,2,1,0:T(4,128)(2,1)} %bitcast.34, bf16[1024,192]{1,0:T(8,128)(2,1)} %constant.41.clone.table_ref), custom_call_target="tpu_custom_call" | custom-call | tf_op jit(solution)/shard_map/pallas_call | solution.py:544
  4.1 0.1 collective-permute-start
  4.2 1.9 collective-permute-done.recv_ref
  6.0 3.9 %shard_map.221 = f32[1440,128]{1,0:T(8,128)} custom-call(s32[1]{0:T(128)} %bitcast.me_ref, f32[2,640,128]{2,1,0:T(8,128)S(1)} %get-tuple-element.33.keep_ref, f32[960,128]{1,0:T(8,128)S(1)} %collective-permute-done.recv_ref, bf16[8,320,512]{2,1,0:T(8,128)(2,1)} %constant.48.clone.high_hbm, bf16[8,320,512]{2,1,0:T(8,128)(2,1)} %constant.49.clone.low_hbm), custom_call_target="tpu_custom_call" | custom-call | tf_op jit(solution)/shard_map/pallas_call | solution.py:544
  9.9 11.4 %all-to-all-start = ((f32[32,1,5760]{2,1,0:T(1,128)}), f32[32,1,5760]{2,1,0:T(1,128)S(1)}, u32[]{:S(2)}, u32[]{:S(2)}) async-start(f32[32,1,5760]{2,1,0:T(1,128)} %bitcast.2), calls=%async_computation | async-start | bytes 1474560 | tf_op jit(solution)/shard_map/all_to_all | solution.py:531
  21.3 5.7 %copy.50 = f32[2,4,5,20,24,3,3]{4,2,0,6,5,1,3:T(8,128)} copy(f32[2,4,5,20,24,3,3]{4,0,6,5,3,2,1:T(2,128)} %bitcast.55) | data formatting | bytes 1382400 | tf_op jit(solution)/shard_map/reshape | solution.py:523
  27.0 4.3 %reshape.72 = f32[20,4,2,9,120]{4,2,3,1,0:T(2,128)S(1)} reshape(f32[20,4,2,3,3,5,24]{6,5,2,4,3,1,0:T(8,128)} %bitcast.54) | data formatting | bytes 1382400 | tf_op jit(solution)/shard_map/reshape | solution.py:524
  31.3 0.0 copy-start.13
  31.3 0.0 copy-start.14
  31.3 0.0 copy-start.11
  31.4 0.2 copy.38
  31.6 0.1 pad.4.w_ref
  31.7 12.0 %all-to-all-done = f32[32,1,5760]{2,1,0:T(1,128)S(1)} async-done(((f32[32,1,5760]{2,1,0:T(1,128)}), f32[32,1,5760]{2,1,0:T(1,128)S(1)}, u32[]{:S(2)}, u32[]{:S(2)}) %all-to-all-start) | async-done | bytes 737312 | tf_op jit(solution)/shard_map/all_to_all | solution.py:531
  43.7 0.4 shard_map.222
  44.2 10.4 %all_to_all.40 = f32[8,1,4608]{2,1,0:T(1,128)S(1)} all-to-all(f32[8,1,4608]{2,1,0:T(1,128)S(1)} %bitcast.46), channel_id=1, replica_groups=mesh['gx'=8,'gy'=32] {'gx'}, dimensions={0} | all-to-all | bytes 294912 | tf_op jit(solution)/shard_map/all_to_all | solution.py:536
  54.6 0.5 shard_map.223
  55.0 8.7 %all_to_all.41 = f32[8,1,4608]{2,1,0:T(1,128)S(1)} all-to-all(f32[8,1,4608]{2,1,0:T(1,128)S(1)} %bitcast.50), channel_id=1, replica_groups=mesh['gx'=8,'gy'=32] {'gx'}, dimensions={0} | all-to-all | bytes 294912 | tf_op jit(solution)/shard_map/all_to_all | solution.py:536
  63.7 1.3 shard_map.224
  65.0 5.0 %all-to-all-start.3 = ((f32[32,1,5760]{2,1,0:T(1,128)}), f32[32,1,5760]{2,1,0:T(1,128)S(1)}, u32[]{:S(2)}, u32[]{:S(2)}) async-start(f32[32,1,5760]{2,1,0:T(1,128)} %bitcast.11), calls=%async_computation.3 | async-start | bytes 1474560 | tf_op jit(solution)/shard_map/all_to_all | solution.py:531
  70.0 0.1 copy.42
  70.1 1.7 copy-done.1
  71.9 1.7 copy-done.3
  73.6 5.5 %shard_map.225 = (f32[1280,1024]{1,0:T(8,128)}, bf16[1280,1024]{1,0:T(8,128)(2,1)}) custom-call(bf16[16,20,4,1024]{3,2,1,0:T(4,128)(2,1)S(1)} %bitcast.35, bf16[16,20,4,1024]{3,2,1,0:T(4,128)(2,1)S(1)} %bitcast.42, bf16[20,20]{1,0:T(8,128)(2,1)S(1)} %bitcast.51, f32[1,20]{1,0:T(1,128)S(1)} %bitcast.52, bf16[160,20]{1,0:T(8,128)(2,1)S(1)} %copy-done.12, ...), custom_call_target="tpu_custom_call" | custom-call | tf_op jit(solution)/shard_map/pallas_call | solution.py:132
  79.1 12.8 %all-to-all-done.3 = f32[32,1,5760]{2,1,0:T(1,128)S(1)} async-done(((f32[32,1,5760]{2,1,0:T(1,128)}), f32[32,1,5760]{2,1,0:T(1,128)S(1)}, u32[]{:S(2)}, u32[]{:S(2)}) %all-to-all-start.3) | async-done | bytes 737312 | tf_op jit(solution)/shard_map/all_to_all | solution.py:531
  91.9 2.8 %shard_map.226 = (f32[2,640,128]{2,1,0:T(8,128)S(1)}, f32[960,128]{1,0:T(8,128)S(1)}) custom-call(s32[1]{0:T(128)} %bitcast.me_ref, f32[1440,128]{1,0:T(8,128)S(1)} %bitcast.41, bf16[8,240,768]{2,1,0:T(8,128)(2,1)} %constant.50.clone.high_hbm, bf16[8,240,768]{2,1,0:T(8,128)(2,1)} %constant.51.clone.low_hbm), custom_call_target="tpu_custom_call" | custom-call | tf_op jit(solution)/shard_map/pallas_call | solution.py:544
  94.8 0.3 collective-permute-start.1
  95.1 1.9 collective-permute-done.1.recv_ref
  96.9 9.4 %shard_map.227 = (bf16[16,20,4,1024]{3,2,1,0:T(4,128)(2,1)}, bf16[1280,1024]{1,0:T(8,128)(2,1)}, f32[2,640,128]{2,1,0:T(8,128)S(1)}, f32[960,128]{1,0:T(8,128)S(1)}) custom-call(s32[1]{0:T(128)} %bitcast.me_ref, f32[2,640,128]{2,1,0:T(8,128)S(1)} %get-tuple-element.44.keep_ref, f32[960,128]{1,0:T(8,128)S(1)} %collective-permute-done.1.recv_ref, ...), custom_call_target="tpu_custom_call" | custom-call | tf_op jit(solution)/shard_map/pallas_call | solution.py:544
  106.4 0.2 collective-permute-start.2
  106.6 1.7 collective-permute-done.2.recv_ref
  108.3 3.0 %shard_map.228 = f32[1440,128]{1,0:T(8,128)S(1)} custom-call(s32[1]{0:T(128)} %bitcast.me_ref, f32[2,640,128]{2,1,0:T(8,128)S(1)} %get-tuple-element.49.keep_ref, f32[960,128]{1,0:T(8,128)S(1)} %collective-permute-done.2.recv_ref, bf16[8,320,512]{2,1,0:T(8,128)(2,1)} %constant.48.clone.high_hbm, bf16[8,320,512]{2,1,0:T(8,128)(2,1)} %constant.49.clone.low_hbm), custom_call_target="tpu_custom_call" | custom-call | tf_op jit(solution)/shard_map/pallas_call | solution.py:544
  111.3 27.2 %all_to_all.42 = f32[32,1,5760]{2,1,0:T(1,128)S(1)} all-to-all(f32[32,1,5760]{2,1,0:T(1,128)S(1)} %bitcast.37), channel_id=1, replica_groups=mesh['gx'=8,'gy'=32] {'gy'}, dimensions={0} | all-to-all | bytes 1474560 | tf_op jit(solution)/shard_map/all_to_all | solution.py:531
  138.5 0.4 shard_map.229
  139.0 8.7 %all_to_all.43 = f32[8,1,4608]{2,1,0:T(1,128)S(1)} all-to-all(f32[8,1,4608]{2,1,0:T(1,128)S(1)} %bitcast.45), channel_id=1, replica_groups=mesh['gx'=8,'gy'=32] {'gx'}, dimensions={0} | all-to-all | bytes 294912 | tf_op jit(solution)/shard_map/all_to_all | solution.py:536
  147.7 0.5 shard_map.230
  148.1 8.7 %all_to_all.44 = f32[8,1,4608]{2,1,0:T(1,128)S(1)} all-to-all(f32[8,1,4608]{2,1,0:T(1,128)S(1)} %bitcast.49), channel_id=1, replica_groups=mesh['gx'=8,'gy'=32] {'gx'}, dimensions={0} | all-to-all | bytes 294912 | tf_op jit(solution)/shard_map/all_to_all | solution.py:536
  156.8 1.3 shard_map.231
  158.1 5.0 %all-to-all-start.7 = ((f32[32,1,5760]{2,1,0:T(1,128)}), f32[32,1,5760]{2,1,0:T(1,128)S(1)}, u32[]{:S(2)}, u32[]{:S(2)}) async-start(f32[32,1,5760]{2,1,0:T(1,128)} %bitcast.22), calls=%async_computation.7 | async-start | bytes 1474560 | tf_op jit(solution)/shard_map/all_to_all | solution.py:531
  163.1 0.1 shard_map.233
  163.2 0.4 copy.47
  163.6 3.6 %reshape.88 = f32[20,4,2,3,3,5,24]{6,5,2,4,3,1,0:T(8,128)} reshape(f32[20,4,2,9,120]{4,2,3,1,0:T(2,128)S(1)} %copy.47) | data formatting | bytes 1382400 | tf_op jit(solution)/shard_map/reshape | solution.py:606
  167.2 6.6 %copy.48 = f32[2,4,5,20,24,3,3]{4,0,6,5,3,2,1:T(2,128)} copy(f32[2,4,5,20,24,3,3]{4,2,0,6,5,1,3:T(8,128)} %bitcast.53) | data formatting | bytes 1382400 | tf_op jit(solution)/shard_map/transpose | solution.py:607
  173.8 4.5 %shard_map.232.lin_ref = f32[1280,1024]{1,0:T(8,128)} custom-call(bf16[1280,1024]{1,0:T(8,128)(2,1)S(1)} %copy-done.4, bf16[20,20]{1,0:T(8,128)(2,1)S(1)} %copy-done.16, bf16[160,20]{1,0:T(8,128)(2,1)S(1)} %copy-done.12, bf16[20,160]{1,0:T(8,128)(2,1)S(1)} %copy-done.15, bf16[160,160]{1,0:T(8,128)(2,1)S(1)} %copy-done.9), custom_call_target="tpu_custom_call" | custom-call | tf_op jit(solution)/shard_map/pallas_call | solution.py:132
  178.3 6.7 %all-to-all-done.7 = f32[32,1,5760]{2,1,0:T(1,128)S(1)} async-done(((f32[32,1,5760]{2,1,0:T(1,128)}), f32[32,1,5760]{2,1,0:T(1,128)S(1)}, u32[]{:S(2)}, u32[]{:S(2)}) %all-to-all-start.7) | async-done | bytes 737312 | tf_op jit(solution)/shard_map/all_to_all | solution.py:531
  185.0 2.8 %shard_map.234 = (f32[2,640,128]{2,1,0:T(8,128)S(1)}, f32[960,128]{1,0:T(8,128)S(1)}) custom-call(s32[1]{0:T(128)} %bitcast.me_ref, f32[1440,128]{1,0:T(8,128)S(1)} %bitcast.40, bf16[8,240,768]{2,1,0:T(8,128)(2,1)} %constant.50.clone.high_hbm, bf16[8,240,768]{2,1,0:T(8,128)(2,1)} %constant.51.clone.low_hbm), custom_call_target="tpu_custom_call" | custom-call | tf_op jit(solution)/shard_map/pallas_call | solution.py:544
  187.9 0.1 collective-permute-start.3
  188.0 1.9 collective-permute-done.3.recv_ref
  189.8 3.3 %shard_map.235 = bf16[16,20,4,1024]{3,2,1,0:T(4,128)(2,1)} custom-call(s32[1]{0:T(128)} %bitcast.me_ref, f32[2,640,128]{2,1,0:T(8,128)S(1)} %get-tuple-element.59.keep_ref, f32[960,128]{1,0:T(8,128)S(1)} %collective-permute-done.3.recv_ref, f32[1280,1024]{1,0:T(8,128)S(1)} %copy-done, bf16[576,1024]{1,0:T(8,128)(2,1)S(1)} %copy-done.5), custom_call_target="tpu_custom_call" | custom-call | tf_op jit(solution)/shard_map/pallas_call | solution.py:544
  (31 shorter events, 0.1 us)
Async XLA Ops:
  4.1 2.0 %collective-permute-start = (f32[960,128]{1,0:T(8,128)S(1)}, f32[960,128]{1,0:T(8,128)S(1)}, u32[]{:S(2)}, u32[]{:S(2)}) collective-permute-start(f32[960,128]{1,0:T(8,128)S(1)} %get-tuple-element.34), channel_id=1, source_target_pairs={{0,32},{32,0},{64,96},{96,64},{128,160},{160,128},{192,224},{224,1... | collective-permute-start | bytes 1474568 | tf_op jit(solution)/shard_map/ppermute | solution.py:541
  9.9 33.7 %all-to-all-start = ((f32[32,1,5760]{2,1,0:T(1,128)}), f32[32,1,5760]{2,1,0:T(1,128)S(1)}, u32[]{:S(2)}, u32[]{:S(2)}) async-start(f32[32,1,5760]{2,1,0:T(1,128)} %bitcast.2), calls=%async_computation | async-start | bytes 1474560 | tf_op jit(solution)/shard_map/all_to_all | solution.py:531
  31.3 12.3 %copy-start.13 = (bf16[48,256]{1,0:T(8,128)(2,1)S(1)}, bf16[48,256]{1,0:T(8,128)(2,1)}, u32[]{:S(2)}) copy-start(bf16[48,256]{1,0:T(8,128)(2,1)} %constant.46.clone.yl_ref) | copy-start | bytes 73732
  31.3 12.3 %copy-start.14 = (bf16[48,256]{1,0:T(8,128)(2,1)S(1)}, bf16[48,256]{1,0:T(8,128)(2,1)}, u32[]{:S(2)}) copy-start(bf16[48,256]{1,0:T(8,128)(2,1)} %constant.45.clone.yh_ref) | copy-start | bytes 73732
  31.3 23.2 %copy-start.11 = (bf16[640,128]{1,0:T(8,128)(2,1)S(1)}, bf16[640,128]{1,0:T(8,128)(2,1)}, u32[]{:S(2)}) copy-start(bf16[640,128]{1,0:T(8,128)(2,1)} %constant.52.clone.e_ref) | copy-start | bytes 491524
  31.5 32.2 %copy-start.7 = (bf16[256,144]{1,0:T(8,128)(2,1)S(1)}, bf16[256,144]{1,0:T(8,128)(2,1)}, u32[]{:S(2)}) copy-start(bf16[256,144]{1,0:T(8,128)(2,1)} %constant.47.clone.y_ref) | copy-start | bytes 221188
  43.7 26.3 %copy-start.16 = (bf16[20,20]{1,0:T(8,128)(2,1)S(1)}, bf16[20,20]{1,0:T(8,128)(2,1)}, u32[]{:S(2)}) copy-start(bf16[20,20]{1,0:T(8,128)(2,1)} %w_ref.1) | copy-start | bytes 2404
  43.7 26.4 %copy-start.9 = (bf16[160,160]{1,0:T(8,128)(2,1)S(1)}, bf16[160,160]{1,0:T(8,128)(2,1)}, u32[]{:S(2)}) copy-start(bf16[160,160]{1,0:T(8,128)(2,1)} %constant.56.clone.mask_ref) | copy-start | bytes 153604
  43.7 26.4 %copy-start.12 = (bf16[160,20]{1,0:T(8,128)(2,1)S(1)}, bf16[160,20]{1,0:T(8,128)(2,1)}, u32[]{:S(2)}) copy-start(bf16[160,20]{1,0:T(8,128)(2,1)} %constant.54.clone.e_ref) | copy-start | bytes 19204
  43.7 26.4 %copy-start.15 = (bf16[20,160]{1,0:T(8,128)(2,1)S(1)}, bf16[20,160]{1,0:T(8,128)(2,1)}, u32[]{:S(2)}) copy-start(bf16[20,160]{1,0:T(8,128)(2,1)} %constant.55.clone.et_ref) | copy-start | bytes 19204
  43.7 26.4 %copy-start.17 = (f32[20]{0:T(128)S(1)}, f32[20]{0:T(128)}, u32[]{:S(2)}) copy-start(f32[20]{0:T(128)} %param.25) | copy-start | bytes 244
  65.0 26.9 %all-to-all-start.3 = ((f32[32,1,5760]{2,1,0:T(1,128)}), f32[32,1,5760]{2,1,0:T(1,128)S(1)}, u32[]{:S(2)}, u32[]{:S(2)}) async-start(f32[32,1,5760]{2,1,0:T(1,128)} %bitcast.11), calls=%async_computation.3 | async-start | bytes 1474560 | tf_op jit(solution)/shard_map/all_to_all | solution.py:531
  70.1 1.7 copy-start.1
  71.9 1.7 copy-start.3
  73.6 23.3 %copy-start.8 = (bf16[1024,192]{1,0:T(8,128)(2,1)S(1)}, bf16[1024,192]{1,0:T(8,128)(2,1)}, u32[]{:S(2)}) copy-start(bf16[1024,192]{1,0:T(8,128)(2,1)} %constant.42.clone.t_ref) | copy-start | bytes 1179652
  91.9 5.0 %copy-start.2 = (f32[1280,1024]{1,0:T(8,128)S(1)}, f32[1280,1024]{1,0:T(8,128)}, u32[]{:S(2)}) copy-start(f32[1280,1024]{1,0:T(8,128)} %get-tuple-element.46.lin_ref) | copy-start | bytes 15728644
  91.9 5.0 %copy-start.6 = (bf16[576,1024]{1,0:T(8,128)(2,1)S(1)}, bf16[576,1024]{1,0:T(8,128)(2,1)}, u32[]{:S(2)}) copy-start(bf16[576,1024]{1,0:T(8,128)(2,1)} %constant.43.clone.s_ref) | copy-start | bytes 3538948
  94.8 2.1 %collective-permute-start.1 = (f32[960,128]{1,0:T(8,128)S(1)}, f32[960,128]{1,0:T(8,128)S(1)}, u32[]{:S(2)}, u32[]{:S(2)}) collective-permute-start(f32[960,128]{1,0:T(8,128)S(1)} %get-tuple-element.45), channel_id=1, source_target_pairs={{0,32},{32,0},{64,96},{96,64},{128,160},{160,128},{192,224},{224,1... | collective-permute-start | bytes 1474568 | tf_op jit(solution)/shard_map/ppermute | solution.py:541
  106.4 2.0 %collective-permute-start.2 = (f32[960,128]{1,0:T(8,128)S(1)}, f32[960,128]{1,0:T(8,128)S(1)}, u32[]{:S(2)}, u32[]{:S(2)}) collective-permute-start(f32[960,128]{1,0:T(8,128)S(1)} %get-tuple-element.50), channel_id=1, source_target_pairs={{0,32},{32,0},{64,96},{96,64},{128,160},{160,128},{192,224},{224,1... | collective-permute-start | bytes 1474568 | tf_op jit(solution)/shard_map/ppermute | solution.py:541
  111.3 36.4 %copy-start.10 = (bf16[128,640]{1,0:T(8,128)(2,1)S(1)}, bf16[128,640]{1,0:T(8,128)(2,1)}, u32[]{:S(2)}) copy-start(bf16[128,640]{1,0:T(8,128)(2,1)} %constant.53.clone.e_ref) | copy-start | bytes 491524
  158.1 26.9 %all-to-all-start.7 = ((f32[32,1,5760]{2,1,0:T(1,128)}), f32[32,1,5760]{2,1,0:T(1,128)S(1)}, u32[]{:S(2)}, u32[]{:S(2)}) async-start(f32[32,1,5760]{2,1,0:T(1,128)} %bitcast.22), calls=%async_computation.7 | async-start | bytes 1474560 | tf_op jit(solution)/shard_map/all_to_all | solution.py:531
  167.2 6.6 %copy-start.4 = (bf16[1280,1024]{1,0:T(8,128)(2,1)S(1)}, bf16[1280,1024]{1,0:T(8,128)(2,1)}, u32[]{:S(2)}) copy-start(bf16[1280,1024]{1,0:T(8,128)(2,1)} %get-tuple-element.55.p_ref) | copy-start | bytes 7864324
  185.0 4.8 %copy-start = (f32[1280,1024]{1,0:T(8,128)S(1)}, f32[1280,1024]{1,0:T(8,128)}, u32[]{:S(2)}) copy-start(f32[1280,1024]{1,0:T(8,128)} %shard_map.232.lin_ref) | copy-start | bytes 15728644
  185.0 4.8 %copy-start.5 = (bf16[576,1024]{1,0:T(8,128)(2,1)S(1)}, bf16[576,1024]{1,0:T(8,128)(2,1)}, u32[]{:S(2)}) copy-start(bf16[576,1024]{1,0:T(8,128)(2,1)} %constant.44.clone.s_ref) | copy-start | bytes 3538948
  187.9 2.0 %collective-permute-start.3 = (f32[960,128]{1,0:T(8,128)S(1)}, f32[960,128]{1,0:T(8,128)S(1)}, u32[]{:S(2)}, u32[]{:S(2)}) collective-permute-start(f32[960,128]{1,0:T(8,128)S(1)} %get-tuple-element.60), channel_id=1, source_target_pairs={{0,32},{32,0},{64,96},{96,64},{128,160},{160,128},{192,224},{224,1... | collective-permute-start | bytes 1474568 | tf_op jit(solution)/shard_map/ppermute | solution.py:541
